TPU v7x, 256 devices: a whole 4x4x8 slice. The times are simulated.
256 devices in a mesh: ens: 8 (over x, core), space: 32 (over y, z).
Axes of the slice: x: 4, y: 4, z: 8, core: 2. Of those that a mesh axis runs over, the one named last changes fastest.
Arguments:
- members_field: bfloat16 [512, 262144], P('ens', 'space'), may hold values from -6 to 6
- predicted: float32 [512, 40960], P('ens', 'space'), may hold values from -6 to 6
- noise: float32 [512, 40960], P('ens', 'space'), may hold values from -6 to 6
- observed: float32 [40960], P('space'), may hold values from -8 to 8
- obs_precision: float32 [40960], P('space'), may hold values from 0.5 to 2
- obs_block: int32 [40960], P('space'), may hold values from 0 to 31
- block_error_scale: float32 [32], replicated, may hold values from 0.5 to 2
- member_ids: int32 [512], replicated, may hold values from 0 to 511, each once
Outputs:
- updated_field: bfloat16 [512, 262144], P('ens', 'space')
Inputs may be any that keep to these rules, and one draw needn't show every extreme that they name: `member_ids`: each member appears exactly once.
All inputs are finite; a program needn't handle non-finite values.
Results may differ from a plain program's by a relative error of at most 0.012.
The roundings to bfloat16 on the way count: a program that leaves them out, or rounds other values in their place, can miss the bound.
Values may be sent and summed in bfloat16 or wider, within the bound.
No kernel may reach another device: no remote copies, remote signals or barrier semaphores. Data moves between devices by JAX's collectives and lax.ppermute only.
A program may use at most 64 MiB of HBM per device.

v0:
```python
import jax
import jax.numpy as jnp
from jax import lax
from jax.sharding import PartitionSpec as P


def body(
    members_field,
    predicted,
    noise,
    observed,
    obs_precision,
    obs_block,
    block_error_scale,
    member_ids,
):
    gathered_pred, gathered_noise = (
        lax.all_to_all(predicted, "ens", split_axis=1, concat_axis=0, tiled=True),
        lax.all_to_all(noise, "ens", split_axis=1, concat_axis=0, tiled=True),
    )
    members = gathered_pred.shape[0]
    width = gathered_pred.shape[1]
    offset = lax.axis_index("ens") * width
    obs_here = lax.dynamic_slice_in_dim(observed, offset, width)
    precision_here = lax.dynamic_slice_in_dim(obs_precision, offset, width)
    block_here = lax.dynamic_slice_in_dim(obs_block, offset, width)
    blocks = block_error_scale.shape[0]
    hits = block_here[:, None] == jnp.arange(blocks, dtype=jnp.int32)[None, :]
    scale = jnp.sum(
        jnp.where(hits, block_error_scale[None, :], jnp.zeros_like(block_error_scale)[None, :]),
        axis=1,
    )
    weight = precision_here / scale
    ordered = jnp.zeros_like(gathered_pred).at[member_ids].set(gathered_pred)
    factor = 1.0 / jnp.sqrt(jnp.float32(members - 1))
    pred_mean = jnp.mean(ordered, axis=0)
    spread = weight[None, :] * (ordered - pred_mean[None, :]) * factor
    innovation = (weight[None, :] * (obs_here[None, :] - ordered) + gathered_noise) * factor
    gram_part = jnp.dot(spread, spread.T, precision=lax.Precision.HIGHEST)
    cross_part = jnp.dot(spread, innovation.T, precision=lax.Precision.HIGHEST)
    gram, cross = lax.psum((gram_part, cross_part), ("ens", "space"))
    system = jnp.eye(members, dtype=jnp.float32) + gram
    lower = jnp.linalg.cholesky(system)
    transform = jax.scipy.linalg.cho_solve((lower, True), cross).astype(jnp.bfloat16)
    cells = lax.all_to_all(members_field, "ens", split_axis=1, concat_axis=0, tiled=True)
    field_mean = jnp.sum(cells, axis=0, dtype=jnp.float32) / members
    widened = cells.astype(jnp.float32)
    anomaly = (widened - field_mean[None, :]).astype(jnp.bfloat16)
    increment = jnp.dot(transform.T, anomaly, preferred_element_type=jnp.float32)
    renewed = (widened + increment).astype(jnp.bfloat16)
    return lax.all_to_all(renewed, "ens", split_axis=0, concat_axis=1, tiled=True)


def solution(mesh):
    placed = (
        P("ens", "space"),
        P("ens", "space"),
        P("ens", "space"),
        P("space"),
        P("space"),
        P("space"),
        P(),
        P(),
    )
    return jax.shard_map(
        body, mesh=mesh, in_specs=placed, out_specs=P("ens", "space"), check_vma=False
    )
```

profile of v0, /device:TPU:1, one launch (start us, length us, event | category | flops | bytes accessed | tf_op | source)
XLA Modules:
  0.0 490.4 jit_solution(14862648538480038171)
XLA Ops:
  6.5 1.3 all_to_all.54
  7.8 1.0 copy.46
  8.8 6.6 %all-to-all-start.1 = ((f32[64,8,160]{2,0,1:T(8,128)}), f32[64,8,160]{2,0,1:T(8,128)S(1)}, u32[]{:S(2)}, u32[]{:S(2)}) async-start(f32[64,8,160]{2,0,1:T(8,128)} %copy.46), calls=%async_computation.1 | async-start | bytes 1048576 | tf_op jit(solution)/shard_map/all_to_all | solution.py:18
  15.7 1.0 copy.51
  16.7 0.8 dynamic_slice.10
  17.5 7.4 %all-to-all-done.1 = f32[64,8,160]{2,0,1:T(8,128)S(1)} async-done(((f32[64,8,160]{2,0,1:T(8,128)}), f32[64,8,160]{2,0,1:T(8,128)S(1)}, u32[]{:S(2)}, u32[]{:S(2)}) %all-to-all-start.1) | async-done | bytes 327712 | tf_op jit(solution)/shard_map/all_to_all | solution.py:18
  24.9 4.3 all-to-all-start.2
  29.2 0.8 dynamic-slice_divide_fusion
  29.9 0.8 dynamic_slice.11
  30.7 1.1 copy.61
  31.8 2.4 scatter_custom_fusion
  34.2 4.5 all-to-all-done.2
  38.7 4.3 all-to-all-start
  43.3 2.1 fusion.28
  45.4 2.1 fusion.27
  47.5 10.6 %all-to-all-done = bf16[64,8,1024]{2,0,1:T(8,128)(2,1)S(1)} async-done(((bf16[64,8,1024]{2,0,1:T(8,128)(2,1)}), bf16[64,8,1024]{2,0,1:T(8,128)(2,1)S(1)}, u32[]{:S(2)}, u32[]{:S(2)}) %all-to-all-start) | async-done | bytes 1048608 | tf_op jit(solution)/shard_map/all_to_all | solution.py:45
  58.3 1.2 fusion
  59.5 252.3 %all-reduce.4.cloned.1.call-done = (f32[512,512]{1,0:T(8,128)}, f32[512,512]{0,1:T(8,128)}) async-done(((f32[512,512]{1,0:T(8,128)}, f32[512,512]{0,1:T(8,128)}), (f32[512,512]{1,0:T(8,128)}, f32[512,512]{0,1:T(8,128)})) %all-reduce.4.cloned.1.call-update) | async-done | bytes 2097168 | tf_op jit(solution)/shard_map/psum | solution.py:41
  311.9 2.3 convert_add_fusion
  314.2 1.6 copy.50
  316.1 1.0 copy-done.1
  317.1 11.7 %cholesky.104 = f32[128,128]{1,0:T(8,128)S(1)} custom-call(f32[128,128]{1,0:T(8,128)S(1)} %cholesky.266), custom_call_target="Cholesky" | custom-call | tf_op jit(solution)/shard_map/jit(cholesky)/cholesky | solution.py:43
  329.0 9.8 %custom-call.34 = f32[1,128,128]{1,2,0:T(8,128)S(1)} custom-call(f32[1,128,128]{2,1,0:T(8,128)S(1)} %get-tuple-element.36), custom_call_target="InvertDiagBlocksLowerTriangular" | custom-call | tf_op jit(solution)/shard_map/jit(cholesky)/cholesky | solution.py:43
  339.5 11.9 %cholesky.217 = f32[128,128]{1,0:T(8,128)S(1)} custom-call(f32[128,128]{1,0:T(8,128)S(1)} %cholesky.270), custom_call_target="Cholesky" | custom-call | tf_op jit(solution)/shard_map/jit(cholesky)/cholesky | solution.py:43
  351.4 9.8 %custom-call.35 = f32[1,128,128]{1,2,0:T(8,128)S(1)} custom-call(f32[1,128,128]{2,1,0:T(8,128)S(1)} %get-tuple-element.33), custom_call_target="InvertDiagBlocksLowerTriangular" | custom-call | tf_op jit(solution)/shard_map/jit(cholesky)/cholesky | solution.py:43
  361.9 11.7 %cholesky.238 = f32[128,128]{1,0:T(8,128)S(1)} custom-call(f32[128,128]{1,0:T(8,128)S(1)} %cholesky.275), custom_call_target="Cholesky" | custom-call | tf_op jit(solution)/shard_map/jit(cholesky)/cholesky | solution.py:43
  373.7 0.7 compare_reduce_fusion.1
  374.4 9.8 %custom-call.36 = f32[1,128,128]{1,2,0:T(8,128)S(1)} custom-call(f32[1,128,128]{2,1,0:T(8,128)S(1)} %get-tuple-element.30), custom_call_target="InvertDiagBlocksLowerTriangular" | custom-call | tf_op jit(solution)/shard_map/jit(cholesky)/cholesky | solution.py:43
  384.8 12.0 %cholesky.255 = f32[128,128]{1,0:T(8,128)S(1)} custom-call(f32[128,128]{1,0:T(8,128)S(1)} %convolution_subtract_fusion.8), custom_call_target="Cholesky" | custom-call | tf_op jit(solution)/shard_map/jit(cholesky)/cholesky | solution.py:43
  396.8 0.6 compare_reduce_fusion
  397.4 0.7 compare_reduce_fusion.2
  400.8 10.6 %while.1 = (s32[]{:T(128)}, f32[512,512]{1,0:T(8,128)S(1)}, s32[4,2]{0,1:T(2,128)S(1)}, f32[4,128,128]{2,1,0:T(8,128)}, s32[]{:T(128)}) while((s32[]{:T(128)}, f32[512,512]{1,0:T(8,128)S(1)}, s32[4,2]{0,1:T(2,128)S(1)}, f32[4,128,128]{2,1,0:T(8,128)}, s32[]{:T(128)}) %tuple.31), condition=%wide.while_cond, body=%wide.while_body.sunk | while | flops 2 | bytes 132705 | solution.py:44
  400.9 0.6 fusion.87
  401.5 2.0 bitcast_dynamic-update-slice_fusion.2
  403.5 0.6 fusion.87
  404.1 2.0 bitcast_dynamic-update-slice_fusion.2
  406.2 0.6 fusion.87
  406.8 2.0 bitcast_dynamic-update-slice_fusion.2
  408.8 0.6 fusion.87
  409.4 2.0 bitcast_dynamic-update-slice_fusion.2
  411.4 40.2 %custom-call.37 = f32[4,128,128]{1,2,0:T(8,128)S(1)} custom-call(f32[4,128,128]{2,1,0:T(8,128)} %get-tuple-element.12), custom_call_target="InvertDiagBlocksLowerTriangular" | custom-call | tf_op jit(solution)/shard_map/jit(_cho_solve)/triangular_solve | solution.py:44
  451.6 1.4 fusion.29
  452.9 1.3 convolution_subtract_fusion.3
  455.6 0.6 convolution_subtract_fusion.5
  458.7 0.7 convolution_subtract_fusion.4
  459.9 0.8 fusion.1
  460.6 21.4 %all_to_all.70 = bf16[8,64,1024]{2,1,0:T(8,128)(2,1)S(1)} all-to-all(bf16[8,64,1024]{2,1,0:T(8,128)(2,1)S(1)} %bitcast.93), channel_id=1, replica_groups=mesh['ens'=8,'space'=32] {'ens'}, dimensions={0} | all-to-all | bytes 2097152 | tf_op jit(solution)/shard_map/all_to_all | solution.py:51
  482.0 1.1 copy.59
  (59 shorter events, 7.9 us)
Async XLA Ops:
  7.8 7.6 %copy-start.6 = (f32[64,1280]{1,0:T(8,128)S(1)}, f32[64,1280]{1,0:T(8,128)}, u32[]{:S(2)}) copy-start(f32[64,1280]{1,0:T(8,128)} %param.10) | copy-start | bytes 983044
  8.8 16.1 %all-to-all-start.1 = ((f32[64,8,160]{2,0,1:T(8,128)}), f32[64,8,160]{2,0,1:T(8,128)S(1)}, u32[]{:S(2)}, u32[]{:S(2)}) async-start(f32[64,8,160]{2,0,1:T(8,128)} %copy.46), calls=%async_computation.1 | async-start | bytes 1048576 | tf_op jit(solution)/shard_map/all_to_all | solution.py:18
  15.4 2.0 copy-start.8
  15.7 15.0 %copy-start.3 = (bf16[64,8192]{1,0:T(8,128)(2,1)S(1)}, bf16[64,8192]{1,0:T(8,128)(2,1)}, u32[]{:S(2)}) copy-start(bf16[64,8192]{1,0:T(8,128)(2,1)} %param.8) | copy-start | bytes 3145732
  24.9 13.8 %all-to-all-start.2 = ((f32[64,8,160]{2,0,1:T(8,128)}), f32[64,8,160]{2,0,1:T(8,128)S(1)}, u32[]{:S(2)}, u32[]{:S(2)}) async-start(f32[64,8,160]{2,0,1:T(8,128)} %copy.51), calls=%async_computation.2 | async-start | bytes 1048576 | tf_op jit(solution)/shard_map/all_to_all | solution.py:19
  30.7 1.1 copy-start.7
  38.7 19.5 %all-to-all-start = ((bf16[64,8,1024]{2,0,1:T(8,128)(2,1)}), bf16[64,8,1024]{2,0,1:T(8,128)(2,1)S(1)}, u32[]{:S(2)}, u32[]{:S(2)}) async-start(bf16[64,8,1024]{2,0,1:T(8,128)(2,1)} %bitcast.84), calls=%async_computation | async-start | bytes 2097152 | tf_op jit(solution)/shard_map/all_to_all | solution.py:45
  43.0 268.9 %all-reduce.4.cloned.1.call-start = ((), (), s32[]{:S(2)}) async-start(), calls=%async_computation.4 | async-start | bytes 4194304 | tf_op jit(solution)/shard_map/psum | solution.py:41
  314.2 1.7 copy-start
  316.1 1.0 copy-start.1
  317.1 21.7 %copy-start.2 = (f32[512,512]{1,0:T(8,128)S(1)}, f32[512,512]{1,0:T(8,128)}, u32[]{:S(2)}) copy-start(f32[512,512]{1,0:T(8,128)} %copy-done.1) | copy-start | bytes 3145732
  411.3 43.4 %copy-start.5 = (f32[512,512]{1,0:T(8,128)S(1)}, f32[512,512]{1,0:T(8,128)}, u32[]{:S(2)}) copy-start(f32[512,512]{1,0:T(8,128)} %get-tuple-element.21) | copy-start | bytes 3145732
  458.7 1.2 copy-start.4
Sparse Core Ops, SparseCore 0:
  49.4 262.4 all-reduce.3
where the time goes:
time: 494 us; the launch traced here: 490 us
  waiting for transfers between devices  275 us (56%)
  other arithmetic  124 us (25%)
  local copies, waits for them, and re-layouts  23 us (5%)
  blocking collectives  21.4 us (4%)
  between operations  16.7 us (3%)
  starting transfers between devices  15.4 us (3%)
  matrix products  14.8 us (3%)
    psum x1, waiting for transfers between devices, body(): gram, cross = lax.psum((gram_part, cross_part), ('ens', 'space'))  252 us
    another operation x14, other arithmetic, body(): lower = jnp.linalg.cholesky(system)  78.9 us
    another operation x3, other arithmetic, body(): jax.scipy.linalg.cho_solve((lower, True), cross).astype(jnp.bfloat16)  40.3 us
    all_to_all x1, blocking collectives, body(): lax.all_to_all(renewed, 'ens', split_axis=0, concat_axis=1, tiled=True)  21.4 us
    all_to_all x1, waiting for transfers between devices, body(): lax.all_to_all(members_field, 'ens', split_axis=1, concat_axis=0, tiled=T...  10.6 us
    another operation x12, local copies, waits for them, and re-layouts  10.5 us
  transfers between devices with their start and end apart: 4, of which 4 were waited for; matrix products, arithmetic and copies ran while one was open for 3% of the time, Pallas kernels for 0%

commit v1 on v0

v1 whole, which is shorter than its diff:
```python
import functools
import jax
import jax.numpy as jnp
from jax import lax
from jax.experimental import pallas as pl
from jax.experimental.pallas import tpu as pltpu
from jax.sharding import PartitionSpec as P

F32 = jnp.float32
BF16 = jnp.bfloat16
EXACT = lax.Precision.HIGHEST
MIB = 1024 * 1024


def across_rows(tile, row):
    return jnp.broadcast_to(tile[row : row + 1, :], tile.shape)


def across_lanes(tile, lane):
    return jnp.broadcast_to(tile[:, lane : lane + 1], tile.shape)


def dot_nt(a, b, precision=None):
    return lax.dot_general(
        a, b, (((1,), (1,)), ((), ())), precision=precision, preferred_element_type=F32
    )


def dot_nn(a, b, precision=None):
    return jnp.dot(a, b, precision=precision, preferred_element_type=F32)


def invert_block(block):
    lanes = lax.broadcasted_iota(jnp.int32, (8, 128), 1)
    subs = lax.broadcasted_iota(jnp.int32, (8, 128), 0)
    tiles = [block[8 * i : 8 * i + 8, :] for i in range(16)]
    for t in range(16):
        cols = [across_lanes(tiles[t], 8 * t + j) for j in range(8)]
        for k in range(8):
            recip = 1.0 / across_rows(cols[k], k)
            pivot = cols[k]
            here = subs == k
            for j in range(8):
                if j != k:
                    scaled = across_rows(cols[j], k) * recip
                    cols[j] = jnp.where(here, scaled, cols[j] - pivot * scaled)
            cols[k] = jnp.where(here, recip, -pivot * recip)
        panel = (lanes >= 8 * t) & (lanes < 8 * t + 8)
        old = tiles[t]
        row = cols[0] * across_rows(old, 0)
        for j in range(1, 8):
            row = row + cols[j] * across_rows(old, j)
        for j in range(8):
            row = jnp.where(lanes == 8 * t + j, cols[j], row)
        rows = [across_rows(row, j) for j in range(8)]
        for i in range(16):
            if i == t:
                continue
            terms = [across_lanes(tiles[i], 8 * t + j) * rows[j] for j in range(8)]
            pairs = [terms[j] + terms[j + 1] for j in range(0, 8, 2)]
            total = (pairs[0] + pairs[1]) + (pairs[2] + pairs[3])
            tiles[i] = jnp.where(panel, 0.0, tiles[i]) - total
        tiles[t] = row
    return jnp.concatenate(tiles, axis=0)


def prepare_kernel(mine_ref, got_ref, scale_ref, out_ref):
    mine = mine_ref[...]
    got = got_ref[...]
    rows = 2 * mine.shape[0]
    mean = (jnp.sum(mine, axis=0, keepdims=True) + jnp.sum(got, axis=0, keepdims=True)) / rows
    scale = scale_ref[...]
    half = mine.shape[0]
    out_ref[0:half, :] = ((mine - mean) * scale).astype(BF16)
    out_ref[half:rows, :] = ((got - mean) * scale).astype(BF16)
    high = mean.astype(BF16)
    rest = mean - high.astype(F32)
    mid = rest.astype(BF16)
    low = (rest - mid.astype(F32)).astype(BF16)
    out_ref[rows : rows + 16, :] = jnp.concatenate(
        [high, mid, low, jnp.zeros((13, mean.shape[1]), BF16)], axis=0
    )


def gram_kernel(p0_ref, p1_ref, p2_ref, p3_ref, mine_ref, got_ref, scale_ref, obs_ref, own_ref, other_ref, *, factor):
    refs = (p0_ref, p1_ref, p2_ref, p3_ref)
    rows = p0_ref.shape[0] - 16
    half = rows // 2
    scale = scale_ref[...]
    means = []
    for ref in refs:
        tail = ref[rows : rows + 16, :].astype(F32)
        means.append(tail[0:1, :] + (tail[1:2, :] + tail[2:3, :]))
    mean = ((means[0] + means[1]) + (means[2] + means[3])) * 0.25
    spreads = [
        (ref[0:rows, :].astype(F32) + scale * (m - mean)).astype(BF16) for ref, m in zip(refs, means)
    ]
    shift = scale * (obs_ref[...] - mean)
    noise = jnp.concatenate([mine_ref[...], got_ref[...]], axis=0)
    right = shift + factor * noise
    high = right.astype(BF16)
    low = (right - high.astype(F32)).astype(BF16)
    left = jnp.concatenate([spreads[0], high, low], axis=0)
    for i in range(4):
        part = dot_nt(left, spreads[i])
        gram = part[0:rows]
        cross = part[rows : 2 * rows] + part[2 * rows : 3 * rows]
        own_ref[i, 0:half, :] = gram[0:half]
        own_ref[i, half:rows, :] = cross[0:half]
        other_ref[i, 0:half, :] = pltpu.roll(gram[half:rows], half, 1)
        other_ref[i, half:rows, :] = pltpu.roll(cross[half:rows], half, 1)


def solve_kernel(
    first_ref, g0_ref, g1_ref, g2_ref, g3_ref, other_ref, cross_ref, ids_row_ref, ids_col_ref, out_ref, a_ref, m_ref
):
    size = 512
    block = 128
    half = 64
    first = first_ref[0]
    unit = (
        lax.broadcasted_iota(jnp.int32, (block, block), 0) == lax.broadcasted_iota(jnp.int32, (block, block), 1)
    ).astype(F32)
    own = (g0_ref, g1_ref, g2_ref, g3_ref)
    for k in range(4):
        for i in range(4):
            j = (i - k) % 4
            piece = jnp.concatenate([own[k][j], pltpu.roll(other_ref[k, j], half, 1)], axis=0)
            if i == k:
                piece = piece + unit
            a_ref[k * block : (k + 1) * block, i * block : (i + 1) * block] = piece
    members = first + lax.broadcasted_iota(jnp.int32, (half, block), 0)
    for i in range(4):
        ids = ids_row_ref[:, i * block : (i + 1) * block]
        m_ref[:, i * block : (i + 1) * block] = cross_ref[i] + (ids == members).astype(F32)

    inverses, uppers = [], []
    for b in range(4):
        lo, hi = b * block, (b + 1) * block
        inverse = invert_block(a_ref[lo:hi, lo:hi])
        inverses.append(inverse)
        if hi < size:
            upper = dot_nn(inverse, a_ref[lo:hi, hi:size], EXACT)
            uppers.append(upper)
            a_ref[hi:size, hi:size] = a_ref[hi:size, hi:size] - dot_nn(a_ref[hi:size, lo:hi], upper, EXACT)
            m_ref[:, hi:size] = m_ref[:, hi:size] - dot_nn(m_ref[:, lo:hi], upper, EXACT)
    for b in range(3, -1, -1):
        lo, hi = b * block, (b + 1) * block
        z = dot_nn(m_ref[:, lo:hi], inverses[b], EXACT)
        if hi < size:
            z = z - dot_nt(m_ref[:, hi:size], uppers[b], EXACT)
        m_ref[:, lo:hi] = z

    place = (ids_col_ref[...] == lax.broadcasted_iota(jnp.int32, (size, size), 1)).astype(F32)
    ordered = dot_nn(m_ref[...], place, EXACT)
    own_unit = (
        lax.broadcasted_iota(jnp.int32, (half, size), 1) == first + lax.broadcasted_iota(jnp.int32, (half, size), 0)
    ).astype(F32)
    out_ref[...] = (ordered - own_unit).astype(BF16)


def body(members_field, predicted, noise, observed, obs_precision, obs_block, block_error_scale, member_ids):
    rows, width = predicted.shape
    members = member_ids.shape[0]
    half = width // 2
    place = lax.axis_index("ens")
    core = lax.rem(place, 2)
    chip = lax.div(place, 2)
    swap = [(i, i ^ 1) for i in range(8)]

    def turned(array, steps):
        return lax.ppermute(array, "ens", [(i, (i + 2 * steps) % 8) for i in range(8)])

    def cut(array, which):
        return lax.dynamic_slice_in_dim(array, which * half, half, array.ndim - 1)

    field = lax.all_gather(members_field, "ens", axis=0, tiled=True)

    pred_mine, noise_mine = cut(predicted, core), cut(noise, core)
    pred_got = lax.ppermute(cut(predicted, 1 - core), "ens", swap)
    noise_got = lax.ppermute(cut(noise, 1 - core), "ens", swap)

    blocks = block_error_scale.shape[0]
    block_here = cut(obs_block, core)
    hits = block_here[None, :] == jnp.arange(blocks, dtype=jnp.int32)[:, None]
    error_scale = jnp.sum(jnp.where(hits, block_error_scale[:, None], 0.0), axis=0)
    factor = float(1.0 / (members - 1) ** 0.5)
    scale = (cut(obs_precision, core) / error_scale * factor)[None, :]
    obs_here = cut(observed, core)[None, :]

    payload = pl.pallas_call(
        prepare_kernel, out_shape=jax.ShapeDtypeStruct((2 * rows + 16, half), BF16), name="prepare"
    )(pred_mine, pred_got, scale)
    payloads = [payload] + [turned(payload, k) for k in (1, 2, 3)]
    shape = jax.ShapeDtypeStruct((4, 2 * rows, 2 * rows), F32)
    own, other = pl.pallas_call(
        functools.partial(gram_kernel, factor=factor), out_shape=(shape, shape), name="gram"
    )(*payloads, noise_mine, noise_got, scale, obs_here)
    part = own + lax.ppermute(other, "ens", swap)

    spread_out = lax.all_to_all(part.reshape(32, 16, 128), "space", split_axis=0, concat_axis=0)
    summed = jnp.sum(spread_out, axis=0)
    whole = lax.all_to_all(
        jnp.broadcast_to(summed[None], (32, 16, 128)), "space", split_axis=0, concat_axis=0
    ).reshape(4, 2 * rows, 2 * rows)
    gram = whole[:, :rows]
    cross = whole[:, rows:]
    grams = [gram] + [turned(gram, k) for k in (1, 2, 3)]
    others = lax.ppermute(jnp.stack(grams), "ens", swap)

    ids = member_ids.reshape(4, 2, rows)
    ids = jnp.stack(
        [
            lax.dynamic_slice(ids, (lax.rem(chip + 4 - k, 4), lax.rem(core + c, 2), 0), (1, 1, rows))[0, 0]
            for k in range(4)
            for c in range(2)
        ]
    ).reshape(members)
    first = (place * rows).reshape(1).astype(jnp.int32)
    vmem = pl.BlockSpec(memory_space=pltpu.VMEM)
    transform = pl.pallas_call(
        solve_kernel,
        out_shape=jax.ShapeDtypeStruct((rows, members), BF16),
        in_specs=[pl.BlockSpec(memory_space=pltpu.SMEM)] + [vmem] * 8,
        out_specs=vmem,
        scratch_shapes=[pltpu.VMEM((members, members), F32), pltpu.VMEM((rows, members), F32)],
        compiler_params=pltpu.CompilerParams(vmem_limit_bytes=32 * MIB),
        name="solve",
    )(first, *grams, others, cross, ids[None, :], ids[:, None])

    field_mean = jnp.sum(field, axis=0, dtype=F32) / members
    anomaly = (field.astype(F32) - field_mean[None, :]).astype(BF16)
    increment = jnp.dot(transform, anomaly, preferred_element_type=F32)
    return (members_field.astype(F32) + increment).astype(BF16)


def solution(mesh):
    placed = (
        P("ens", "space"),
        P("ens", "space"),
        P("ens", "space"),
        P("space"),
        P("space"),
        P("space"),
        P(),
        P(),
    )
    return jax.shard_map(
        body, mesh=mesh, in_specs=placed, out_specs=P("ens", "space"), check_vma=False
    )
```

time: 494 us -> 125 us (0.25)
  waiting for transfers between devices: 275 us -> 11.1 us
  other arithmetic: 124 us -> 8.21 us
  Pallas kernels: 0 us -> 25.2 us
  local copies, waits for them, and re-layouts: 23 us -> 8.66 us
  blocking collectives: 21.4 us -> 35 us
  matrix products: 14.8 us -> 3 us
    psum x1 -> x0, waiting for transfers between devices: 252 us -> none  [body(): gram, cross = lax.psum((gram_part, cross_part), ('ens', 'space'))]
    another operation x17 -> x1, other arithmetic: 119 us -> 0.03 us  [body(): others = lax.ppermute(jnp.stack(grams), 'ens', swap)]
    pallas_call x0 -> x3, Pallas kernels: none -> 25.2 us  [the longest x1 20.6 us: body(): pl.pallas_call(solve_kernel, out_shape=jax.ShapeDtypeStruct((rows, member...]
    all_to_all x3 -> x0, waiting for transfers between devices: 22.5 us -> none  [the longest x1 10.6 us: body(): lax.all_to_all(members_field, 'ens', split_axis=1, concat_axis=0, tiled=T...]
    ppermute x0 -> x10, starting transfers between devices: none -> 19.3 us  [the longest x6 8.37 us: turned(): lax.ppermute(array, 'ens', [(i, (i + 2 * steps) % 8) for i in range(8)])]
    all_to_all x3 -> x0, starting transfers between devices: 15.2 us -> none  [the longest x1 6.64 us: body(): lax.all_to_all(predicted, 'ens', split_axis=1, concat_axis=0, tiled=True)]
    all_to_all x1 -> x2, blocking collectives: 21.4 us -> 35 us  [the longest x1 18.8 us: body(): lax.all_to_all(part.reshape(32, 16, 128), 'space', split_axis=0, concat_a...]
    ppermute x0 -> x10, waiting for transfers between devices: none -> 10.4 us  [the longest x6 8.59 us: turned(): lax.ppermute(array, 'ens', [(i, (i + 2 * steps) % 8) for i in range(8)])]
  transfers between devices with their start and end apart: 4 -> 11, of which waited for: 4 -> 6; matrix products, arithmetic and copies ran while one was open for 3% -> 8% of each run, Pallas kernels for 0% -> 20%
where the time goes in v1:
time: 125 us; the launch traced here: 124 us
  blocking collectives  35 us (28%)
  Pallas kernels  25.2 us (20%)
  starting transfers between devices  19.3 us (15%)
  between operations  13.5 us (11%)
  waiting for transfers between devices  11.1 us (9%)
  local copies, waits for them, and re-layouts  8.66 us (7%)
  other arithmetic  8.21 us (7%)
  matrix products  3 us (2%)
    pallas_call x1, Pallas kernels, body(): pl.pallas_call(solve_kernel, out_shape=jax.ShapeDtypeStruct((rows, member...  20.6 us
    all_to_all x1, blocking collectives, body(): lax.all_to_all(part.reshape(32, 16, 128), 'space', split_axis=0, concat_a...  18.8 us
    all_to_all x1, blocking collectives, body(): lax.all_to_all(jnp.broadcast_to(summed[None], (32, 16, 128)), 'space', sp...  16.2 us
    ppermute x6, waiting for transfers between devices, turned(): lax.ppermute(array, 'ens', [(i, (i + 2 * steps) % 8) for i in range(8)])  8.59 us
    ppermute x6, starting transfers between devices, turned(): lax.ppermute(array, 'ens', [(i, (i + 2 * steps) % 8) for i in range(8)])  8.37 us
    reduce_sum x1, other arithmetic, body(): field_mean = jnp.sum(field, axis=0, dtype=F32) / members  5.62 us
    ppermute x1, starting transfers between devices, body(): others = lax.ppermute(jnp.stack(grams), 'ens', swap)  5.57 us
    dynamic_slice x4, local copies, waits for them, and re-layouts, cut(): return lax.dynamic_slice_in_dim(array, which * half, half, array.ndim - 1)  4.91 us
  transfers between devices with their start and end apart: 11, of which 6 were waited for; matrix products, arithmetic and copies ran while one was open for 8% of the time, Pallas kernels for 20%

profile of v1, /device:TPU:1, one launch (start us, length us, event | category | flops | bytes accessed | tf_op | source)
XLA Modules:
  0.0 124.1 jit_solution(14126486287277676169)
XLA Ops:
  6.5 0.0 all-gather.2.cloned.1.call-start
  6.5 0.7 all-gather.2.cloned.1.call-update
  7.3 1.7 %constant_dynamic-slice_fusion.10 = (f32[64,640]{1,0:T(8,128)S(1)}, f32[64,640]{1,0:T(8,128)}) fusion(f32[64,1280]{1,0:T(8,128)} %param.9, s32[]{:T(128)S(6)} %select_n.21, s32[]{:T(128)S(6)} %select_n.20), kind=kLoop, calls=%fused_computation.21 | loop fusion | bytes 655368 | tf_op jit(solution)/shard_map/dynamic_slice | solution.py:175
  9.0 3.2 %collective-permute-start = (f32[64,640]{1,0:T(8,128)S(1)}, f32[64,640]{1,0:T(8,128)S(1)}, u32[]{:S(2)}, u32[]{:S(2)}) collective-permute-start(f32[64,640]{1,0:T(8,128)S(1)} %get-tuple-element.11), channel_id=1, source_target_pairs={{0,32},{32,0},{64,96},{96,64},{128,160},{160,128},{192,224},{224,1... | collective-permute-start | bytes 491528 | tf_op jit(solution)/shard_map/ppermute | solution.py:180
  12.2 0.8 dynamic_slice.48
  13.0 0.7 select_reduce_fusion
  13.7 0.8 divide_multiply_fusion
  14.5 0.6 broadcast_in_dim.30.scale_ref
  15.1 0.0 collective-permute-done.got_ref
  15.1 0.7 copy-done.6
  15.8 1.8 %prepare.1.p0_ref = bf16[144,640]{1,0:T(8,128)(2,1)} custom-call(f32[64,640]{1,0:T(8,128)} %get-tuple-element.12.mine_ref, f32[64,640]{1,0:T(8,128)} %copy-done.6, f32[1,640]{1,0:T(1,128)} %broadcast_in_dim.30.scale_ref), custom_call_target="tpu_custom_call" | custom-call | tf_op jit(solution)/shard_map/prepare/pallas_call | solution.py:191
  17.6 0.0 collective-permute-start.1
  17.6 1.9 %collective-permute-start.2 = (bf16[144,640]{1,0:T(8,128)(2,1)}, bf16[144,640]{1,0:T(8,128)(2,1)S(1)}, u32[]{:S(2)}, u32[]{:S(2)}) collective-permute-start(bf16[144,640]{1,0:T(8,128)(2,1)} %prepare.1.p0_ref), channel_id=1, source_target_pairs={{0,128},{32,160},{64,192},{96,224},{128,0},{160,32},{192,64},{224,... | collective-permute-start | bytes 552968 | tf_op jit(solution)/shard_map/ppermute | solution.py:172
  19.5 1.2 collective-permute-start.3
  20.7 1.7 %constant_dynamic-slice_fusion.8 = (f32[64,640]{1,0:T(8,128)S(1)}, f32[64,640]{1,0:T(8,128)}) fusion(f32[64,1280]{1,0:T(8,128)} %param.10, s32[]{:T(128)S(6)} %select_n.21, s32[]{:T(128)S(6)} %select_n.20), kind=kLoop, calls=%fused_computation.19 | loop fusion | bytes 655368 | tf_op jit(solution)/shard_map/dynamic_slice | solution.py:175
  22.4 0.8 collective-permute-start.4
  23.2 0.8 dynamic_slice.51
  24.0 0.6 broadcast_in_dim.31.obs_ref
  24.6 0.0 collective-permute-done.4.got_ref
  24.6 4.7 %collective-permute-done.1.p1_ref = bf16[144,640]{1,0:T(8,128)(2,1)S(1)} collective-permute-done((bf16[144,640]{1,0:T(8,128)(2,1)}, bf16[144,640]{1,0:T(8,128)(2,1)S(1)}, u32[]{:S(2)}, u32[]{:S(2)}) %collective-permute-start.1) | collective-permute-done | bytes 184352 | tf_op jit(solution)/shard_map/ppermute | solution.py:172
  29.2 0.0 collective-permute-done.2.p2_ref
  29.2 1.5 %collective-permute-done.3.p3_ref = bf16[144,640]{1,0:T(8,128)(2,1)S(1)} collective-permute-done((bf16[144,640]{1,0:T(8,128)(2,1)}, bf16[144,640]{1,0:T(8,128)(2,1)S(1)}, u32[]{:S(2)}, u32[]{:S(2)}) %collective-permute-start.3) | collective-permute-done | bytes 184352 | tf_op jit(solution)/shard_map/ppermute | solution.py:172
  30.7 0.0 copy-done.5
  30.7 0.0 copy-done.3
  30.7 0.7 copy-done.4
  31.4 2.8 %gram.1 = (f32[4,128,128]{2,1,0:T(8,128)}, f32[4,128,128]{2,1,0:T(8,128)}) custom-call(bf16[144,640]{1,0:T(8,128)(2,1)} %prepare.1.p0_ref, bf16[144,640]{1,0:T(8,128)(2,1)} %copy-done.2, bf16[144,640]{1,0:T(8,128)(2,1)} %copy-done.3, bf16[144,640]{1,0:T(8,128)(2,1)} %copy-done.4, f32[64,640]{1,0:T(8,128)} %get-tuple-element.10.mine_ref, ...), custom_call_target="tpu_custom_call" | custom-call | tf_op jit(solution)/shard_map/gram/pallas_call | solution.py:196
  34.2 1.3 %collective-permute-start.5 = (f32[4,128,128]{2,1,0:T(8,128)}, f32[4,128,128]{2,1,0:T(8,128)S(1)}, u32[]{:S(2)}, u32[]{:S(2)}) collective-permute-start(f32[4,128,128]{2,1,0:T(8,128)} %get-tuple-element.8), channel_id=1, source_target_pairs={{0,32},{32,0},{64,96},{96,64},{128,160},{160,128},{192,224},{224,1... | collective-permute-start | bytes 786440 | tf_op jit(solution)/shard_map/ppermute | solution.py:199
  35.5 1.4 %collective-permute-done.5 = f32[4,128,128]{2,1,0:T(8,128)S(1)} collective-permute-done((f32[4,128,128]{2,1,0:T(8,128)}, f32[4,128,128]{2,1,0:T(8,128)S(1)}, u32[]{:S(2)}, u32[]{:S(2)}) %collective-permute-start.5) | collective-permute-done | bytes 262176 | tf_op jit(solution)/shard_map/ppermute | solution.py:199
  36.9 1.0 add.35
  37.9 18.8 %all_to_all.10 = f32[32,16,128]{2,1,0:T(8,128)S(1)} all-to-all(f32[32,16,128]{2,1,0:T(8,128)S(1)} %bitcast.28), channel_id=1, replica_groups=mesh['ens'=8,'space'=32] {'space'}, dimensions={0} | all-to-all | bytes 524288 | tf_op jit(solution)/shard_map/all_to_all | solution.py:201
  56.7 16.2 %all_to_all.11 = f32[32,16,128]{2,1,0:T(8,128)S(1)} all-to-all(f32[32,16,128]{2,1,0:T(8,128)S(1)} %broadcast_in_dim.32), channel_id=1, replica_groups=mesh['ens'=8,'space'=32] {'space'}, dimensions={0} | all-to-all | bytes 524288 | tf_op jit(solution)/shard_map/all_to_all | solution.py:203
  73.0 1.9 %collective-permute-start.6 = (f32[4,64,128]{2,1,0:T(8,128)S(1)}, f32[4,64,128]{2,1,0:T(8,128)S(1)}, u32[]{:S(2)}, u32[]{:S(2)}) collective-permute-start(f32[4,64,128]{2,1,0:T(8,128)S(1)} %get-tuple-element.15.g0_ref), channel_id=1, source_target_pairs={{0,64},{32,96},{64,128},{96,160},{128,192},{160,224},{192,0},{224,... | collective-permute-start | bytes 393224 | tf_op jit(solution)/shard_map/ppermute | solution.py:172
  74.8 2.0 %collective-permute-start.7 = (f32[4,64,128]{2,1,0:T(8,128)S(1)}, f32[4,64,128]{2,1,0:T(8,128)S(1)}, u32[]{:S(2)}, u32[]{:S(2)}) collective-permute-start(f32[4,64,128]{2,1,0:T(8,128)S(1)} %get-tuple-element.15.g0_ref), channel_id=1, source_target_pairs={{0,128},{32,160},{64,192},{96,224},{128,0},{160,32},{192,64},{224,... | collective-permute-start | bytes 393224 | tf_op jit(solution)/shard_map/ppermute | solution.py:172
  76.9 1.4 %collective-permute-start.8 = (f32[4,64,128]{2,1,0:T(8,128)S(1)}, f32[4,64,128]{2,1,0:T(8,128)S(1)}, u32[]{:S(2)}, u32[]{:S(2)}) collective-permute-start(f32[4,64,128]{2,1,0:T(8,128)S(1)} %get-tuple-element.15.g0_ref), channel_id=1, source_target_pairs={{0,192},{32,224},{64,0},{96,32},{128,64},{160,96},{192,128},{224,1... | collective-permute-start | bytes 393224 | tf_op jit(solution)/shard_map/ppermute | solution.py:172
  78.2 0.0 collective-permute-done.6.g1_ref
  78.3 2.4 %collective-permute-done.7.g2_ref = f32[4,64,128]{2,1,0:T(8,128)S(1)} collective-permute-done((f32[4,64,128]{2,1,0:T(8,128)S(1)}, f32[4,64,128]{2,1,0:T(8,128)S(1)}, u32[]{:S(2)}, u32[]{:S(2)}) %collective-permute-start.7) | collective-permute-done | bytes 131104 | tf_op jit(solution)/shard_map/ppermute | solution.py:172
  80.6 0.1 collective-permute-done.8.g3_ref
  80.7 5.6 %collective-permute-start.9 = (f32[4,4,64,128]{3,2,1,0:T(8,128)S(1)}, f32[4,4,64,128]{3,2,1,0:T(8,128)S(1)}, u32[]{:S(2)}, u32[]{:S(2)}) collective-permute-start(f32[4,4,64,128]{3,2,1,0:T(8,128)S(1)} %pad_maximum_fusion), channel_id=1, source_target_pairs={{0,32},{32,0},{64,96},{96,64},{128,160},{160,128},{192,224},{224,1... | collective-permute-start | bytes 1572872 | tf_op jit(solution)/shard_map/ppermute | solution.py:209
  86.3 0.8 reshape.21
  87.1 0.2 broadcast_in_dim_reshape.8.ids_col_ref
  87.3 0.1 broadcast_in_dim_reshape.6.ids_row_ref
  87.4 0.4 collective-permute-done.9.other_ref
  87.8 20.6 %solve.1 = bf16[64,512]{1,0:T(8,128)(2,1)S(1)} custom-call(s32[1]{0:T(128)} %bitcast.first_ref, f32[4,64,128]{2,1,0:T(8,128)S(1)} %get-tuple-element.15.g0_ref, f32[4,64,128]{2,1,0:T(8,128)S(1)} %collective-permute-done.6.g1_ref, f32[4,64,128]{2,1,0:T(8,128)S(1)} %collective-permute-done.7.g2_ref, f32[4,64,128]{2,1,0:T(8,128)S(1)} %collective-permute-done.8.g3_ref, ...), custom_call_target="tpu_custom_call" | custom-call | tf_op jit(solution)/shard_map/solve/pallas_call | solution.py:221
  108.4 0.0 all-gather.2.cloned.1.call-done
  108.5 5.6 %convert_reduce_fusion = f32[8192]{0:T(1024)S(1)} fusion(bf16[512,8192]{1,0:T(8,128)(2,1)} %all-gather.2.cloned.1.call-done), kind=kLoop, calls=%fused_computation.1 | loop fusion | flops 8380416 | bytes 8421376 | tf_op jit(solution)/shard_map/reduce_sum | solution.py:231
  114.1 0.0 copy-done.1
  114.1 0.1 copy-done
  114.2 3.0 %fusion.1 = bf16[64,8192]{1,0:T(8,128)(2,1)} fusion(bf16[64,512]{1,0:T(8,128)(2,1)S(1)} %solve.1, bf16[512,8192]{1,0:T(8,128)(2,1)S(1)} %copy-done, f32[8192]{0:T(1024)S(1)} %broadcast_multiply_fusion, bf16[64,8192]{1,0:T(8,128)(2,1)S(1)} %copy-done.1), kind=kOutput, calls=%fused_computation.4 | convolution fusion | flops 551026688 | bytes 10584064 | tf_op jit(solution)/shard_map/dot_general | solution.py:233
  (15 shorter events, 0.2 us)
Async XLA Ops:
  6.5 101.9 %all-gather.2.cloned.1.call-start = ((), (), s32[]{:S(2)}) async-start(), calls=%async_computation.2 | async-start | bytes 9437184 | tf_op jit(solution)/shard_map/all_gather | solution.py:177
  9.0 6.1 %collective-permute-start = (f32[64,640]{1,0:T(8,128)S(1)}, f32[64,640]{1,0:T(8,128)S(1)}, u32[]{:S(2)}, u32[]{:S(2)}) collective-permute-start(f32[64,640]{1,0:T(8,128)S(1)} %get-tuple-element.11), channel_id=1, source_target_pairs={{0,32},{32,0},{64,96},{96,64},{128,160},{160,128},{192,224},{224,1... | collective-permute-start | bytes 491528 | tf_op jit(solution)/shard_map/ppermute | solution.py:180
  15.1 0.7 copy-start.6
  15.8 98.4 %copy-start.1 = (bf16[64,8192]{1,0:T(8,128)(2,1)S(1)}, bf16[64,8192]{1,0:T(8,128)(2,1)}, u32[]{:S(2)}) copy-start(bf16[64,8192]{1,0:T(8,128)(2,1)} %param.8) | copy-start | bytes 3145732
  17.6 11.6 %collective-permute-start.1 = (bf16[144,640]{1,0:T(8,128)(2,1)}, bf16[144,640]{1,0:T(8,128)(2,1)S(1)}, u32[]{:S(2)}, u32[]{:S(2)}) collective-permute-start(bf16[144,640]{1,0:T(8,128)(2,1)} %prepare.1.p0_ref), channel_id=1, source_target_pairs={{0,64},{32,96},{64,128},{96,160},{128,192},{160,224},{192,0},{224,... | collective-permute-start | bytes 552968 | tf_op jit(solution)/shard_map/ppermute | solution.py:172
  17.6 11.6 %collective-permute-start.2 = (bf16[144,640]{1,0:T(8,128)(2,1)}, bf16[144,640]{1,0:T(8,128)(2,1)S(1)}, u32[]{:S(2)}, u32[]{:S(2)}) collective-permute-start(bf16[144,640]{1,0:T(8,128)(2,1)} %prepare.1.p0_ref), channel_id=1, source_target_pairs={{0,128},{32,160},{64,192},{96,224},{128,0},{160,32},{192,64},{224,... | collective-permute-start | bytes 552968 | tf_op jit(solution)/shard_map/ppermute | solution.py:172
  19.5 11.2 %collective-permute-start.3 = (bf16[144,640]{1,0:T(8,128)(2,1)}, bf16[144,640]{1,0:T(8,128)(2,1)S(1)}, u32[]{:S(2)}, u32[]{:S(2)}) collective-permute-start(bf16[144,640]{1,0:T(8,128)(2,1)} %prepare.1.p0_ref), channel_id=1, source_target_pairs={{0,192},{32,224},{64,0},{96,32},{128,64},{160,96},{192,128},{224,1... | collective-permute-start | bytes 552968 | tf_op jit(solution)/shard_map/ppermute | solution.py:172
  22.4 2.2 %collective-permute-start.4 = (f32[64,640]{1,0:T(8,128)S(1)}, f32[64,640]{1,0:T(8,128)S(1)}, u32[]{:S(2)}, u32[]{:S(2)}) collective-permute-start(f32[64,640]{1,0:T(8,128)S(1)} %get-tuple-element.9), channel_id=1, source_target_pairs={{0,32},{32,0},{64,96},{96,64},{128,160},{160,128},{192,224},{224,1... | collective-permute-start | bytes 491528 | tf_op jit(solution)/shard_map/ppermute | solution.py:181
  24.6 6.2 %copy-start.5 = (f32[64,640]{1,0:T(8,128)}, f32[64,640]{1,0:T(8,128)S(1)}, u32[]{:S(2)}) copy-start(f32[64,640]{1,0:T(8,128)S(1)} %collective-permute-done.4.got_ref) | copy-start | bytes 491524
  29.2 1.5 %copy-start.2 = (bf16[144,640]{1,0:T(8,128)(2,1)}, bf16[144,640]{1,0:T(8,128)(2,1)S(1)}, u32[]{:S(2)}) copy-start(bf16[144,640]{1,0:T(8,128)(2,1)S(1)} %collective-permute-done.1.p1_ref) | copy-start | bytes 552964
  29.2 1.5 %copy-start.3 = (bf16[144,640]{1,0:T(8,128)(2,1)}, bf16[144,640]{1,0:T(8,128)(2,1)S(1)}, u32[]{:S(2)}) copy-start(bf16[144,640]{1,0:T(8,128)(2,1)S(1)} %collective-permute-done.2.p2_ref) | copy-start | bytes 552964
  30.7 0.7 copy-start.4
  34.2 2.7 %collective-permute-start.5 = (f32[4,128,128]{2,1,0:T(8,128)}, f32[4,128,128]{2,1,0:T(8,128)S(1)}, u32[]{:S(2)}, u32[]{:S(2)}) collective-permute-start(f32[4,128,128]{2,1,0:T(8,128)} %get-tuple-element.8), channel_id=1, source_target_pairs={{0,32},{32,0},{64,96},{96,64},{128,160},{160,128},{192,224},{224,1... | collective-permute-start | bytes 786440 | tf_op jit(solution)/shard_map/ppermute | solution.py:199
  73.0 5.3 %collective-permute-start.6 = (f32[4,64,128]{2,1,0:T(8,128)S(1)}, f32[4,64,128]{2,1,0:T(8,128)S(1)}, u32[]{:S(2)}, u32[]{:S(2)}) collective-permute-start(f32[4,64,128]{2,1,0:T(8,128)S(1)} %get-tuple-element.15.g0_ref), channel_id=1, source_target_pairs={{0,64},{32,96},{64,128},{96,160},{128,192},{160,224},{192,0},{224,... | collective-permute-start | bytes 393224 | tf_op jit(solution)/shard_map/ppermute | solution.py:172
  74.8 5.8 %collective-permute-start.7 = (f32[4,64,128]{2,1,0:T(8,128)S(1)}, f32[4,64,128]{2,1,0:T(8,128)S(1)}, u32[]{:S(2)}, u32[]{:S(2)}) collective-permute-start(f32[4,64,128]{2,1,0:T(8,128)S(1)} %get-tuple-element.15.g0_ref), channel_id=1, source_target_pairs={{0,128},{32,160},{64,192},{96,224},{128,0},{160,32},{192,64},{224,... | collective-permute-start | bytes 393224 | tf_op jit(solution)/shard_map/ppermute | solution.py:172
  76.9 3.8 %collective-permute-start.8 = (f32[4,64,128]{2,1,0:T(8,128)S(1)}, f32[4,64,128]{2,1,0:T(8,128)S(1)}, u32[]{:S(2)}, u32[]{:S(2)}) collective-permute-start(f32[4,64,128]{2,1,0:T(8,128)S(1)} %get-tuple-element.15.g0_ref), channel_id=1, source_target_pairs={{0,192},{32,224},{64,0},{96,32},{128,64},{160,96},{192,128},{224,1... | collective-permute-start | bytes 393224 | tf_op jit(solution)/shard_map/ppermute | solution.py:172
  80.7 7.1 %collective-permute-start.9 = (f32[4,4,64,128]{3,2,1,0:T(8,128)S(1)}, f32[4,4,64,128]{3,2,1,0:T(8,128)S(1)}, u32[]{:S(2)}, u32[]{:S(2)}) collective-permute-start(f32[4,4,64,128]{3,2,1,0:T(8,128)S(1)} %pad_maximum_fusion), channel_id=1, source_target_pairs={{0,32},{32,0},{64,96},{96,64},{128,160},{160,128},{192,224},{224,1... | collective-permute-start | bytes 1572872 | tf_op jit(solution)/shard_map/ppermute | solution.py:209
  108.5 5.8 %copy-start = (bf16[512,8192]{1,0:T(8,128)(2,1)S(1)}, bf16[512,8192]{1,0:T(8,128)(2,1)}, u32[]{:S(2)}) copy-start(bf16[512,8192]{1,0:T(8,128)(2,1)} %all-gather.2.cloned.1.call-done) | copy-start | bytes 25165828
Sparse Core Ops, SparseCore 0:
  9.2 56.4 all-gather.1

commit v2 on v1

v2 whole, which is shorter than its diff:
```python
import functools
import jax
import jax.numpy as jnp
from jax import lax
from jax.experimental import pallas as pl
from jax.experimental.pallas import tpu as pltpu
from jax.sharding import PartitionSpec as P

F32 = jnp.float32
BF16 = jnp.bfloat16
EXACT = lax.Precision.HIGHEST
MIB = 1024 * 1024


def across_rows(tile, row):
    return jnp.broadcast_to(tile[row : row + 1, :], tile.shape)


def across_lanes(tile, lane):
    return jnp.broadcast_to(tile[:, lane : lane + 1], tile.shape)


def dot_nt(a, b, precision=None):
    return lax.dot_general(
        a, b, (((1,), (1,)), ((), ())), precision=precision, preferred_element_type=F32
    )


def dot_tn(a, b, precision=None):
    return lax.dot_general(
        a, b, (((0,), (0,)), ((), ())), precision=precision, preferred_element_type=F32
    )


def dot_nn(a, b, precision=None):
    return jnp.dot(a, b, precision=precision, preferred_element_type=F32)


def tree_sum(terms):
    while len(terms) > 1:
        terms = [terms[i] + terms[i + 1] if i + 1 < len(terms) else terms[i] for i in range(0, len(terms), 2)]
    return terms[0]


def unit_block(rows, cols):
    at = lax.broadcasted_iota(jnp.int32, (rows, cols), 0)
    return (at == lax.broadcasted_iota(jnp.int32, (rows, cols), 1)).astype(F32)


def invert_block(block):
    lanes = lax.broadcasted_iota(jnp.int32, (8, 128), 1)
    subs = lax.broadcasted_iota(jnp.int32, (8, 128), 0)
    tiles = [block[8 * i : 8 * i + 8, :] for i in range(16)]
    for t in range(16):
        old = tiles[t]
        cols = [across_lanes(old, 8 * t + j) for j in range(8)]
        panel = (lanes >= 8 * t) & (lanes < 8 * t + 8)
        old = jnp.where(panel, (lanes - 8 * t == subs).astype(F32), old)
        olds = [across_rows(old, j) for j in range(8)]
        for k in range(8):
            recip = 1.0 / across_rows(cols[k], k)
            pivot = cols[k]
            here = subs == k
            for j in range(8):
                if j != k:
                    scaled = across_rows(cols[j], k) * recip
                    cols[j] = jnp.where(here, scaled, cols[j] - pivot * scaled)
            cols[k] = jnp.where(here, recip, -pivot * recip)
        row = tree_sum([cols[j] * olds[j] for j in range(8)])
        rows = [across_rows(row, j) for j in range(8)]
        for i in [(t + 1 + n) % 16 for n in range(15)]:
            total = tree_sum([across_lanes(tiles[i], 8 * t + j) * rows[j] for j in range(8)])
            tiles[i] = jnp.where(panel, 0.0, tiles[i]) - total
        tiles[t] = row
    return jnp.concatenate(tiles, axis=0)


def prepare_kernel(place_ref, table_ref, mine_ref, got_ref, facts_ref, out_ref, side_ref, *, factor):
    half = mine_ref.shape[0]
    rows = 2 * half
    width = out_ref.shape[1]
    here = pl.ds(pl.multiple_of(lax.rem(place_ref[0], 2) * width, 128), width)
    block = facts_ref[2:3, here]
    error_scale = jnp.zeros_like(block)
    for b in range(table_ref.shape[0]):
        error_scale = jnp.where(block == float(b), table_ref[b], error_scale)
    scale = facts_ref[0:1, here] / error_scale * factor
    side_ref[...] = jnp.concatenate([scale, facts_ref[1:2, here], jnp.zeros((6, width), F32)], axis=0)
    mine = mine_ref[:, here]
    got = got_ref[:, here]
    mean = (jnp.sum(mine, axis=0, keepdims=True) + jnp.sum(got, axis=0, keepdims=True)) / rows
    out_ref[0:half, :] = ((mine - mean) * scale).astype(BF16)
    out_ref[half:rows, :] = ((got - mean) * scale).astype(BF16)
    high = mean.astype(BF16)
    rest = mean - high.astype(F32)
    mid = rest.astype(BF16)
    low = (rest - mid.astype(F32)).astype(BF16)
    out_ref[rows : rows + 16, :] = jnp.concatenate([high, mid, low, jnp.zeros((13, width), BF16)], axis=0)


def gram_kernel(
    place_ref, p0_ref, p1_ref, p2_ref, p3_ref, mine_ref, got_ref, side_ref, own_ref, other_ref, *, factor
):
    refs = (p0_ref, p1_ref, p2_ref, p3_ref)
    rows = p0_ref.shape[0] - 16
    half = rows // 2
    width = p0_ref.shape[1]
    here = pl.ds(pl.multiple_of(lax.rem(place_ref[0], 2) * width, 128), width)
    scale = side_ref[0:1, :]
    means = []
    for ref in refs:
        tail = ref[rows : rows + 16, :].astype(F32)
        means.append(tail[0:1, :] + (tail[1:2, :] + tail[2:3, :]))
    mean = ((means[0] + means[1]) + (means[2] + means[3])) * 0.25
    spreads = [
        (ref[0:rows, :].astype(F32) + scale * (m - mean)).astype(BF16) for ref, m in zip(refs, means)
    ]
    left_over = tree_sum([jnp.sum(s.astype(F32), axis=0, keepdims=True) for s in spreads]) / (4 * rows)
    over_high = left_over.astype(BF16)
    over_low = (left_over - over_high.astype(F32)).astype(BF16)
    over = jnp.concatenate([over_high, over_low, jnp.zeros((14, width), BF16)], axis=0)
    shift = scale * (side_ref[1:2, :] - mean)
    noise = jnp.concatenate([mine_ref[:, here], got_ref[:, here]], axis=0)
    right = shift + factor * noise
    high = right.astype(BF16)
    low = (right - high.astype(F32)).astype(BF16)
    left = jnp.concatenate([spreads[0], high, low, over], axis=0)
    at_over = dot_nt(left, over)
    at_over = at_over[:, 0:1] + at_over[:, 1:2]
    gram_over = at_over[0:rows]
    cross_over = at_over[rows : 2 * rows] + at_over[2 * rows : 3 * rows]
    both = at_over[3 * rows : 3 * rows + 1] + at_over[3 * rows + 1 : 3 * rows + 2]
    for i in range(4):
        part = dot_nt(left, spreads[i])
        over_row = part[3 * rows : 3 * rows + 1] + part[3 * rows + 1 : 3 * rows + 2]
        gram = part[0:rows] - gram_over - (over_row - both)
        cross = part[rows : 2 * rows] + part[2 * rows : 3 * rows] - cross_over
        own_ref[i, 0:half, :] = gram[0:half]
        own_ref[i, half:rows, :] = cross[0:half]
        other_ref[i, 0:half, :] = pltpu.roll(gram[half:rows], half, 1)
        other_ref[i, half:rows, :] = pltpu.roll(cross[half:rows], half, 1)


def local_ids(ids_ref, place, k):
    chip = lax.rem(lax.div(place, 2) + 4 - k, 4)
    ids = ids_ref[pl.ds(chip, 1), :]
    return jnp.where(lax.rem(place, 2) == 1, pltpu.roll(ids, 64, 1), ids)


def local_members(place, k, rows):
    chip = lax.rem(lax.div(place, 2) + 4 - k, 4)
    lane = lax.broadcasted_iota(jnp.int32, (rows, 128), 1)
    return chip * 128 + lax.rem(lane + 64 * lax.rem(place, 2), 128)


def begin_kernel(place_ref, ids_ref, own_ref, other_ref, inverse_ref, upper_ref, row_ref, m_ref):
    half, block = 64, 128
    place = place_ref[0]
    members = place * half + lax.broadcasted_iota(jnp.int32, (half, block), 0)
    for i in range(4):
        match = (local_ids(ids_ref, place, i) == members).astype(F32)
        m_ref[:, i * block : (i + 1) * block] = own_ref[i, half:block, :] + match

    def piece(i):
        return jnp.concatenate([own_ref[i, 0:half, :], pltpu.roll(other_ref[i], half, 1)], axis=0)

    inverse = invert_block(piece(0) + unit_block(block, block))
    inverse_ref[...] = inverse
    for i in range(1, 4):
        row_ref[:, (i - 1) * block : i * block] = piece(i)
    upper = dot_nn(inverse, row_ref[...], EXACT)
    upper_ref[...] = upper
    m_ref[:, block:] = m_ref[:, block:] - dot_nn(m_ref[:, :block], upper, EXACT)


def solve_kernel(
    place_ref, ids_ref, inverse_ref, upper_ref, row_ref, right_ref,
    g1_ref, g2_ref, g3_ref, h1_ref, h2_ref, h3_ref, out_ref, m_ref
):
    size, block, half = 512, 128, 64
    place = place_ref[0]
    unit = unit_block(block, block)

    def piece(mine, other, i):
        return jnp.concatenate([mine[i], pltpu.roll(other[i], half, 1)], axis=0)

    upper = upper_ref[...]
    row = row_ref[...]
    m_ref[...] = right_ref[...]
    a = {
        (1, 1): piece(g1_ref, h1_ref, 0) + unit,
        (1, 2): piece(g1_ref, h1_ref, 1),
        (2, 2): piece(g2_ref, h2_ref, 0) + unit,
        (2, 3): piece(g2_ref, h2_ref, 1),
        (3, 3): piece(g3_ref, h3_ref, 0) + unit,
        (1, 3): piece(g3_ref, h3_ref, 1).T,
    }
    inverses, uppers = {0: inverse_ref[...]}, {0: upper}
    for b in range(4):
        hi = (b + 1) * block
        if b:
            inverses[b] = invert_block(a[b, b])
            if hi < size:
                row = jnp.concatenate([a[b, j] for j in range(b + 1, 4)], axis=1)
                upper = dot_nn(inverses[b], row, EXACT)
                uppers[b] = upper
                m_ref[:, hi:] = m_ref[:, hi:] - dot_nn(m_ref[:, hi - block : hi], upper, EXACT)
        for i in range(b + 1, 4):
            left = row[:, (i - b - 1) * block : (i - b) * block]
            change = dot_tn(left, upper[:, (i - b - 1) * block :], EXACT)
            for j in range(i, 4):
                a[i, j] = a[i, j] - change[:, (j - i) * block : (j - i + 1) * block]
    for b in range(3, -1, -1):
        lo, hi = b * block, (b + 1) * block
        z = dot_nn(m_ref[:, lo:hi], inverses[b], EXACT)
        if hi < size:
            z = z - dot_nt(m_ref[:, hi:size], uppers[b], EXACT)
        m_ref[:, lo:hi] = z

    columns = jnp.concatenate(
        [jnp.broadcast_to(local_ids(ids_ref, place, k), (block, block)).T for k in range(4)], axis=0
    )
    own = place * half + lax.broadcasted_iota(jnp.int32, (half, block), 0)
    for k in range(4):
        match = (columns == local_members(place, k, size)).astype(F32)
        ordered = dot_nn(m_ref[...], match, EXACT)
        own_unit = (own == local_members(place, k, half)).astype(F32)
        out_ref[:, k * block : (k + 1) * block] = (ordered - own_unit).astype(BF16)


def update_kernel(t_ref, *rest):
    refs, out_ref = rest[:-1], rest[-1]
    members = t_ref.shape[1]
    mean = tree_sum([jnp.sum(ref[...].astype(F32), axis=0, keepdims=True) for ref in refs]) / members
    anomaly = jnp.concatenate([(ref[...].astype(F32) - mean).astype(BF16) for ref in refs], axis=0)
    increment = dot_nn(t_ref[...], anomaly)
    out_ref[...] = (refs[0][...].astype(F32) + increment).astype(BF16)


def body(members_field, predicted, noise, observed, obs_precision, obs_block, block_error_scale, member_ids):
    rows, width = predicted.shape
    members = member_ids.shape[0]
    cells = members_field.shape[1]
    half = width // 2
    factor = float(1.0 / (members - 1) ** 0.5)
    place = lax.axis_index("ens").reshape(1).astype(jnp.int32)
    swap = [(i, i ^ 1) for i in range(8)]
    smem = pl.BlockSpec(memory_space=pltpu.SMEM)
    vmem = pl.BlockSpec(memory_space=pltpu.VMEM)
    params = pltpu.CompilerParams(vmem_limit_bytes=32 * MIB)

    def shaped(*shape, dtype=F32):
        return jax.ShapeDtypeStruct(shape, dtype)

    def turned(array, steps):
        return lax.ppermute(array, "ens", [(i, (i + 2 * steps) % 8) for i in range(8)])

    def swapped(array):
        return lax.ppermute(array, "ens", swap)

    pred_got = swapped(predicted)
    noise_got = swapped(noise)
    facts = jnp.stack([obs_precision, observed, obs_block.astype(F32)])
    payload, side = pl.pallas_call(
        functools.partial(prepare_kernel, factor=factor),
        out_shape=(shaped(2 * rows + 16, half, dtype=BF16), shaped(8, half)),
        in_specs=[smem, smem, vmem, vmem, vmem],
        compiler_params=params,
        name="prepare",
    )(place, block_error_scale, predicted, pred_got, facts)
    payloads = [payload] + [turned(payload, k) for k in (1, 2, 3)]

    after_spread = lax.optimization_barrier((members_field, *payloads))
    field, payloads = after_spread[0], after_spread[1:]
    back, ahead = turned(field, 1), turned(field, 3)

    own, other = pl.pallas_call(
        functools.partial(gram_kernel, factor=factor),
        out_shape=(shaped(4, 2 * rows, 2 * rows),) * 2,
        in_specs=[smem] + [vmem] * 7,
        compiler_params=params,
        name="gram",
    )(place, *payloads, noise, noise_got, side)
    part = own + swapped(other)

    spread_out = lax.all_to_all(part.reshape(32, 16, 128), "space", split_axis=0, concat_axis=0)
    summed = jnp.sum(spread_out, axis=0)
    summed, back, ahead = lax.optimization_barrier((summed, back, ahead))
    cut = rows // 2
    beyond = [turned(back[:cut], 1), turned(ahead[cut:], 3)]
    whole = lax.all_to_all(
        jnp.broadcast_to(summed[None], (32, 16, 128)), "space", split_axis=0, concat_axis=0
    ).reshape(4, 2 * rows, 2 * rows)

    whole, *beyond = lax.optimization_barrier((whole, *beyond))
    gram = whole[:, :rows]
    near = gram[0:2]
    far = jnp.stack([gram[0], gram[2]])
    grams = [turned(near, 1), turned(near, 2), turned(far, 3)]
    ids = member_ids.reshape(4, 128)
    inverse, upper, row, right = pl.pallas_call(
        begin_kernel,
        out_shape=(shaped(128, 128), shaped(128, 384), shaped(128, 384), shaped(rows, members)),
        in_specs=[smem] + [vmem] * 3,
        compiler_params=params,
        name="begin",
    )(place, ids, whole, swapped(gram))
    inverse, *grams = lax.optimization_barrier((inverse, *grams))
    grams = grams + [swapped(g) for g in grams]
    inverse, *ready = lax.optimization_barrier((inverse, *grams, field, back, *beyond, ahead))
    grams, shares = ready[:6], ready[6:]
    others = [swapped(f) for f in shares]
    transform = pl.pallas_call(
        solve_kernel,
        out_shape=shaped(rows, members, dtype=BF16),
        in_specs=[smem] + [vmem] * 11,
        scratch_shapes=[pltpu.VMEM((rows, members), F32)],
        compiler_params=params,
        name="solve",
    )(place, ids, inverse, upper, row, right, *grams)

    pieces = [field, others[0], back, others[1], *shares[2:4], *others[2:4], ahead, others[4]]
    wide = 1024
    strips = [pl.BlockSpec((piece.shape[0], wide), lambda i: (0, i)) for piece in pieces]
    return pl.pallas_call(
        update_kernel,
        grid=(cells // wide,),
        out_shape=shaped(rows, cells, dtype=BF16),
        in_specs=[pl.BlockSpec((rows, members), lambda i: (0, 0))] + strips,
        out_specs=strips[0],
        compiler_params=params,
        name="update",
    )(transform, *pieces)


def solution(mesh):
    placed = (
        P("ens", "space"),
        P("ens", "space"),
        P("ens", "space"),
        P("space"),
        P("space"),
        P("space"),
        P(),
        P(),
    )
    return jax.shard_map(
        body, mesh=mesh, in_specs=placed, out_specs=P("ens", "space"), check_vma=False
    )
```

time: 125 us -> 106 us (0.85)
  between operations: 13.5 us -> 0.2 us
  other arithmetic: 8.21 us -> 0.1 us
  local copies, waits for them, and re-layouts: 8.66 us -> 3.15 us
  blocking collectives: 35 us -> 40.5 us
  matrix products: 3 us -> 0 us
  Pallas kernels: 25.2 us -> 28 us
  waiting for transfers between devices: 11.1 us -> 13.4 us
    reduce_sum x2 -> x0, other arithmetic: 6.36 us -> none  [the longest x1 5.62 us: body(): field_mean = jnp.sum(field, axis=0, dtype=F32) / members]
    dynamic_slice x4 -> x0, local copies, waits for them, and re-layouts: 4.91 us -> none  [cut(): return lax.dynamic_slice_in_dim(array, which * half, half, array.ndim - 1)]
    pallas_call x2 -> x4, Pallas kernels: 22.4 us -> 26.8 us  [the longest x1 15.2 us: body(): pl.pallas_call(solve_kernel, out_shape=shaped(rows, members, dtype=BF16),...]
    all_to_all x1, blocking collectives: 16.2 us -> 19.8 us  [body(): lax.all_to_all(jnp.broadcast_to(summed[None], (32, 16, 128)), 'space', sp...]
    dot_general x1 -> x0, matrix products: 3 us -> none  [body(): increment = jnp.dot(transform, anomaly, preferred_element_type=F32)]
    ppermute x6 -> x10, waiting for transfers between devices: 8.59 us -> 11.3 us  [turned(): lax.ppermute(array, 'ens', [(i, (i + 2 * steps) % 8) for i in range(8)])]
    all_to_all x1, blocking collectives: 18.8 us -> 20.7 us  [body(): lax.all_to_all(part.reshape(32, 16, 128), 'space', split_axis=0, concat_a...]
    pallas_call x1, Pallas kernels: 2.81 us -> 1.22 us  [body(): pl.pallas_call(functools.partial(gram_kernel, factor=factor), out_shape=(...]
  transfers between devices with their start and end apart: 11 -> 22, of which waited for: 6 -> 8; matrix products, arithmetic and copies ran while one was open for 8% -> 1% of each run, Pallas kernels for 20% -> 20%
where the time goes in v2:
time: 106 us; the launch traced here: 105 us
  blocking collectives  40.5 us (38%)
  Pallas kernels  28 us (26%)
  starting transfers between devices  19.9 us (19%)
  waiting for transfers between devices  13.4 us (13%)
  local copies, waits for them, and re-layouts  3.15 us (3%)
    all_to_all x1, blocking collectives, body(): lax.all_to_all(part.reshape(32, 16, 128), 'space', split_axis=0, concat_a...  20.7 us
    all_to_all x1, blocking collectives, body(): lax.all_to_all(jnp.broadcast_to(summed[None], (32, 16, 128)), 'space', sp...  19.8 us
    pallas_call x1, Pallas kernels, body(): pl.pallas_call(solve_kernel, out_shape=shaped(rows, members, dtype=BF16),...  15.2 us
    ppermute x12, starting transfers between devices, swapped(): return lax.ppermute(array, 'ens', swap)  12.3 us
    ppermute x10, waiting for transfers between devices, turned(): lax.ppermute(array, 'ens', [(i, (i + 2 * steps) % 8) for i in range(8)])  11.3 us
    ppermute x10, starting transfers between devices, turned(): lax.ppermute(array, 'ens', [(i, (i + 2 * steps) % 8) for i in range(8)])  7.63 us
    pallas_call x1, Pallas kernels, body(): pl.pallas_call(update_kernel, grid=(cells // wide,), out_shape=shaped(row...  6.4 us
    pallas_call x1, Pallas kernels, body(): pl.pallas_call(begin_kernel, out_shape=(shaped(128, 128), shaped(128, 384...  4.55 us
  transfers between devices with their start and end apart: 22, of which 8 were waited for; matrix products, arithmetic and copies ran while one was open for 1% of the time, Pallas kernels for 20%

profile of v2, /device:TPU:1, one launch (start us, length us, event | category | flops | bytes accessed | tf_op | source)
XLA Modules:
  0.0 105.3 jit_solution(8749038937787354722)
XLA Ops:
  0.0 3.2 %collective-permute-start = (f32[64,1280]{1,0:T(8,128)}, f32[64,1280]{1,0:T(8,128)S(1)}, u32[]{:S(2)}, u32[]{:S(2)}) collective-permute-start(f32[64,1280]{1,0:T(8,128)} %mine_ref.2), channel_id=1, source_target_pairs={{0,32},{32,0},{64,96},{96,64},{128,160},{160,128},{192,224},{224,1... | collective-permute-start | bytes 983048 | tf_op jit(solution)/shard_map/ppermute | solution.py:259
  3.2 0.7 stack.16
  4.0 0.7 copy-done.5
  4.7 0.0 copy-start.4
  4.7 0.0 collective-permute-done.got_ref
  4.7 0.6 copy-done.4
  5.4 1.0 copy-done.2
  6.3 0.6 prepare.1
  7.0 0.8 collective-permute-start.3
  7.8 0.5 collective-permute-start.2
  8.3 0.6 collective-permute-start.1
  8.9 0.8 collective-permute-start.4
  9.7 3.6 %collective-permute-done.3.p3_ref = bf16[144,640]{1,0:T(8,128)(2,1)S(1)} collective-permute-done((bf16[144,640]{1,0:T(8,128)(2,1)S(1)}, bf16[144,640]{1,0:T(8,128)(2,1)S(1)}, u32[]{:S(2)}, u32[]{:S(2)}) %collective-permute-start.3) | collective-permute-done | bytes 184352 | tf_op jit(solution)/shard_map/ppermute | solution.py:256
  13.3 2.0 %collective-permute-done.2.p2_ref = bf16[144,640]{1,0:T(8,128)(2,1)S(1)} collective-permute-done((bf16[144,640]{1,0:T(8,128)(2,1)S(1)}, bf16[144,640]{1,0:T(8,128)(2,1)S(1)}, u32[]{:S(2)}, u32[]{:S(2)}) %collective-permute-start.2) | collective-permute-done | bytes 184352 | tf_op jit(solution)/shard_map/ppermute | solution.py:256
  15.3 4.5 %collective-permute-done.1.p1_ref = bf16[144,640]{1,0:T(8,128)(2,1)S(1)} collective-permute-done((bf16[144,640]{1,0:T(8,128)(2,1)S(1)}, bf16[144,640]{1,0:T(8,128)(2,1)S(1)}, u32[]{:S(2)}, u32[]{:S(2)}) %collective-permute-start.1) | collective-permute-done | bytes 184352 | tf_op jit(solution)/shard_map/ppermute | solution.py:256
  19.8 1.5 %collective-permute-start.6 = (bf16[64,8192]{1,0:T(8,128)(2,1)}, bf16[64,8192]{1,0:T(8,128)(2,1)S(1)}, u32[]{:S(2)}, u32[]{:S(2)}) collective-permute-start(bf16[64,8192]{1,0:T(8,128)(2,1)} %rest_0_), channel_id=1, source_target_pairs={{0,64},{32,96},{64,128},{96,160},{128,192},{160,224},{192,0},{224,... | collective-permute-start | bytes 3145736 | tf_op jit(solution)/shard_map/ppermute | solution.py:256
  21.3 1.2 %gram.1 = (f32[4,128,128]{2,1,0:T(8,128)S(1)}, f32[4,128,128]{2,1,0:T(8,128)S(1)}) custom-call(s32[1]{0:T(128)} %bitcast.place_ref, bf16[144,640]{1,0:T(8,128)(2,1)S(1)} %get-tuple-element.41.p0_ref, bf16[144,640]{1,0:T(8,128)(2,1)S(1)} %collective-permute-done.1.p1_ref, bf16[144,640]{1,0:T(8,128)(2,1)S(1)} %collective-permute-done.2.p2_ref, ...), custom_call_target="tpu_custom_call" | custom-call | tf_op jit(solution)/shard_map/gram/pallas_call | solution.py:277
  22.5 1.1 %collective-permute-start.5 = (f32[4,128,128]{2,1,0:T(8,128)S(1)}, f32[4,128,128]{2,1,0:T(8,128)S(1)}, u32[]{:S(2)}, u32[]{:S(2)}) collective-permute-start(f32[4,128,128]{2,1,0:T(8,128)S(1)} %get-tuple-element.47), channel_id=1, source_target_pairs={{0,32},{32,0},{64,96},{96,64},{128,160},{160,128},{192,224},{224,1... | collective-permute-start | bytes 786440 | tf_op jit(solution)/shard_map/ppermute | solution.py:259
  23.6 1.2 %collective-permute-done.5 = f32[4,128,128]{2,1,0:T(8,128)S(1)} collective-permute-done((f32[4,128,128]{2,1,0:T(8,128)S(1)}, f32[4,128,128]{2,1,0:T(8,128)S(1)}, u32[]{:S(2)}, u32[]{:S(2)}) %collective-permute-start.5) | collective-permute-done | bytes 262176 | tf_op jit(solution)/shard_map/ppermute | solution.py:259
  24.8 20.7 %all_to_all.10 = f32[32,16,128]{2,1,0:T(8,128)S(1)} all-to-all(f32[32,16,128]{2,1,0:T(8,128)S(1)} %bitcast.10), channel_id=1, replica_groups=mesh['ens'=8,'space'=32] {'space'}, dimensions={0} | all-to-all | bytes 524288 | tf_op jit(solution)/shard_map/all_to_all | solution.py:286
  45.6 0.0 collective-permute-done.6.rest_2_
  45.7 0.0 copy-start
  45.7 1.6 %collective-permute-start.9 = (bf16[32,8192]{1,0:T(8,128)(2,1)S(1)}, bf16[32,8192]{1,0:T(8,128)(2,1)S(1)}, u32[]{:S(2)}, u32[]{:S(2)}) collective-permute-start(bf16[32,8192]{1,0:T(8,128)(2,1)S(1)} %slice.22), channel_id=1, source_target_pairs={{0,192},{32,224},{64,0},{96,32},{128,64},{160,96},{192,128},{224,1... | collective-permute-start | bytes 1572872 | tf_op jit(solution)/shard_map/ppermute | solution.py:256
  47.3 0.0 collective-permute-start.8
  47.3 19.8 %all_to_all.11 = f32[32,16,128]{2,1,0:T(8,128)S(1)} all-to-all(f32[32,16,128]{2,1,0:T(8,128)S(1)} %broadcast_in_dim.2), channel_id=1, replica_groups=mesh['ens'=8,'space'=32] {'space'}, dimensions={0} | all-to-all | bytes 524288 | tf_op jit(solution)/shard_map/all_to_all | solution.py:291
  67.1 0.0 collective-permute-done.9.rest_5_
  67.1 0.0 collective-permute-done.8.rest_4_
  67.1 4.4 %collective-permute-start.10 = (f32[4,64,128]{2,1,0:T(8,128)S(1)}, f32[4,64,128]{2,1,0:T(8,128)S(1)}, u32[]{:S(2)}, u32[]{:S(2)}) collective-permute-start(f32[4,64,128]{2,1,0:T(8,128)S(1)} %slice.23), channel_id=1, source_target_pairs={{0,32},{32,0},{64,96},{96,64},{128,160},{160,128},{192,224},{224,1... | collective-permute-start | bytes 393224 | tf_op jit(solution)/shard_map/ppermute | solution.py:259
  71.5 1.8 %collective-permute-start.13 = (f32[2,64,128]{2,1,0:T(8,128)S(1)}, f32[2,64,128]{2,1,0:T(8,128)S(1)}, u32[]{:S(2)}, u32[]{:S(2)}) collective-permute-start(f32[2,64,128]{2,1,0:T(8,128)S(1)} %pad_maximum_fusion), channel_id=1, source_target_pairs={{0,192},{32,224},{64,0},{96,32},{128,64},{160,96},{192,128},{224,1... | collective-permute-start | bytes 196616 | tf_op jit(solution)/shard_map/ppermute | solution.py:256
  73.4 0.8 collective-permute-start.12
  74.1 0.0 collective-permute-start.11
  74.1 0.0 collective-permute-done.10.other_ref
  74.1 4.5 %begin.1 = (f32[128,128]{1,0:T(8,128)S(1)}, f32[128,384]{1,0:T(8,128)S(1)}, f32[128,384]{1,0:T(8,128)S(1)}, f32[64,512]{1,0:T(8,128)S(1)}) custom-call(s32[1]{0:T(128)} %bitcast.place_ref, s32[4,128]{1,0:T(4,128)S(1)} %bitcast.8, f32[4,128,128]{2,1,0:T(8,128)S(1)} %bitcast.7, f32[4,64,128]{2,1,0:T(8,128)S(1)} %collective-permute-done.10.other_ref), custom_call_target="tpu_custom_call" | custom-call | tf_op jit(solution)/shard_map/begin/pallas_call | solution.py:301
  78.7 0.0 collective-permute-done.13.g3_ref
  78.7 1.2 %collective-permute-done.11.g1_ref = f32[2,64,128]{2,1,0:T(8,128)S(1)} collective-permute-done((f32[2,64,128]{2,1,0:T(8,128)S(1)}, f32[2,64,128]{2,1,0:T(8,128)S(1)}, u32[]{:S(2)}, u32[]{:S(2)}) %collective-permute-start.11) | collective-permute-done | bytes 65568 | tf_op jit(solution)/shard_map/ppermute | solution.py:256
  79.9 0.8 collective-permute-start.14
  80.8 0.0 collective-permute-start.15
  80.8 0.5 collective-permute-start.16
  81.3 0.4 collective-permute-done.14.h1_ref
  81.7 0.4 collective-permute-done.15.h2_ref
  82.0 0.2 collective-permute-done.16.h3_ref
  82.2 0.4 collective-permute-start.17
  82.5 0.2 collective-permute-start.18
  82.7 0.4 collective-permute-start.21
  83.0 0.2 collective-permute-start.19
  83.2 0.4 collective-permute-start.20
  83.6 15.2 %solve.1.t_ref = bf16[64,512]{1,0:T(8,128)(2,1)S(1)} custom-call(s32[1]{0:T(128)} %bitcast.place_ref, s32[4,128]{1,0:T(4,128)S(1)} %bitcast.9, f32[128,128]{1,0:T(8,128)S(1)} %get-tuple-element.60.inverse_ref, f32[128,384]{1,0:T(8,128)S(1)} %get-tuple-element.61.upper_ref, f32[128,384]{1,0:T(8,128)S(1)} %get-tuple-element.62.row_ref, ...), custom_call_target="tpu_custom_call" | custom-call | tf_op jit(solution)/shard_map/solve/pallas_call | solution.py:313
  98.9 6.4 %update.1 = bf16[64,8192]{1,0:T(8,128)(2,1)} custom-call(bf16[64,512]{1,0:T(8,128)(2,1)S(1)} %solve.1.t_ref, bf16[64,8192]{1,0:T(8,128)(2,1)S(1)} %copy-done, bf16[64,8192]{1,0:T(8,128)(2,1)S(1)} %collective-permute-done.17.rest_1_, bf16[64,8192]{1,0:T(8,128)(2,1)S(1)} %collective-permute-done.6.rest_2_, ...), custom_call_target="tpu_custom_call" | custom-call | tf_op jit(solution)/shard_map/update/pallas_call | solution.py:325
  (31 shorter events, 0.3 us)
Async XLA Ops:
  0.0 4.7 %collective-permute-start = (f32[64,1280]{1,0:T(8,128)}, f32[64,1280]{1,0:T(8,128)S(1)}, u32[]{:S(2)}, u32[]{:S(2)}) collective-permute-start(f32[64,1280]{1,0:T(8,128)} %mine_ref.2), channel_id=1, source_target_pairs={{0,32},{32,0},{64,96},{96,64},{128,160},{160,128},{192,224},{224,1... | collective-permute-start | bytes 983048 | tf_op jit(solution)/shard_map/ppermute | solution.py:259
  3.2 0.7 copy-start.6
  4.0 0.7 copy-start.5
  4.7 0.7 copy-start.4
  5.3 1.0 copy-start.2
  6.3 2.6 %copy-start.1 = (f32[64,1280]{1,0:T(8,128)S(1)}, f32[64,1280]{1,0:T(8,128)}, u32[]{:S(2)}) copy-start(f32[64,1280]{1,0:T(8,128)} %mine_ref.3) | copy-start | bytes 983044
  7.0 6.3 %collective-permute-start.3 = (bf16[144,640]{1,0:T(8,128)(2,1)S(1)}, bf16[144,640]{1,0:T(8,128)(2,1)S(1)}, u32[]{:S(2)}, u32[]{:S(2)}) collective-permute-start(bf16[144,640]{1,0:T(8,128)(2,1)S(1)} %get-tuple-element.41.p0_ref), channel_id=1, source_target_pairs={{0,192},{32,224},{64,0},{96,32},{128,64},{160,96},{192,128},{224,1... | collective-permute-start | bytes 552968 | tf_op jit(solution)/shard_map/ppermute | solution.py:256
  7.8 7.5 %collective-permute-start.2 = (bf16[144,640]{1,0:T(8,128)(2,1)S(1)}, bf16[144,640]{1,0:T(8,128)(2,1)S(1)}, u32[]{:S(2)}, u32[]{:S(2)}) collective-permute-start(bf16[144,640]{1,0:T(8,128)(2,1)S(1)} %get-tuple-element.41.p0_ref), channel_id=1, source_target_pairs={{0,128},{32,160},{64,192},{96,224},{128,0},{160,32},{192,64},{224,... | collective-permute-start | bytes 552968 | tf_op jit(solution)/shard_map/ppermute | solution.py:256
  8.3 11.5 %collective-permute-start.1 = (bf16[144,640]{1,0:T(8,128)(2,1)S(1)}, bf16[144,640]{1,0:T(8,128)(2,1)S(1)}, u32[]{:S(2)}, u32[]{:S(2)}) collective-permute-start(bf16[144,640]{1,0:T(8,128)(2,1)S(1)} %get-tuple-element.41.p0_ref), channel_id=1, source_target_pairs={{0,64},{32,96},{64,128},{96,160},{128,192},{160,224},{192,0},{224,... | collective-permute-start | bytes 552968 | tf_op jit(solution)/shard_map/ppermute | solution.py:256
  8.9 12.4 %collective-permute-start.4 = (f32[64,1280]{1,0:T(8,128)S(1)}, f32[64,1280]{1,0:T(8,128)S(1)}, u32[]{:S(2)}, u32[]{:S(2)}) collective-permute-start(f32[64,1280]{1,0:T(8,128)S(1)} %copy-done.1), channel_id=1, source_target_pairs={{0,32},{32,0},{64,96},{96,64},{128,160},{160,128},{192,224},{224,1... | collective-permute-start | bytes 983048 | tf_op jit(solution)/shard_map/ppermute | solution.py:259
  19.8 25.8 %collective-permute-start.7 = (bf16[64,8192]{1,0:T(8,128)(2,1)}, bf16[64,8192]{1,0:T(8,128)(2,1)S(1)}, u32[]{:S(2)}, u32[]{:S(2)}) collective-permute-start(bf16[64,8192]{1,0:T(8,128)(2,1)} %rest_0_), channel_id=1, source_target_pairs={{0,192},{32,224},{64,0},{96,32},{128,64},{160,96},{192,128},{224,1... | collective-permute-start | bytes 3145736 | tf_op jit(solution)/shard_map/ppermute | solution.py:256
  19.8 25.8 %collective-permute-start.6 = (bf16[64,8192]{1,0:T(8,128)(2,1)}, bf16[64,8192]{1,0:T(8,128)(2,1)S(1)}, u32[]{:S(2)}, u32[]{:S(2)}) collective-permute-start(bf16[64,8192]{1,0:T(8,128)(2,1)} %rest_0_), channel_id=1, source_target_pairs={{0,64},{32,96},{64,128},{96,160},{128,192},{160,224},{192,0},{224,... | collective-permute-start | bytes 3145736 | tf_op jit(solution)/shard_map/ppermute | solution.py:256
  22.5 2.3 %collective-permute-start.5 = (f32[4,128,128]{2,1,0:T(8,128)S(1)}, f32[4,128,128]{2,1,0:T(8,128)S(1)}, u32[]{:S(2)}, u32[]{:S(2)}) collective-permute-start(f32[4,128,128]{2,1,0:T(8,128)S(1)} %get-tuple-element.47), channel_id=1, source_target_pairs={{0,32},{32,0},{64,96},{96,64},{128,160},{160,128},{192,224},{224,1... | collective-permute-start | bytes 786440 | tf_op jit(solution)/shard_map/ppermute | solution.py:259
  45.7 36.5 %copy-start = (bf16[64,8192]{1,0:T(8,128)(2,1)S(1)}, bf16[64,8192]{1,0:T(8,128)(2,1)}, u32[]{:S(2)}) copy-start(bf16[64,8192]{1,0:T(8,128)(2,1)} %rest_0_) | copy-start | bytes 3145732
  45.7 21.4 %collective-permute-start.9 = (bf16[32,8192]{1,0:T(8,128)(2,1)S(1)}, bf16[32,8192]{1,0:T(8,128)(2,1)S(1)}, u32[]{:S(2)}, u32[]{:S(2)}) collective-permute-start(bf16[32,8192]{1,0:T(8,128)(2,1)S(1)} %slice.22), channel_id=1, source_target_pairs={{0,192},{32,224},{64,0},{96,32},{128,64},{160,96},{192,128},{224,1... | collective-permute-start | bytes 1572872 | tf_op jit(solution)/shard_map/ppermute | solution.py:256
  47.3 19.8 %collective-permute-start.8 = (bf16[32,8192]{1,0:T(8,128)(2,1)S(1)}, bf16[32,8192]{1,0:T(8,128)(2,1)S(1)}, u32[]{:S(2)}, u32[]{:S(2)}) collective-permute-start(bf16[32,8192]{1,0:T(8,128)(2,1)S(1)} %slice.21), channel_id=1, source_target_pairs={{0,64},{32,96},{64,128},{96,160},{128,192},{160,224},{192,0},{224,... | collective-permute-start | bytes 1572872 | tf_op jit(solution)/shard_map/ppermute | solution.py:256
  67.1 7.0 %collective-permute-start.10 = (f32[4,64,128]{2,1,0:T(8,128)S(1)}, f32[4,64,128]{2,1,0:T(8,128)S(1)}, u32[]{:S(2)}, u32[]{:S(2)}) collective-permute-start(f32[4,64,128]{2,1,0:T(8,128)S(1)} %slice.23), channel_id=1, source_target_pairs={{0,32},{32,0},{64,96},{96,64},{128,160},{160,128},{192,224},{224,1... | collective-permute-start | bytes 393224 | tf_op jit(solution)/shard_map/ppermute | solution.py:259
  71.5 2.6 %copy-start.3 = (s32[512]{0:T(512)S(1)}, s32[512]{0:T(512)}, u32[]{:S(2)}) copy-start(s32[512]{0:T(512)} %param.15) | copy-start | bytes 6148
  71.5 7.2 %collective-permute-start.13 = (f32[2,64,128]{2,1,0:T(8,128)S(1)}, f32[2,64,128]{2,1,0:T(8,128)S(1)}, u32[]{:S(2)}, u32[]{:S(2)}) collective-permute-start(f32[2,64,128]{2,1,0:T(8,128)S(1)} %pad_maximum_fusion), channel_id=1, source_target_pairs={{0,192},{32,224},{64,0},{96,32},{128,64},{160,96},{192,128},{224,1... | collective-permute-start | bytes 196616 | tf_op jit(solution)/shard_map/ppermute | solution.py:256
  73.4 5.3 %collective-permute-start.12 = (f32[2,64,128]{2,1,0:T(8,128)S(1)}, f32[2,64,128]{2,1,0:T(8,128)S(1)}, u32[]{:S(2)}, u32[]{:S(2)}) collective-permute-start(f32[2,64,128]{2,1,0:T(8,128)S(1)} %slice.24), channel_id=1, source_target_pairs={{0,128},{32,160},{64,192},{96,224},{128,0},{160,32},{192,64},{224,... | collective-permute-start | bytes 196616 | tf_op jit(solution)/shard_map/ppermute | solution.py:256
  74.1 5.8 %collective-permute-start.11 = (f32[2,64,128]{2,1,0:T(8,128)S(1)}, f32[2,64,128]{2,1,0:T(8,128)S(1)}, u32[]{:S(2)}, u32[]{:S(2)}) collective-permute-start(f32[2,64,128]{2,1,0:T(8,128)S(1)} %slice.24), channel_id=1, source_target_pairs={{0,64},{32,96},{64,128},{96,160},{128,192},{160,224},{192,0},{224,... | collective-permute-start | bytes 196616 | tf_op jit(solution)/shard_map/ppermute | solution.py:256
  79.9 1.7 %collective-permute-start.14 = (f32[2,64,128]{2,1,0:T(8,128)S(1)}, f32[2,64,128]{2,1,0:T(8,128)S(1)}, u32[]{:S(2)}, u32[]{:S(2)}) collective-permute-start(f32[2,64,128]{2,1,0:T(8,128)S(1)} %collective-permute-done.11.g1_ref), channel_id=1, source_target_pairs={{0,32},{32,0},{64,96},{96,64},{128,160},{160,128},{192,224},{224,1... | collective-permute-start | bytes 196616 | tf_op jit(solution)/shard_map/ppermute | solution.py:259
  80.8 1.3 %collective-permute-start.15 = (f32[2,64,128]{2,1,0:T(8,128)S(1)}, f32[2,64,128]{2,1,0:T(8,128)S(1)}, u32[]{:S(2)}, u32[]{:S(2)}) collective-permute-start(f32[2,64,128]{2,1,0:T(8,128)S(1)} %collective-permute-done.12.g2_ref), channel_id=1, source_target_pairs={{0,32},{32,0},{64,96},{96,64},{128,160},{160,128},{192,224},{224,1... | collective-permute-start | bytes 196616 | tf_op jit(solution)/shard_map/ppermute | solution.py:259
  80.8 1.4 %collective-permute-start.16 = (f32[2,64,128]{2,1,0:T(8,128)S(1)}, f32[2,64,128]{2,1,0:T(8,128)S(1)}, u32[]{:S(2)}, u32[]{:S(2)}) collective-permute-start(f32[2,64,128]{2,1,0:T(8,128)S(1)} %collective-permute-done.13.g3_ref), channel_id=1, source_target_pairs={{0,32},{32,0},{64,96},{96,64},{128,160},{160,128},{192,224},{224,1... | collective-permute-start | bytes 196616 | tf_op jit(solution)/shard_map/ppermute | solution.py:259
  82.2 16.6 %collective-permute-start.17 = (bf16[64,8192]{1,0:T(8,128)(2,1)S(1)}, bf16[64,8192]{1,0:T(8,128)(2,1)S(1)}, u32[]{:S(2)}, u32[]{:S(2)}) collective-permute-start(bf16[64,8192]{1,0:T(8,128)(2,1)S(1)} %copy-done), channel_id=1, source_target_pairs={{0,32},{32,0},{64,96},{96,64},{128,160},{160,128},{192,224},{224,1... | collective-permute-start | bytes 3145736 | tf_op jit(solution)/shard_map/ppermute | solution.py:259
  82.5 16.3 %collective-permute-start.18 = (bf16[64,8192]{1,0:T(8,128)(2,1)S(1)}, bf16[64,8192]{1,0:T(8,128)(2,1)S(1)}, u32[]{:S(2)}, u32[]{:S(2)}) collective-permute-start(bf16[64,8192]{1,0:T(8,128)(2,1)S(1)} %collective-permute-done.6.rest_2_), channel_id=1, source_target_pairs={{0,32},{32,0},{64,96},{96,64},{128,160},{160,128},{192,224},{224,1... | collective-permute-start | bytes 3145736 | tf_op jit(solution)/shard_map/ppermute | solution.py:259
  82.7 16.2 %collective-permute-start.21 = (bf16[64,8192]{1,0:T(8,128)(2,1)S(1)}, bf16[64,8192]{1,0:T(8,128)(2,1)S(1)}, u32[]{:S(2)}, u32[]{:S(2)}) collective-permute-start(bf16[64,8192]{1,0:T(8,128)(2,1)S(1)} %collective-permute-done.7.rest_8_), channel_id=1, source_target_pairs={{0,32},{32,0},{64,96},{96,64},{128,160},{160,128},{192,224},{224,1... | collective-permute-start | bytes 3145736 | tf_op jit(solution)/shard_map/ppermute | solution.py:259
  83.0 15.8 %collective-permute-start.19 = (bf16[32,8192]{1,0:T(8,128)(2,1)S(1)}, bf16[32,8192]{1,0:T(8,128)(2,1)S(1)}, u32[]{:S(2)}, u32[]{:S(2)}) collective-permute-start(bf16[32,8192]{1,0:T(8,128)(2,1)S(1)} %collective-permute-done.8.rest_4_), channel_id=1, source_target_pairs={{0,32},{32,0},{64,96},{96,64},{128,160},{160,128},{192,224},{224,1... | collective-permute-start | bytes 1572872 | tf_op jit(solution)/shard_map/ppermute | solution.py:259
  83.2 15.6 %collective-permute-start.20 = (bf16[32,8192]{1,0:T(8,128)(2,1)S(1)}, bf16[32,8192]{1,0:T(8,128)(2,1)S(1)}, u32[]{:S(2)}, u32[]{:S(2)}) collective-permute-start(bf16[32,8192]{1,0:T(8,128)(2,1)S(1)} %collective-permute-done.9.rest_5_), channel_id=1, source_target_pairs={{0,32},{32,0},{64,96},{96,64},{128,160},{160,128},{192,224},{224,1... | collective-permute-start | bytes 1572872 | tf_op jit(solution)/shard_map/ppermute | solution.py:259

commit v3 on v2

--- a/solution.py
+++ b/solution.py
@@ -47,7 +47,7 @@
     return (at == lax.broadcasted_iota(jnp.int32, (rows, cols), 1)).astype(F32)
 
 
-def invert_block(block):
+def invert_block(block, beside=None):
     lanes = lax.broadcasted_iota(jnp.int32, (8, 128), 1)
     subs = lax.broadcasted_iota(jnp.int32, (8, 128), 0)
     tiles = [block[8 * i : 8 * i + 8, :] for i in range(16)]
@@ -72,21 +72,30 @@
             total = tree_sum([across_lanes(tiles[i], 8 * t + j) * rows[j] for j in range(8)])
             tiles[i] = jnp.where(panel, 0.0, tiles[i]) - total
         tiles[t] = row
+        if beside is not None:
+            beside(t)
     return jnp.concatenate(tiles, axis=0)
 
 
-def prepare_kernel(place_ref, table_ref, mine_ref, got_ref, facts_ref, out_ref, side_ref, *, factor):
+def prepare_kernel(place_ref, table_ref, facts_ref, mine_ref, got_ref, out_ref, side_ref, *, factor):
     half = mine_ref.shape[0]
     rows = 2 * half
     width = out_ref.shape[1]
-    here = pl.ds(pl.multiple_of(lax.rem(place_ref[0], 2) * width, 128), width)
-    block = facts_ref[2:3, here]
+    core = lax.rem(place_ref[0], 2)
+    here = pl.ds(pl.multiple_of(core * width, 128), width)
+
+    def line(which):
+        count = width // 128
+        return jnp.concatenate([facts_ref[which, pl.ds(core * count + j, 1), :] for j in range(count)], axis=1)
+
+    block = line(2)
     error_scale = jnp.zeros_like(block)
-    for b in range(table_ref.shape[0]):
-        error_scale = jnp.where(block == float(b), table_ref[b], error_scale)
-    scale = facts_ref[0:1, here] / error_scale * factor
-    side_ref[...] = jnp.concatenate([scale, facts_ref[1:2, here], jnp.zeros((6, width), F32)], axis=0)
-    mine = mine_ref[:, here]
+    for b in range(32):
+        level = jnp.broadcast_to(table_ref[:, b : b + 1], block.shape)
+        error_scale = jnp.where(block == float(b), level, error_scale)
+    scale = line(0) / error_scale * factor
+    side_ref[...] = jnp.concatenate([scale, line(1), jnp.zeros((6, width), F32)], axis=0)
+    mine = mine_ref[...]
     got = got_ref[:, here]
     mean = (jnp.sum(mine, axis=0, keepdims=True) + jnp.sum(got, axis=0, keepdims=True)) / rows
     out_ref[0:half, :] = ((mine - mean) * scale).astype(BF16)
@@ -120,7 +129,7 @@
     over_low = (left_over - over_high.astype(F32)).astype(BF16)
     over = jnp.concatenate([over_high, over_low, jnp.zeros((14, width), BF16)], axis=0)
     shift = scale * (side_ref[1:2, :] - mean)
-    noise = jnp.concatenate([mine_ref[:, here], got_ref[:, here]], axis=0)
+    noise = jnp.concatenate([mine_ref[...], got_ref[:, here]], axis=0)
     right = shift + factor * noise
     high = right.astype(BF16)
     low = (right - high.astype(F32)).astype(BF16)
@@ -156,11 +165,6 @@
 def begin_kernel(place_ref, ids_ref, own_ref, other_ref, inverse_ref, upper_ref, row_ref, m_ref):
     half, block = 64, 128
     place = place_ref[0]
-    members = place * half + lax.broadcasted_iota(jnp.int32, (half, block), 0)
-    for i in range(4):
-        match = (local_ids(ids_ref, place, i) == members).astype(F32)
-        m_ref[:, i * block : (i + 1) * block] = own_ref[i, half:block, :] + match
-
     def piece(i):
         return jnp.concatenate([own_ref[i, 0:half, :], pltpu.roll(other_ref[i], half, 1)], axis=0)
 
@@ -170,36 +174,57 @@
         row_ref[:, (i - 1) * block : i * block] = piece(i)
     upper = dot_nn(inverse, row_ref[...], EXACT)
     upper_ref[...] = upper
+    members = place * half + lax.broadcasted_iota(jnp.int32, (half, block), 0)
+    for i in range(4):
+        match = (local_ids(ids_ref, place, i) == members.astype(F32)).astype(F32)
+        m_ref[:, i * block : (i + 1) * block] = own_ref[i, half:block, :] + match
     m_ref[:, block:] = m_ref[:, block:] - dot_nn(m_ref[:, :block], upper, EXACT)
 
 
 def solve_kernel(
     place_ref, ids_ref, inverse_ref, upper_ref, row_ref, right_ref,
-    g1_ref, g2_ref, g3_ref, h1_ref, h2_ref, h3_ref, out_ref, m_ref
+    g1_ref, g2_ref, g3_ref, theirs_ref, *rest
 ):
+    fields, (out_ref, anomaly_ref, m_ref) = rest[:-3], rest[-3:]
     size, block, half = 512, 128, 64
     place = place_ref[0]
     unit = unit_block(block, block)
 
-    def piece(mine, other, i):
-        return jnp.concatenate([mine[i], pltpu.roll(other[i], half, 1)], axis=0)
+    def piece(mine, k, i):
+        return jnp.concatenate([mine[i], pltpu.roll(theirs_ref[2 * (k - 1) + i], half, 1)], axis=0)
+
+    def centre(strip):
+        here = slice(strip * block, (strip + 1) * block)
+        sums = [jnp.sum(ref[:, here].astype(F32), axis=0, keepdims=True) for ref in fields]
+        mean = tree_sum(sums) / size
+        at = 0
+        for ref in fields:
+            anomaly_ref[at : at + ref.shape[0], here] = (ref[:, here].astype(F32) - mean).astype(BF16)
+            at += ref.shape[0]
+
+    strips = anomaly_ref.shape[1] // block
+
+    def beside(b, t):
+        step = (b - 1) * 16 + t
+        for strip in range(step * strips // 48, (step + 1) * strips // 48):
+            centre(strip)
 
     upper = upper_ref[...]
     row = row_ref[...]
     m_ref[...] = right_ref[...]
     a = {
-        (1, 1): piece(g1_ref, h1_ref, 0) + unit,
-        (1, 2): piece(g1_ref, h1_ref, 1),
-        (2, 2): piece(g2_ref, h2_ref, 0) + unit,
-        (2, 3): piece(g2_ref, h2_ref, 1),
-        (3, 3): piece(g3_ref, h3_ref, 0) + unit,
-        (1, 3): piece(g3_ref, h3_ref, 1).T,
+        (1, 1): piece(g1_ref, 1, 0) + unit,
+        (1, 2): piece(g1_ref, 1, 1),
+        (2, 2): piece(g2_ref, 2, 0) + unit,
+        (2, 3): piece(g2_ref, 2, 1),
+        (3, 3): piece(g3_ref, 3, 0) + unit,
+        (1, 3): piece(g3_ref, 3, 1).T,
     }
     inverses, uppers = {0: inverse_ref[...]}, {0: upper}
     for b in range(4):
         hi = (b + 1) * block
         if b:
-            inverses[b] = invert_block(a[b, b])
+            inverses[b] = invert_block(a[b, b], functools.partial(beside, b))
             if hi < size:
                 row = jnp.concatenate([a[b, j] for j in range(b + 1, 4)], axis=1)
                 upper = dot_nn(inverses[b], row, EXACT)
@@ -222,19 +247,18 @@
     )
     own = place * half + lax.broadcasted_iota(jnp.int32, (half, block), 0)
     for k in range(4):
-        match = (columns == local_members(place, k, size)).astype(F32)
+        match = (columns == local_members(place, k, size).astype(F32)).astype(F32)
         ordered = dot_nn(m_ref[...], match, EXACT)
         own_unit = (own == local_members(place, k, half)).astype(F32)
         out_ref[:, k * block : (k + 1) * block] = (ordered - own_unit).astype(BF16)
 
 
-def update_kernel(t_ref, *rest):
-    refs, out_ref = rest[:-1], rest[-1]
-    members = t_ref.shape[1]
-    mean = tree_sum([jnp.sum(ref[...].astype(F32), axis=0, keepdims=True) for ref in refs]) / members
-    anomaly = jnp.concatenate([(ref[...].astype(F32) - mean).astype(BF16) for ref in refs], axis=0)
-    increment = dot_nn(t_ref[...], anomaly)
-    out_ref[...] = (refs[0][...].astype(F32) + increment).astype(BF16)
+def update_kernel(t_ref, field_ref, anomaly_ref, out_ref):
+    wide = 1024
+    for at in range(0, out_ref.shape[1], wide):
+        here = slice(at, at + wide)
+        increment = dot_nn(t_ref[...], anomaly_ref[:, here])
+        out_ref[:, here] = (field_ref[:, here].astype(F32) + increment).astype(BF16)
 
 
 def body(members_field, predicted, noise, observed, obs_precision, obs_block, block_error_scale, member_ids):
@@ -247,7 +271,9 @@
     swap = [(i, i ^ 1) for i in range(8)]
     smem = pl.BlockSpec(memory_space=pltpu.SMEM)
     vmem = pl.BlockSpec(memory_space=pltpu.VMEM)
-    params = pltpu.CompilerParams(vmem_limit_bytes=32 * MIB)
+
+    def room(mib):
+        return pltpu.CompilerParams(vmem_limit_bytes=mib * MIB)
 
     def shaped(*shape, dtype=F32):
         return jax.ShapeDtypeStruct(shape, dtype)
@@ -259,78 +285,85 @@
         return lax.ppermute(array, "ens", swap)
 
     pred_got = swapped(predicted)
-    noise_got = swapped(noise)
-    facts = jnp.stack([obs_precision, observed, obs_block.astype(F32)])
+    core = lax.rem(lax.axis_index("ens"), 2)
+    pred_mine = lax.dynamic_slice_in_dim(predicted, core * half, half, 1)
+    noise_mine = lax.dynamic_slice_in_dim(noise, core * half, half, 1)
+    facts = jnp.stack([a.reshape(-1, 128).astype(F32) for a in (obs_precision, observed, obs_block)])
+    table = jnp.pad(block_error_scale, (0, 128 - block_error_scale.shape[0])).reshape(1, 128)
     payload, side = pl.pallas_call(
         functools.partial(prepare_kernel, factor=factor),
         out_shape=(shaped(2 * rows + 16, half, dtype=BF16), shaped(8, half)),
-        in_specs=[smem, smem, vmem, vmem, vmem],
-        compiler_params=params,
+        in_specs=[smem] + [vmem] * 4,
+        compiler_params=room(32),
         name="prepare",
-    )(place, block_error_scale, predicted, pred_got, facts)
+    )(place, table, facts, pred_mine, pred_got)
+    payload, noise_after = lax.optimization_barrier((payload, noise))
+    noise_got = swapped(noise_after)
     payloads = [payload] + [turned(payload, k) for k in (1, 2, 3)]
 
-    after_spread = lax.optimization_barrier((members_field, *payloads))
-    field, payloads = after_spread[0], after_spread[1:]
+    ids = member_ids.astype(F32).reshape(4, 128)
+    after_spread = lax.optimization_barrier((members_field, noise_mine, ids, *payloads))
+    (field, noise_mine, ids), payloads = after_spread[:3], after_spread[3:]
     back, ahead = turned(field, 1), turned(field, 3)
 
     own, other = pl.pallas_call(
         functools.partial(gram_kernel, factor=factor),
         out_shape=(shaped(4, 2 * rows, 2 * rows),) * 2,
         in_specs=[smem] + [vmem] * 7,
-        compiler_params=params,
+        compiler_params=room(8),
         name="gram",
-    )(place, *payloads, noise, noise_got, side)
+    )(place, *payloads, noise_mine, noise_got, side)
     part = own + swapped(other)
 
     spread_out = lax.all_to_all(part.reshape(32, 16, 128), "space", split_axis=0, concat_axis=0)
     summed = jnp.sum(spread_out, axis=0)
-    summed, back, ahead = lax.optimization_barrier((summed, back, ahead))
+    summed, back, ahead, near_field = lax.optimization_barrier((summed, back, ahead, field))
     cut = rows // 2
     beyond = [turned(back[:cut], 1), turned(ahead[cut:], 3)]
+    others = [swapped(back), swapped(ahead), swapped(near_field)]
     whole = lax.all_to_all(
         jnp.broadcast_to(summed[None], (32, 16, 128)), "space", split_axis=0, concat_axis=0
     ).reshape(4, 2 * rows, 2 * rows)
 
-    whole, *beyond = lax.optimization_barrier((whole, *beyond))
+    whole, *moved = lax.optimization_barrier((whole, *beyond, *others))
+    beyond, others = moved[:2], moved[2:]
     gram = whole[:, :rows]
     near = gram[0:2]
     far = jnp.stack([gram[0], gram[2]])
     grams = [turned(near, 1), turned(near, 2), turned(far, 3)]
-    ids = member_ids.reshape(4, 128)
+    gram_other = swapped(gram)
     inverse, upper, row, right = pl.pallas_call(
         begin_kernel,
-        out_shape=(shaped(128, 128), shaped(128, 384), shaped(128, 384), shaped(rows, members)),
-        in_specs=[smem] + [vmem] * 3,
-        compiler_params=params,
+        out_shape=(
+            shaped(128, 128),
+            shaped(128, 384),
+            shaped(128, 384),
+            shaped(rows, members),
+        ),
+        in_specs=[smem, vmem, vmem, vmem],
+        compiler_params=room(8),
         name="begin",
-    )(place, ids, whole, swapped(gram))
-    inverse, *grams = lax.optimization_barrier((inverse, *grams))
-    grams = grams + [swapped(g) for g in grams]
-    inverse, *ready = lax.optimization_barrier((inverse, *grams, field, back, *beyond, ahead))
-    grams, shares = ready[:6], ready[6:]
-    others = [swapped(f) for f in shares]
-    transform = pl.pallas_call(
+    )(place, ids, whole, gram_other)
+    inverse, *after = lax.optimization_barrier((inverse, *grams, *beyond))
+    grams, beyond = after[:3], after[3:]
+    beyond_others = [swapped(f) for f in beyond]
+    theirs = swapped(jnp.concatenate(grams, axis=0))
+    fields = [field, others[2], back, others[0], *beyond, *beyond_others, ahead, others[1]]
+    transform, anomaly = pl.pallas_call(
         solve_kernel,
-        out_shape=shaped(rows, members, dtype=BF16),
-        in_specs=[smem] + [vmem] * 11,
+        out_shape=(shaped(rows, members, dtype=BF16), shaped(members, cells, dtype=BF16)),
+        in_specs=[smem] + [vmem] * (9 + len(fields)),
         scratch_shapes=[pltpu.VMEM((rows, members), F32)],
-        compiler_params=params,
+        compiler_params=room(22),
         name="solve",
-    )(place, ids, inverse, upper, row, right, *grams)
-
-    pieces = [field, others[0], back, others[1], *shares[2:4], *others[2:4], ahead, others[4]]
-    wide = 1024
-    strips = [pl.BlockSpec((piece.shape[0], wide), lambda i: (0, i)) for piece in pieces]
+    )(place, ids, inverse, upper, row, right, *grams, theirs, *fields)
     return pl.pallas_call(
         update_kernel,
-        grid=(cells // wide,),
         out_shape=shaped(rows, cells, dtype=BF16),
-        in_specs=[pl.BlockSpec((rows, members), lambda i: (0, 0))] + strips,
-        out_specs=strips[0],
-        compiler_params=params,
+        in_specs=[vmem] * 3,
+        compiler_params=room(14),
         name="update",
-    )(transform, *pieces)
+    )(transform, field, anomaly)
 
 
 def solution(mesh):

time: 106 us -> 104 us (0.981)
  starting transfers between devices: 19.9 us -> 22.7 us
  Pallas kernels: 28 us -> 25.7 us
  other arithmetic: 0.1 us -> 2.18 us
  blocking collectives: 40.5 us -> 38.7 us
  waiting for transfers between devices: 13.4 us -> 11.9 us
    ppermute x12 -> x10, starting transfers between devices: 12.3 us -> 15.6 us  [swapped(): return lax.ppermute(array, 'ens', swap)]
    unnamed x14 -> x2, local copies, waits for them, and re-layouts: 2.31 us -> 0.01 us
    ppermute x10, waiting for transfers between devices: 11.3 us -> 8.99 us  [turned(): lax.ppermute(array, 'ens', [(i, (i + 2 * steps) % 8) for i in range(8)])]
    pallas_call x2, Pallas kernels: 21.6 us -> 19.7 us  [the longest x1 17.1 us: body(): pl.pallas_call(solve_kernel, out_shape=(shaped(rows, members, dtype=BF16)...]
    dynamic_slice x0 -> x2, local copies, waits for them, and re-layouts: none -> 1.85 us  [the longest x1 0.93 us: body(): pred_mine = lax.dynamic_slice_in_dim(predicted, core * half, half, 1)]
    all_to_all x1, blocking collectives: 19.8 us -> 18 us  [body(): lax.all_to_all(jnp.broadcast_to(summed[None], (32, 16, 128)), 'space', sp...]
    ppermute x12 -> x10, waiting for transfers between devices: 2.09 us -> 2.92 us  [swapped(): return lax.ppermute(array, 'ens', swap)]
  transfers between devices with their start and end apart: 22 -> 20, of which waited for: 8 -> 6; matrix products, arithmetic and copies ran while one was open for 1% -> 5% of each run, Pallas kernels for 20% -> 6%
where the time goes in v3:
time: 104 us
  blocking collectives  38.7 us (37%)
  Pallas kernels  25.7 us (25%)
  starting transfers between devices  22.7 us (22%)
  waiting for transfers between devices  11.9 us (11%)
  local copies, waits for them, and re-layouts  2.63 us (3%)
  other arithmetic  2.18 us (2%)
    all_to_all x1, blocking collectives, body(): lax.all_to_all(part.reshape(32, 16, 128), 'space', split_axis=0, concat_a...  20.7 us
    all_to_all x1, blocking collectives, body(): lax.all_to_all(jnp.broadcast_to(summed[None], (32, 16, 128)), 'space', sp...  18 us
    pallas_call x1, Pallas kernels, body(): pl.pallas_call(solve_kernel, out_shape=(shaped(rows, members, dtype=BF16)...  17.1 us
    ppermute x10, starting transfers between devices, swapped(): return lax.ppermute(array, 'ens', swap)  15.6 us
    ppermute x10, waiting for transfers between devices, turned(): lax.ppermute(array, 'ens', [(i, (i + 2 * steps) % 8) for i in range(8)])  8.99 us
    ppermute x10, starting transfers between devices, turned(): lax.ppermute(array, 'ens', [(i, (i + 2 * steps) % 8) for i in range(8)])  7.11 us
    pallas_call x1, Pallas kernels, body(): pl.pallas_call(begin_kernel, out_shape=(shaped(128, 128), shaped(128, 384...  4.61 us
    ppermute x10, waiting for transfers between devices, swapped(): return lax.ppermute(array, 'ens', swap)  2.92 us
  transfers between devices with their start and end apart: 20, of which 6 were waited for; matrix products, arithmetic and copies ran while one was open for 5% of the time, Pallas kernels for 6%

profile of v3, /device:TPU:1, one launch (start us, length us, event | category | flops | bytes accessed | tf_op | source)
XLA Modules:
  0.0 104.0 jit_solution(4552192369382744595)
XLA Ops:
  0.0 3.2 %collective-permute-start = (f32[64,1280]{1,0:T(8,128)}, f32[64,1280]{1,0:T(8,128)S(1)}, u32[]{:S(2)}, u32[]{:S(2)}) collective-permute-start(f32[64,1280]{1,0:T(8,128)} %param.9), channel_id=1, source_target_pairs={{0,32},{32,0},{64,96},{96,64},{128,160},{160,128},{192,224},{224,1... | collective-permute-start | bytes 983048 | tf_op jit(solution)/shard_map/ppermute | solution.py:285
  3.2 0.7 convert_bitcast_fusion
  3.9 0.7 pad_bitcast_fusion.table_ref
  4.6 0.7 pad_maximum_fusion.2.facts_ref
  5.3 0.9 constant_dynamic-slice_fusion.mine_ref
  6.2 0.0 collective-permute-done.got_ref
  6.3 0.2 prepare.1
  6.4 0.8 collective-permute-start.3
  7.3 0.5 collective-permute-start.2
  7.8 0.6 collective-permute-start.1
  8.4 0.7 convert_bitcast_fusion.1.ids_ref
  9.1 0.9 collective-permute-start.4
  10.0 0.9 constant_dynamic-slice_fusion.1.mine_ref
  10.9 1.8 %collective-permute-done.3.p3_ref = bf16[144,640]{1,0:T(8,128)(2,1)S(1)} collective-permute-done((bf16[144,640]{1,0:T(8,128)(2,1)S(1)}, bf16[144,640]{1,0:T(8,128)(2,1)S(1)}, u32[]{:S(2)}, u32[]{:S(2)}) %collective-permute-start.3) | collective-permute-done | bytes 184352 | tf_op jit(solution)/shard_map/ppermute | solution.py:282
  12.7 2.0 %collective-permute-done.2.p2_ref = bf16[144,640]{1,0:T(8,128)(2,1)S(1)} collective-permute-done((bf16[144,640]{1,0:T(8,128)(2,1)S(1)}, bf16[144,640]{1,0:T(8,128)(2,1)S(1)}, u32[]{:S(2)}, u32[]{:S(2)}) %collective-permute-start.2) | collective-permute-done | bytes 184352 | tf_op jit(solution)/shard_map/ppermute | solution.py:282
  14.7 4.6 %collective-permute-done.1.p1_ref = bf16[144,640]{1,0:T(8,128)(2,1)S(1)} collective-permute-done((bf16[144,640]{1,0:T(8,128)(2,1)S(1)}, bf16[144,640]{1,0:T(8,128)(2,1)S(1)}, u32[]{:S(2)}, u32[]{:S(2)}) %collective-permute-start.1) | collective-permute-done | bytes 184352 | tf_op jit(solution)/shard_map/ppermute | solution.py:282
  19.3 0.0 collective-permute-start.7
  19.3 1.5 %collective-permute-start.6 = (bf16[64,8192]{1,0:T(8,128)(2,1)}, bf16[64,8192]{1,0:T(8,128)(2,1)S(1)}, u32[]{:S(2)}, u32[]{:S(2)}) collective-permute-start(bf16[64,8192]{1,0:T(8,128)(2,1)} %field_ref), channel_id=1, source_target_pairs={{0,64},{32,96},{64,128},{96,160},{128,192},{160,224},{192,0},{224,... | collective-permute-start | bytes 3145736 | tf_op jit(solution)/shard_map/ppermute | solution.py:282
  20.8 1.2 %gram.1 = (f32[4,128,128]{2,1,0:T(8,128)S(1)}, f32[4,128,128]{2,1,0:T(8,128)S(1)}) custom-call(s32[1]{0:T(128)} %bitcast.place_ref, bf16[144,640]{1,0:T(8,128)(2,1)S(1)} %get-tuple-element.43.p0_ref, bf16[144,640]{1,0:T(8,128)(2,1)S(1)} %collective-permute-done.1.p1_ref, bf16[144,640]{1,0:T(8,128)(2,1)S(1)} %collective-permute-done.2.p2_ref, ...), custom_call_target="tpu_custom_call" | custom-call | tf_op jit(solution)/shard_map/gram/pallas_call | solution.py:309
  22.0 1.1 %collective-permute-start.5 = (f32[4,128,128]{2,1,0:T(8,128)S(1)}, f32[4,128,128]{2,1,0:T(8,128)S(1)}, u32[]{:S(2)}, u32[]{:S(2)}) collective-permute-start(f32[4,128,128]{2,1,0:T(8,128)S(1)} %get-tuple-element.51), channel_id=1, source_target_pairs={{0,32},{32,0},{64,96},{96,64},{128,160},{160,128},{192,224},{224,1... | collective-permute-start | bytes 786440 | tf_op jit(solution)/shard_map/ppermute | solution.py:285
  23.1 1.2 %collective-permute-done.5 = f32[4,128,128]{2,1,0:T(8,128)S(1)} collective-permute-done((f32[4,128,128]{2,1,0:T(8,128)S(1)}, f32[4,128,128]{2,1,0:T(8,128)S(1)}, u32[]{:S(2)}, u32[]{:S(2)}) %collective-permute-start.5) | collective-permute-done | bytes 262176 | tf_op jit(solution)/shard_map/ppermute | solution.py:285
  24.3 20.7 %all_to_all.10 = f32[32,16,128]{2,1,0:T(8,128)S(1)} all-to-all(f32[32,16,128]{2,1,0:T(8,128)S(1)} %bitcast.15), channel_id=1, replica_groups=mesh['ens'=8,'space'=32] {'space'}, dimensions={0} | all-to-all | bytes 524288 | tf_op jit(solution)/shard_map/all_to_all | solution.py:318
  45.1 0.0 collective-permute-done.6.rest_2_
  45.1 3.8 %collective-permute-start.12 = (bf16[64,8192]{1,0:T(8,128)(2,1)}, bf16[64,8192]{1,0:T(8,128)(2,1)S(1)}, u32[]{:S(2)}, u32[]{:S(2)}) collective-permute-start(bf16[64,8192]{1,0:T(8,128)(2,1)} %field_ref), channel_id=1, source_target_pairs={{0,32},{32,0},{64,96},{96,64},{128,160},{160,128},{192,224},{224,1... | collective-permute-start | bytes 3145736 | tf_op jit(solution)/shard_map/ppermute | solution.py:285
  48.9 0.1 collective-permute-start.10
  49.0 0.4 collective-permute-start.11
  49.4 1.6 %collective-permute-start.9 = (bf16[32,8192]{1,0:T(8,128)(2,1)S(1)}, bf16[32,8192]{1,0:T(8,128)(2,1)S(1)}, u32[]{:S(2)}, u32[]{:S(2)}) collective-permute-start(bf16[32,8192]{1,0:T(8,128)(2,1)S(1)} %slice.22), channel_id=1, source_target_pairs={{0,192},{32,224},{64,0},{96,32},{128,64},{160,96},{192,128},{224,1... | collective-permute-start | bytes 1572872 | tf_op jit(solution)/shard_map/ppermute | solution.py:282
  51.1 0.0 collective-permute-start.8
  51.1 18.0 %all_to_all.11 = f32[32,16,128]{2,1,0:T(8,128)S(1)} all-to-all(f32[32,16,128]{2,1,0:T(8,128)S(1)} %broadcast_in_dim.2), channel_id=1, replica_groups=mesh['ens'=8,'space'=32] {'space'}, dimensions={0} | all-to-all | bytes 524288 | tf_op jit(solution)/shard_map/all_to_all | solution.py:324
  69.1 0.0 collective-permute-done.9.rest_5_
  69.1 0.0 collective-permute-done.8.rest_4_
  69.1 0.0 collective-permute-done.12.rest_1_
  69.1 0.0 collective-permute-done.10.rest_3_
  69.2 0.0 collective-permute-done.11.rest_9_
  69.2 3.8 %collective-permute-start.13 = (f32[4,64,128]{2,1,0:T(8,128)S(1)}, f32[4,64,128]{2,1,0:T(8,128)S(1)}, u32[]{:S(2)}, u32[]{:S(2)}) collective-permute-start(f32[4,64,128]{2,1,0:T(8,128)S(1)} %slice.23), channel_id=1, source_target_pairs={{0,32},{32,0},{64,96},{96,64},{128,160},{160,128},{192,224},{224,1... | collective-permute-start | bytes 393224 | tf_op jit(solution)/shard_map/ppermute | solution.py:285
  73.0 1.3 %collective-permute-start.16 = (f32[2,64,128]{2,1,0:T(8,128)S(1)}, f32[2,64,128]{2,1,0:T(8,128)S(1)}, u32[]{:S(2)}, u32[]{:S(2)}) collective-permute-start(f32[2,64,128]{2,1,0:T(8,128)S(1)} %pad_maximum_fusion.1), channel_id=1, source_target_pairs={{0,192},{32,224},{64,0},{96,32},{128,64},{160,96},{192,128},{224,1... | collective-permute-start | bytes 196616 | tf_op jit(solution)/shard_map/ppermute | solution.py:282
  74.3 0.7 collective-permute-start.15
  75.0 0.0 collective-permute-start.14
  75.0 0.0 collective-permute-done.13.other_ref
  75.0 4.6 %begin.1 = (f32[128,128]{1,0:T(8,128)S(1)}, f32[128,384]{1,0:T(8,128)S(1)}, f32[128,384]{1,0:T(8,128)S(1)}, f32[64,512]{1,0:T(8,128)S(1)}) custom-call(s32[1]{0:T(128)} %bitcast.place_ref, f32[4,128]{1,0:T(4,128)S(1)} %convert_bitcast_fusion.1.ids_ref, f32[4,128,128]{2,1,0:T(8,128)S(1)} %bitcast.14, f32[4,64,128]{2,1,0:T(8,128)S(1)} %collective-permute-done.13.other_ref), custom_call_target="tpu_custom_call" | custom-call | tf_op jit(solution)/shard_map/begin/pallas_call | solution.py:335
  79.6 0.0 collective-permute-done.16.g3_ref
  79.7 0.6 collective-permute-done.14.g1_ref
  80.3 1.4 %collective-permute-start.18 = (bf16[32,8192]{1,0:T(8,128)(2,1)S(1)}, bf16[32,8192]{1,0:T(8,128)(2,1)S(1)}, u32[]{:S(2)}, u32[]{:S(2)}) collective-permute-start(bf16[32,8192]{1,0:T(8,128)(2,1)S(1)} %collective-permute-done.8.rest_4_), channel_id=1, source_target_pairs={{0,32},{32,0},{64,96},{96,64},{128,160},{160,128},{192,224},{224,1... | collective-permute-start | bytes 1572872 | tf_op jit(solution)/shard_map/ppermute | solution.py:285
  81.7 0.0 collective-permute-start.19
  81.7 0.8 collective-permute-start.17
  82.5 1.7 %collective-permute-done.17.theirs_ref = f32[6,64,128]{2,1,0:T(8,128)S(1)} collective-permute-done((f32[6,64,128]{2,1,0:T(8,128)S(1)}, f32[6,64,128]{2,1,0:T(8,128)S(1)}, u32[]{:S(2)}, u32[]{:S(2)}) %collective-permute-start.17) | collective-permute-done | bytes 196640 | tf_op jit(solution)/shard_map/ppermute | solution.py:285
  84.3 17.1 %solve.1 = (bf16[64,512]{1,0:T(8,128)(2,1)S(1)}, bf16[512,8192]{1,0:T(8,128)(2,1)S(1)}) custom-call(s32[1]{0:T(128)} %bitcast.place_ref, f32[4,128]{1,0:T(4,128)S(1)} %convert_bitcast_fusion.1.ids_ref, f32[128,128]{1,0:T(8,128)S(1)} %get-tuple-element.61.inverse_ref, f32[128,384]{1,0:T(8,128)S(1)} %get-tuple-element.62.upper_ref, ...), custom_call_target="tpu_custom_call" | custom-call | tf_op jit(solution)/shard_map/solve/pallas_call | solution.py:352
  101.4 2.5 %update.1 = bf16[64,8192]{1,0:T(8,128)(2,1)} custom-call(bf16[64,512]{1,0:T(8,128)(2,1)S(1)} %get-tuple-element.73.t_ref, bf16[64,8192]{1,0:T(8,128)(2,1)S(1)} %copy-done, bf16[512,8192]{1,0:T(8,128)(2,1)S(1)} %get-tuple-element.74.anomaly_ref), custom_call_target="tpu_custom_call" | custom-call | tf_op jit(solution)/shard_map/update/pallas_call | solution.py:360
  (17 shorter events, 0.2 us)
Async XLA Ops:
  0.0 84.3 %copy-start = (bf16[64,8192]{1,0:T(8,128)(2,1)S(1)}, bf16[64,8192]{1,0:T(8,128)(2,1)}, u32[]{:S(2)}) copy-start(bf16[64,8192]{1,0:T(8,128)(2,1)} %field_ref) | copy-start | bytes 3145732
  0.0 6.2 %collective-permute-start = (f32[64,1280]{1,0:T(8,128)}, f32[64,1280]{1,0:T(8,128)S(1)}, u32[]{:S(2)}, u32[]{:S(2)}) collective-permute-start(f32[64,1280]{1,0:T(8,128)} %param.9), channel_id=1, source_target_pairs={{0,32},{32,0},{64,96},{96,64},{128,160},{160,128},{192,224},{224,1... | collective-permute-start | bytes 983048 | tf_op jit(solution)/shard_map/ppermute | solution.py:285
  6.4 6.3 %collective-permute-start.3 = (bf16[144,640]{1,0:T(8,128)(2,1)S(1)}, bf16[144,640]{1,0:T(8,128)(2,1)S(1)}, u32[]{:S(2)}, u32[]{:S(2)}) collective-permute-start(bf16[144,640]{1,0:T(8,128)(2,1)S(1)} %get-tuple-element.43.p0_ref), channel_id=1, source_target_pairs={{0,192},{32,224},{64,0},{96,32},{128,64},{160,96},{192,128},{224,1... | collective-permute-start | bytes 552968 | tf_op jit(solution)/shard_map/ppermute | solution.py:282
  7.3 7.4 %collective-permute-start.2 = (bf16[144,640]{1,0:T(8,128)(2,1)S(1)}, bf16[144,640]{1,0:T(8,128)(2,1)S(1)}, u32[]{:S(2)}, u32[]{:S(2)}) collective-permute-start(bf16[144,640]{1,0:T(8,128)(2,1)S(1)} %get-tuple-element.43.p0_ref), channel_id=1, source_target_pairs={{0,128},{32,160},{64,192},{96,224},{128,0},{160,32},{192,64},{224,... | collective-permute-start | bytes 552968 | tf_op jit(solution)/shard_map/ppermute | solution.py:282
  7.8 11.5 %collective-permute-start.1 = (bf16[144,640]{1,0:T(8,128)(2,1)S(1)}, bf16[144,640]{1,0:T(8,128)(2,1)S(1)}, u32[]{:S(2)}, u32[]{:S(2)}) collective-permute-start(bf16[144,640]{1,0:T(8,128)(2,1)S(1)} %get-tuple-element.43.p0_ref), channel_id=1, source_target_pairs={{0,64},{32,96},{64,128},{96,160},{128,192},{160,224},{192,0},{224,... | collective-permute-start | bytes 552968 | tf_op jit(solution)/shard_map/ppermute | solution.py:282
  9.1 11.7 %collective-permute-start.4 = (f32[64,1280]{1,0:T(8,128)}, f32[64,1280]{1,0:T(8,128)S(1)}, u32[]{:S(2)}, u32[]{:S(2)}) collective-permute-start(f32[64,1280]{1,0:T(8,128)} %param.10), channel_id=1, source_target_pairs={{0,32},{32,0},{64,96},{96,64},{128,160},{160,128},{192,224},{224,1... | collective-permute-start | bytes 983048 | tf_op jit(solution)/shard_map/ppermute | solution.py:285
  19.3 25.8 %collective-permute-start.7 = (bf16[64,8192]{1,0:T(8,128)(2,1)}, bf16[64,8192]{1,0:T(8,128)(2,1)S(1)}, u32[]{:S(2)}, u32[]{:S(2)}) collective-permute-start(bf16[64,8192]{1,0:T(8,128)(2,1)} %field_ref), channel_id=1, source_target_pairs={{0,192},{32,224},{64,0},{96,32},{128,64},{160,96},{192,128},{224,1... | collective-permute-start | bytes 3145736 | tf_op jit(solution)/shard_map/ppermute | solution.py:282
  19.3 25.8 %collective-permute-start.6 = (bf16[64,8192]{1,0:T(8,128)(2,1)}, bf16[64,8192]{1,0:T(8,128)(2,1)S(1)}, u32[]{:S(2)}, u32[]{:S(2)}) collective-permute-start(bf16[64,8192]{1,0:T(8,128)(2,1)} %field_ref), channel_id=1, source_target_pairs={{0,64},{32,96},{64,128},{96,160},{128,192},{160,224},{192,0},{224,... | collective-permute-start | bytes 3145736 | tf_op jit(solution)/shard_map/ppermute | solution.py:282
  22.0 2.3 %collective-permute-start.5 = (f32[4,128,128]{2,1,0:T(8,128)S(1)}, f32[4,128,128]{2,1,0:T(8,128)S(1)}, u32[]{:S(2)}, u32[]{:S(2)}) collective-permute-start(f32[4,128,128]{2,1,0:T(8,128)S(1)} %get-tuple-element.51), channel_id=1, source_target_pairs={{0,32},{32,0},{64,96},{96,64},{128,160},{160,128},{192,224},{224,1... | collective-permute-start | bytes 786440 | tf_op jit(solution)/shard_map/ppermute | solution.py:285
  45.1 24.1 %collective-permute-start.12 = (bf16[64,8192]{1,0:T(8,128)(2,1)}, bf16[64,8192]{1,0:T(8,128)(2,1)S(1)}, u32[]{:S(2)}, u32[]{:S(2)}) collective-permute-start(bf16[64,8192]{1,0:T(8,128)(2,1)} %field_ref), channel_id=1, source_target_pairs={{0,32},{32,0},{64,96},{96,64},{128,160},{160,128},{192,224},{224,1... | collective-permute-start | bytes 3145736 | tf_op jit(solution)/shard_map/ppermute | solution.py:285
  48.9 20.3 %collective-permute-start.10 = (bf16[64,8192]{1,0:T(8,128)(2,1)S(1)}, bf16[64,8192]{1,0:T(8,128)(2,1)S(1)}, u32[]{:S(2)}, u32[]{:S(2)}) collective-permute-start(bf16[64,8192]{1,0:T(8,128)(2,1)S(1)} %collective-permute-done.6.rest_2_), channel_id=1, source_target_pairs={{0,32},{32,0},{64,96},{96,64},{128,160},{160,128},{192,224},{224,1... | collective-permute-start | bytes 3145736 | tf_op jit(solution)/shard_map/ppermute | solution.py:285
  49.0 20.2 %collective-permute-start.11 = (bf16[64,8192]{1,0:T(8,128)(2,1)S(1)}, bf16[64,8192]{1,0:T(8,128)(2,1)S(1)}, u32[]{:S(2)}, u32[]{:S(2)}) collective-permute-start(bf16[64,8192]{1,0:T(8,128)(2,1)S(1)} %collective-permute-done.7.rest_8_), channel_id=1, source_target_pairs={{0,32},{32,0},{64,96},{96,64},{128,160},{160,128},{192,224},{224,1... | collective-permute-start | bytes 3145736 | tf_op jit(solution)/shard_map/ppermute | solution.py:285
  49.4 19.7 %collective-permute-start.9 = (bf16[32,8192]{1,0:T(8,128)(2,1)S(1)}, bf16[32,8192]{1,0:T(8,128)(2,1)S(1)}, u32[]{:S(2)}, u32[]{:S(2)}) collective-permute-start(bf16[32,8192]{1,0:T(8,128)(2,1)S(1)} %slice.22), channel_id=1, source_target_pairs={{0,192},{32,224},{64,0},{96,32},{128,64},{160,96},{192,128},{224,1... | collective-permute-start | bytes 1572872 | tf_op jit(solution)/shard_map/ppermute | solution.py:282
  51.1 18.1 %collective-permute-start.8 = (bf16[32,8192]{1,0:T(8,128)(2,1)S(1)}, bf16[32,8192]{1,0:T(8,128)(2,1)S(1)}, u32[]{:S(2)}, u32[]{:S(2)}) collective-permute-start(bf16[32,8192]{1,0:T(8,128)(2,1)S(1)} %slice.21), channel_id=1, source_target_pairs={{0,64},{32,96},{64,128},{96,160},{128,192},{160,224},{192,0},{224,... | collective-permute-start | bytes 1572872 | tf_op jit(solution)/shard_map/ppermute | solution.py:282
  69.2 5.8 %collective-permute-start.13 = (f32[4,64,128]{2,1,0:T(8,128)S(1)}, f32[4,64,128]{2,1,0:T(8,128)S(1)}, u32[]{:S(2)}, u32[]{:S(2)}) collective-permute-start(f32[4,64,128]{2,1,0:T(8,128)S(1)} %slice.23), channel_id=1, source_target_pairs={{0,32},{32,0},{64,96},{96,64},{128,160},{160,128},{192,224},{224,1... | collective-permute-start | bytes 393224 | tf_op jit(solution)/shard_map/ppermute | solution.py:285
  73.0 6.7 %collective-permute-start.16 = (f32[2,64,128]{2,1,0:T(8,128)S(1)}, f32[2,64,128]{2,1,0:T(8,128)S(1)}, u32[]{:S(2)}, u32[]{:S(2)}) collective-permute-start(f32[2,64,128]{2,1,0:T(8,128)S(1)} %pad_maximum_fusion.1), channel_id=1, source_target_pairs={{0,192},{32,224},{64,0},{96,32},{128,64},{160,96},{192,128},{224,1... | collective-permute-start | bytes 196616 | tf_op jit(solution)/shard_map/ppermute | solution.py:282
  74.3 5.4 %collective-permute-start.15 = (f32[2,64,128]{2,1,0:T(8,128)S(1)}, f32[2,64,128]{2,1,0:T(8,128)S(1)}, u32[]{:S(2)}, u32[]{:S(2)}) collective-permute-start(f32[2,64,128]{2,1,0:T(8,128)S(1)} %slice.24), channel_id=1, source_target_pairs={{0,128},{32,160},{64,192},{96,224},{128,0},{160,32},{192,64},{224,... | collective-permute-start | bytes 196616 | tf_op jit(solution)/shard_map/ppermute | solution.py:282
  75.0 5.3 %collective-permute-start.14 = (f32[2,64,128]{2,1,0:T(8,128)S(1)}, f32[2,64,128]{2,1,0:T(8,128)S(1)}, u32[]{:S(2)}, u32[]{:S(2)}) collective-permute-start(f32[2,64,128]{2,1,0:T(8,128)S(1)} %slice.24), channel_id=1, source_target_pairs={{0,64},{32,96},{64,128},{96,160},{128,192},{160,224},{192,0},{224,... | collective-permute-start | bytes 196616 | tf_op jit(solution)/shard_map/ppermute | solution.py:282
  80.3 4.0 %collective-permute-start.18 = (bf16[32,8192]{1,0:T(8,128)(2,1)S(1)}, bf16[32,8192]{1,0:T(8,128)(2,1)S(1)}, u32[]{:S(2)}, u32[]{:S(2)}) collective-permute-start(bf16[32,8192]{1,0:T(8,128)(2,1)S(1)} %collective-permute-done.8.rest_4_), channel_id=1, source_target_pairs={{0,32},{32,0},{64,96},{96,64},{128,160},{160,128},{192,224},{224,1... | collective-permute-start | bytes 1572872 | tf_op jit(solution)/shard_map/ppermute | solution.py:285
  81.7 2.6 %collective-permute-start.19 = (bf16[32,8192]{1,0:T(8,128)(2,1)S(1)}, bf16[32,8192]{1,0:T(8,128)(2,1)S(1)}, u32[]{:S(2)}, u32[]{:S(2)}) collective-permute-start(bf16[32,8192]{1,0:T(8,128)(2,1)S(1)} %collective-permute-done.9.rest_5_), channel_id=1, source_target_pairs={{0,32},{32,0},{64,96},{96,64},{128,160},{160,128},{192,224},{224,1... | collective-permute-start | bytes 1572872 | tf_op jit(solution)/shard_map/ppermute | solution.py:285
  81.7 2.5 %collective-permute-start.17 = (f32[6,64,128]{2,1,0:T(8,128)S(1)}, f32[6,64,128]{2,1,0:T(8,128)S(1)}, u32[]{:S(2)}, u32[]{:S(2)}) collective-permute-start(f32[6,64,128]{2,1,0:T(8,128)S(1)} %pad_maximum_fusion), channel_id=1, source_target_pairs={{0,32},{32,0},{64,96},{96,64},{128,160},{160,128},{192,224},{224,1... | collective-permute-start | bytes 589832 | tf_op jit(solution)/shard_map/ppermute | solution.py:285

commit v4 on v3

--- a/solution.py
+++ b/solution.py
@@ -77,10 +77,30 @@
     return jnp.concatenate(tiles, axis=0)
 
 
-def prepare_kernel(place_ref, table_ref, facts_ref, mine_ref, got_ref, out_ref, side_ref, *, factor):
+def prepare_kernel(place_ref, mine_ref, got_ref, out_ref):
     half = mine_ref.shape[0]
     rows = 2 * half
     width = out_ref.shape[1]
+    here = pl.ds(pl.multiple_of(lax.rem(place_ref[0], 2) * width, 128), width)
+    mine = mine_ref[...]
+    got = got_ref[:, here]
+    mean = (jnp.sum(mine, axis=0, keepdims=True) + jnp.sum(got, axis=0, keepdims=True)) / rows
+    out_ref[0:half, :] = (mine - mean).astype(BF16)
+    out_ref[half:rows, :] = (got - mean).astype(BF16)
+    high = mean.astype(BF16)
+    rest = mean - high.astype(F32)
+    mid = rest.astype(BF16)
+    low = (rest - mid.astype(F32)).astype(BF16)
+    out_ref[rows : rows + 16, :] = jnp.concatenate([high, mid, low, jnp.zeros((13, width), BF16)], axis=0)
+
+
+def gram_kernel(
+    place_ref, p0_ref, p1_ref, p2_ref, p3_ref, mine_ref, got_ref, facts_ref, table_ref, own_ref, other_ref, *, factor
+):
+    refs = (p0_ref, p1_ref, p2_ref, p3_ref)
+    rows = p0_ref.shape[0] - 16
+    half = rows // 2
+    width = p0_ref.shape[1]
     core = lax.rem(place_ref[0], 2)
     here = pl.ds(pl.multiple_of(core * width, 128), width)
 
@@ -94,41 +114,19 @@
         level = jnp.broadcast_to(table_ref[:, b : b + 1], block.shape)
         error_scale = jnp.where(block == float(b), level, error_scale)
     scale = line(0) / error_scale * factor
-    side_ref[...] = jnp.concatenate([scale, line(1), jnp.zeros((6, width), F32)], axis=0)
-    mine = mine_ref[...]
-    got = got_ref[:, here]
-    mean = (jnp.sum(mine, axis=0, keepdims=True) + jnp.sum(got, axis=0, keepdims=True)) / rows
-    out_ref[0:half, :] = ((mine - mean) * scale).astype(BF16)
-    out_ref[half:rows, :] = ((got - mean) * scale).astype(BF16)
-    high = mean.astype(BF16)
-    rest = mean - high.astype(F32)
-    mid = rest.astype(BF16)
-    low = (rest - mid.astype(F32)).astype(BF16)
-    out_ref[rows : rows + 16, :] = jnp.concatenate([high, mid, low, jnp.zeros((13, width), BF16)], axis=0)
-
-
-def gram_kernel(
-    place_ref, p0_ref, p1_ref, p2_ref, p3_ref, mine_ref, got_ref, side_ref, own_ref, other_ref, *, factor
-):
-    refs = (p0_ref, p1_ref, p2_ref, p3_ref)
-    rows = p0_ref.shape[0] - 16
-    half = rows // 2
-    width = p0_ref.shape[1]
-    here = pl.ds(pl.multiple_of(lax.rem(place_ref[0], 2) * width, 128), width)
-    scale = side_ref[0:1, :]
     means = []
     for ref in refs:
         tail = ref[rows : rows + 16, :].astype(F32)
         means.append(tail[0:1, :] + (tail[1:2, :] + tail[2:3, :]))
     mean = ((means[0] + means[1]) + (means[2] + means[3])) * 0.25
     spreads = [
-        (ref[0:rows, :].astype(F32) + scale * (m - mean)).astype(BF16) for ref, m in zip(refs, means)
+        (scale * (ref[0:rows, :].astype(F32) + (m - mean))).astype(BF16) for ref, m in zip(refs, means)
     ]
     left_over = tree_sum([jnp.sum(s.astype(F32), axis=0, keepdims=True) for s in spreads]) / (4 * rows)
     over_high = left_over.astype(BF16)
     over_low = (left_over - over_high.astype(F32)).astype(BF16)
     over = jnp.concatenate([over_high, over_low, jnp.zeros((14, width), BF16)], axis=0)
-    shift = scale * (side_ref[1:2, :] - mean)
+    shift = scale * (line(1) - mean)
     noise = jnp.concatenate([mine_ref[...], got_ref[:, here]], axis=0)
     right = shift + factor * noise
     high = right.astype(BF16)
@@ -287,32 +285,34 @@
     pred_got = swapped(predicted)
     core = lax.rem(lax.axis_index("ens"), 2)
     pred_mine = lax.dynamic_slice_in_dim(predicted, core * half, half, 1)
+    payload = pl.pallas_call(
+        prepare_kernel,
+        out_shape=shaped(2 * rows + 16, half, dtype=BF16),
+        in_specs=[smem, vmem, vmem],
+        compiler_params=room(32),
+        name="prepare",
+    )(place, pred_mine, pred_got)
+    payload, noise, member_ids, obs_precision, observed, obs_block, block_error_scale = lax.optimization_barrier(
+        (payload, noise, member_ids, obs_precision, observed, obs_block, block_error_scale)
+    )
+    noise_got = swapped(noise)
     noise_mine = lax.dynamic_slice_in_dim(noise, core * half, half, 1)
     facts = jnp.stack([a.reshape(-1, 128).astype(F32) for a in (obs_precision, observed, obs_block)])
     table = jnp.pad(block_error_scale, (0, 128 - block_error_scale.shape[0])).reshape(1, 128)
-    payload, side = pl.pallas_call(
-        functools.partial(prepare_kernel, factor=factor),
-        out_shape=(shaped(2 * rows + 16, half, dtype=BF16), shaped(8, half)),
-        in_specs=[smem] + [vmem] * 4,
-        compiler_params=room(32),
-        name="prepare",
-    )(place, table, facts, pred_mine, pred_got)
-    payload, noise_after = lax.optimization_barrier((payload, noise))
-    noise_got = swapped(noise_after)
     payloads = [payload] + [turned(payload, k) for k in (1, 2, 3)]
 
     ids = member_ids.astype(F32).reshape(4, 128)
-    after_spread = lax.optimization_barrier((members_field, noise_mine, ids, *payloads))
-    (field, noise_mine, ids), payloads = after_spread[:3], after_spread[3:]
+    after_spread = lax.optimization_barrier((members_field, noise_mine, ids, facts, table, *payloads))
+    (field, noise_mine, ids, facts, table), payloads = after_spread[:5], after_spread[5:]
     back, ahead = turned(field, 1), turned(field, 3)
 
     own, other = pl.pallas_call(
         functools.partial(gram_kernel, factor=factor),
         out_shape=(shaped(4, 2 * rows, 2 * rows),) * 2,
-        in_specs=[smem] + [vmem] * 7,
+        in_specs=[smem] + [vmem] * 8,
         compiler_params=room(8),
         name="gram",
-    )(place, *payloads, noise_mine, noise_got, side)
+    )(place, *payloads, noise_mine, noise_got, facts, table)
     part = own + swapped(other)
 
     spread_out = lax.all_to_all(part.reshape(32, 16, 128), "space", split_axis=0, concat_axis=0)

time: 104 us -> 103 us (level)
  waiting for transfers between devices: 11.9 us -> 9.98 us
    ppermute x10, waiting for transfers between devices: 8.99 us -> 6.53 us  [turned(): lax.ppermute(array, 'ens', [(i, (i + 2 * steps) % 8) for i in range(8)])]
where the time goes in v4:
time: 103 us; the launch traced here: 102 us
  blocking collectives  38.6 us (37%)
  Pallas kernels  25.7 us (25%)
  starting transfers between devices  23.1 us (22%)
  waiting for transfers between devices  9.98 us (10%)
  local copies, waits for them, and re-layouts  2.63 us (3%)
  other arithmetic  2.18 us (2%)
    all_to_all x1, blocking collectives, body(): lax.all_to_all(part.reshape(32, 16, 128), 'space', split_axis=0, concat_a...  20.7 us
    all_to_all x1, blocking collectives, body(): lax.all_to_all(jnp.broadcast_to(summed[None], (32, 16, 128)), 'space', sp...  17.9 us
    pallas_call x1, Pallas kernels, body(): pl.pallas_call(solve_kernel, out_shape=(shaped(rows, members, dtype=BF16)...  17.1 us
    ppermute x10, starting transfers between devices, swapped(): return lax.ppermute(array, 'ens', swap)  16 us
    ppermute x10, starting transfers between devices, turned(): lax.ppermute(array, 'ens', [(i, (i + 2 * steps) % 8) for i in range(8)])  7.09 us
    ppermute x10, waiting for transfers between devices, turned(): lax.ppermute(array, 'ens', [(i, (i + 2 * steps) % 8) for i in range(8)])  6.53 us
    pallas_call x1, Pallas kernels, body(): pl.pallas_call(begin_kernel, out_shape=(shaped(128, 128), shaped(128, 384...  4.61 us
    ppermute x10, waiting for transfers between devices, swapped(): return lax.ppermute(array, 'ens', swap)  3.45 us
  transfers between devices with their start and end apart: 20, of which 6 were waited for; matrix products, arithmetic and copies ran while one was open for 5% of the time, Pallas kernels for 6%

profile of v4, /device:TPU:1, one launch (start us, length us, event | category | flops | bytes accessed | tf_op | source)
XLA Modules:
  0.0 102.3 jit_solution(9849104143637321836)
XLA Ops:
  0.0 3.2 %collective-permute-start = (f32[64,1280]{1,0:T(8,128)}, f32[64,1280]{1,0:T(8,128)S(1)}, u32[]{:S(2)}, u32[]{:S(2)}) collective-permute-start(f32[64,1280]{1,0:T(8,128)} %param.9), channel_id=1, source_target_pairs={{0,32},{32,0},{64,96},{96,64},{128,160},{160,128},{192,224},{224,1... | collective-permute-start | bytes 983048 | tf_op jit(solution)/shard_map/ppermute | solution.py:283
  3.2 0.9 constant_dynamic-slice_fusion.1.mine_ref
  4.2 0.5 collective-permute-done.got_ref
  4.7 0.1 prepare.1.p0_ref
  4.8 0.8 collective-permute-start.3
  5.6 0.5 collective-permute-start.2
  6.1 0.6 collective-permute-start.1
  6.7 0.9 constant_dynamic-slice_fusion.mine_ref
  7.6 1.3 %collective-permute-start.4 = (f32[64,1280]{1,0:T(8,128)}, f32[64,1280]{1,0:T(8,128)S(1)}, u32[]{:S(2)}, u32[]{:S(2)}) collective-permute-start(f32[64,1280]{1,0:T(8,128)} %param.10), channel_id=1, source_target_pairs={{0,32},{32,0},{64,96},{96,64},{128,160},{160,128},{192,224},{224,1... | collective-permute-start | bytes 983048 | tf_op jit(solution)/shard_map/ppermute | solution.py:283
  8.9 0.7 convert_bitcast_fusion.1.ids_ref
  9.6 0.7 convert_bitcast_fusion
  10.3 0.7 pad_maximum_fusion.2.facts_ref
  11.0 0.7 pad_bitcast_fusion.table_ref
  11.7 0.0 collective-permute-done.3.p3_ref
  11.7 1.0 collective-permute-done.2.p2_ref
  12.7 4.9 %collective-permute-done.1.p1_ref = bf16[144,640]{1,0:T(8,128)(2,1)S(1)} collective-permute-done((bf16[144,640]{1,0:T(8,128)(2,1)S(1)}, bf16[144,640]{1,0:T(8,128)(2,1)S(1)}, u32[]{:S(2)}, u32[]{:S(2)}) %collective-permute-start.1) | collective-permute-done | bytes 184352 | tf_op jit(solution)/shard_map/ppermute | solution.py:280
  17.6 0.0 collective-permute-start.7
  17.6 1.5 %collective-permute-start.6 = (bf16[64,8192]{1,0:T(8,128)(2,1)}, bf16[64,8192]{1,0:T(8,128)(2,1)S(1)}, u32[]{:S(2)}, u32[]{:S(2)}) collective-permute-start(bf16[64,8192]{1,0:T(8,128)(2,1)} %field_ref), channel_id=1, source_target_pairs={{0,64},{32,96},{64,128},{96,160},{128,192},{160,224},{192,0},{224,... | collective-permute-start | bytes 3145736 | tf_op jit(solution)/shard_map/ppermute | solution.py:280
  19.1 0.0 collective-permute-done.4.got_ref
  19.1 1.4 %gram.1 = (f32[4,128,128]{2,1,0:T(8,128)S(1)}, f32[4,128,128]{2,1,0:T(8,128)S(1)}) custom-call(s32[1]{0:T(128)} %bitcast.place_ref, bf16[144,640]{1,0:T(8,128)(2,1)S(1)} %prepare.1.p0_ref, bf16[144,640]{1,0:T(8,128)(2,1)S(1)} %collective-permute-done.1.p1_ref, bf16[144,640]{1,0:T(8,128)(2,1)S(1)} %collective-permute-done.2.p2_ref, ...), custom_call_target="tpu_custom_call" | custom-call | tf_op jit(solution)/shard_map/gram/pallas_call | solution.py:309
  20.4 1.1 %collective-permute-start.5 = (f32[4,128,128]{2,1,0:T(8,128)S(1)}, f32[4,128,128]{2,1,0:T(8,128)S(1)}, u32[]{:S(2)}, u32[]{:S(2)}) collective-permute-start(f32[4,128,128]{2,1,0:T(8,128)S(1)} %get-tuple-element.61), channel_id=1, source_target_pairs={{0,32},{32,0},{64,96},{96,64},{128,160},{160,128},{192,224},{224,1... | collective-permute-start | bytes 786440 | tf_op jit(solution)/shard_map/ppermute | solution.py:283
  21.6 1.2 %collective-permute-done.5 = f32[4,128,128]{2,1,0:T(8,128)S(1)} collective-permute-done((f32[4,128,128]{2,1,0:T(8,128)S(1)}, f32[4,128,128]{2,1,0:T(8,128)S(1)}, u32[]{:S(2)}, u32[]{:S(2)}) %collective-permute-start.5) | collective-permute-done | bytes 262176 | tf_op jit(solution)/shard_map/ppermute | solution.py:283
  22.8 20.7 %all_to_all.10 = f32[32,16,128]{2,1,0:T(8,128)S(1)} all-to-all(f32[32,16,128]{2,1,0:T(8,128)S(1)} %bitcast.15), channel_id=1, replica_groups=mesh['ens'=8,'space'=32] {'space'}, dimensions={0} | all-to-all | bytes 524288 | tf_op jit(solution)/shard_map/all_to_all | solution.py:318
  43.5 0.0 collective-permute-done.7.rest_8_
  43.5 3.8 %collective-permute-start.12 = (bf16[64,8192]{1,0:T(8,128)(2,1)}, bf16[64,8192]{1,0:T(8,128)(2,1)S(1)}, u32[]{:S(2)}, u32[]{:S(2)}) collective-permute-start(bf16[64,8192]{1,0:T(8,128)(2,1)} %field_ref), channel_id=1, source_target_pairs={{0,32},{32,0},{64,96},{96,64},{128,160},{160,128},{192,224},{224,1... | collective-permute-start | bytes 3145736 | tf_op jit(solution)/shard_map/ppermute | solution.py:283
  47.3 0.1 collective-permute-start.10
  47.4 0.4 collective-permute-start.11
  47.9 1.6 %collective-permute-start.9 = (bf16[32,8192]{1,0:T(8,128)(2,1)S(1)}, bf16[32,8192]{1,0:T(8,128)(2,1)S(1)}, u32[]{:S(2)}, u32[]{:S(2)}) collective-permute-start(bf16[32,8192]{1,0:T(8,128)(2,1)S(1)} %slice.22), channel_id=1, source_target_pairs={{0,192},{32,224},{64,0},{96,32},{128,64},{160,96},{192,128},{224,1... | collective-permute-start | bytes 1572872 | tf_op jit(solution)/shard_map/ppermute | solution.py:280
  49.5 0.0 collective-permute-start.8
  49.6 17.9 %all_to_all.11 = f32[32,16,128]{2,1,0:T(8,128)S(1)} all-to-all(f32[32,16,128]{2,1,0:T(8,128)S(1)} %broadcast_in_dim.2), channel_id=1, replica_groups=mesh['ens'=8,'space'=32] {'space'}, dimensions={0} | all-to-all | bytes 524288 | tf_op jit(solution)/shard_map/all_to_all | solution.py:324
  67.4 0.0 collective-permute-done.9.rest_5_
  67.4 0.0 collective-permute-done.8.rest_4_
  67.5 0.0 collective-permute-done.12.rest_1_
  67.5 0.0 collective-permute-done.11.rest_9_
  67.5 3.8 %collective-permute-start.13 = (f32[4,64,128]{2,1,0:T(8,128)S(1)}, f32[4,64,128]{2,1,0:T(8,128)S(1)}, u32[]{:S(2)}, u32[]{:S(2)}) collective-permute-start(f32[4,64,128]{2,1,0:T(8,128)S(1)} %slice.23), channel_id=1, source_target_pairs={{0,32},{32,0},{64,96},{96,64},{128,160},{160,128},{192,224},{224,1... | collective-permute-start | bytes 393224 | tf_op jit(solution)/shard_map/ppermute | solution.py:283
  71.3 1.3 %collective-permute-start.16 = (f32[2,64,128]{2,1,0:T(8,128)S(1)}, f32[2,64,128]{2,1,0:T(8,128)S(1)}, u32[]{:S(2)}, u32[]{:S(2)}) collective-permute-start(f32[2,64,128]{2,1,0:T(8,128)S(1)} %pad_maximum_fusion.1), channel_id=1, source_target_pairs={{0,192},{32,224},{64,0},{96,32},{128,64},{160,96},{192,128},{224,1... | collective-permute-start | bytes 196616 | tf_op jit(solution)/shard_map/ppermute | solution.py:280
  72.6 0.7 collective-permute-start.15
  73.3 0.0 collective-permute-start.14
  73.3 4.6 %begin.1 = (f32[128,128]{1,0:T(8,128)S(1)}, f32[128,384]{1,0:T(8,128)S(1)}, f32[128,384]{1,0:T(8,128)S(1)}, f32[64,512]{1,0:T(8,128)S(1)}) custom-call(s32[1]{0:T(128)} %bitcast.place_ref, f32[4,128]{1,0:T(4,128)S(1)} %convert_bitcast_fusion.1.ids_ref, f32[4,128,128]{2,1,0:T(8,128)S(1)} %bitcast.14, f32[4,64,128]{2,1,0:T(8,128)S(1)} %collective-permute-done.13.other_ref), custom_call_target="tpu_custom_call" | custom-call | tf_op jit(solution)/shard_map/begin/pallas_call | solution.py:335
  78.0 0.0 collective-permute-done.15.g2_ref
  78.0 0.6 collective-permute-done.14.g1_ref
  78.6 1.4 %collective-permute-start.18 = (bf16[32,8192]{1,0:T(8,128)(2,1)S(1)}, bf16[32,8192]{1,0:T(8,128)(2,1)S(1)}, u32[]{:S(2)}, u32[]{:S(2)}) collective-permute-start(bf16[32,8192]{1,0:T(8,128)(2,1)S(1)} %collective-permute-done.8.rest_4_), channel_id=1, source_target_pairs={{0,32},{32,0},{64,96},{96,64},{128,160},{160,128},{192,224},{224,1... | collective-permute-start | bytes 1572872 | tf_op jit(solution)/shard_map/ppermute | solution.py:283
  80.0 0.0 collective-permute-start.19
  80.0 0.8 collective-permute-start.17
  80.9 1.7 %collective-permute-done.17.theirs_ref = f32[6,64,128]{2,1,0:T(8,128)S(1)} collective-permute-done((f32[6,64,128]{2,1,0:T(8,128)S(1)}, f32[6,64,128]{2,1,0:T(8,128)S(1)}, u32[]{:S(2)}, u32[]{:S(2)}) %collective-permute-start.17) | collective-permute-done | bytes 196640 | tf_op jit(solution)/shard_map/ppermute | solution.py:283
  82.6 0.0 collective-permute-done.19.rest_7_
  82.6 17.1 %solve.1 = (bf16[64,512]{1,0:T(8,128)(2,1)S(1)}, bf16[512,8192]{1,0:T(8,128)(2,1)S(1)}) custom-call(s32[1]{0:T(128)} %bitcast.place_ref, f32[4,128]{1,0:T(4,128)S(1)} %convert_bitcast_fusion.1.ids_ref, f32[128,128]{1,0:T(8,128)S(1)} %get-tuple-element.71.inverse_ref, f32[128,384]{1,0:T(8,128)S(1)} %get-tuple-element.72.upper_ref, ...), custom_call_target="tpu_custom_call" | custom-call | tf_op jit(solution)/shard_map/solve/pallas_call | solution.py:352
  99.7 2.5 %update.1 = bf16[64,8192]{1,0:T(8,128)(2,1)} custom-call(bf16[64,512]{1,0:T(8,128)(2,1)S(1)} %get-tuple-element.83.t_ref, bf16[64,8192]{1,0:T(8,128)(2,1)S(1)} %copy-done, bf16[512,8192]{1,0:T(8,128)(2,1)S(1)} %get-tuple-element.84.anomaly_ref), custom_call_target="tpu_custom_call" | custom-call | tf_op jit(solution)/shard_map/update/pallas_call | solution.py:360
  (17 shorter events, 0.2 us)
Async XLA Ops:
  0.0 82.6 %copy-start = (bf16[64,8192]{1,0:T(8,128)(2,1)S(1)}, bf16[64,8192]{1,0:T(8,128)(2,1)}, u32[]{:S(2)}) copy-start(bf16[64,8192]{1,0:T(8,128)(2,1)} %field_ref) | copy-start | bytes 3145732
  0.0 4.7 %collective-permute-start = (f32[64,1280]{1,0:T(8,128)}, f32[64,1280]{1,0:T(8,128)S(1)}, u32[]{:S(2)}, u32[]{:S(2)}) collective-permute-start(f32[64,1280]{1,0:T(8,128)} %param.9), channel_id=1, source_target_pairs={{0,32},{32,0},{64,96},{96,64},{128,160},{160,128},{192,224},{224,1... | collective-permute-start | bytes 983048 | tf_op jit(solution)/shard_map/ppermute | solution.py:283
  4.8 6.9 %collective-permute-start.3 = (bf16[144,640]{1,0:T(8,128)(2,1)S(1)}, bf16[144,640]{1,0:T(8,128)(2,1)S(1)}, u32[]{:S(2)}, u32[]{:S(2)}) collective-permute-start(bf16[144,640]{1,0:T(8,128)(2,1)S(1)} %prepare.1.p0_ref), channel_id=1, source_target_pairs={{0,192},{32,224},{64,0},{96,32},{128,64},{160,96},{192,128},{224,1... | collective-permute-start | bytes 552968 | tf_op jit(solution)/shard_map/ppermute | solution.py:280
  5.6 7.1 %collective-permute-start.2 = (bf16[144,640]{1,0:T(8,128)(2,1)S(1)}, bf16[144,640]{1,0:T(8,128)(2,1)S(1)}, u32[]{:S(2)}, u32[]{:S(2)}) collective-permute-start(bf16[144,640]{1,0:T(8,128)(2,1)S(1)} %prepare.1.p0_ref), channel_id=1, source_target_pairs={{0,128},{32,160},{64,192},{96,224},{128,0},{160,32},{192,64},{224,... | collective-permute-start | bytes 552968 | tf_op jit(solution)/shard_map/ppermute | solution.py:280
  6.1 11.5 %collective-permute-start.1 = (bf16[144,640]{1,0:T(8,128)(2,1)S(1)}, bf16[144,640]{1,0:T(8,128)(2,1)S(1)}, u32[]{:S(2)}, u32[]{:S(2)}) collective-permute-start(bf16[144,640]{1,0:T(8,128)(2,1)S(1)} %prepare.1.p0_ref), channel_id=1, source_target_pairs={{0,64},{32,96},{64,128},{96,160},{128,192},{160,224},{192,0},{224,... | collective-permute-start | bytes 552968 | tf_op jit(solution)/shard_map/ppermute | solution.py:280
  7.6 11.4 %collective-permute-start.4 = (f32[64,1280]{1,0:T(8,128)}, f32[64,1280]{1,0:T(8,128)S(1)}, u32[]{:S(2)}, u32[]{:S(2)}) collective-permute-start(f32[64,1280]{1,0:T(8,128)} %param.10), channel_id=1, source_target_pairs={{0,32},{32,0},{64,96},{96,64},{128,160},{160,128},{192,224},{224,1... | collective-permute-start | bytes 983048 | tf_op jit(solution)/shard_map/ppermute | solution.py:283
  17.6 25.9 %collective-permute-start.7 = (bf16[64,8192]{1,0:T(8,128)(2,1)}, bf16[64,8192]{1,0:T(8,128)(2,1)S(1)}, u32[]{:S(2)}, u32[]{:S(2)}) collective-permute-start(bf16[64,8192]{1,0:T(8,128)(2,1)} %field_ref), channel_id=1, source_target_pairs={{0,192},{32,224},{64,0},{96,32},{128,64},{160,96},{192,128},{224,1... | collective-permute-start | bytes 3145736 | tf_op jit(solution)/shard_map/ppermute | solution.py:280
  17.6 25.9 %collective-permute-start.6 = (bf16[64,8192]{1,0:T(8,128)(2,1)}, bf16[64,8192]{1,0:T(8,128)(2,1)S(1)}, u32[]{:S(2)}, u32[]{:S(2)}) collective-permute-start(bf16[64,8192]{1,0:T(8,128)(2,1)} %field_ref), channel_id=1, source_target_pairs={{0,64},{32,96},{64,128},{96,160},{128,192},{160,224},{192,0},{224,... | collective-permute-start | bytes 3145736 | tf_op jit(solution)/shard_map/ppermute | solution.py:280
  20.4 2.3 %collective-permute-start.5 = (f32[4,128,128]{2,1,0:T(8,128)S(1)}, f32[4,128,128]{2,1,0:T(8,128)S(1)}, u32[]{:S(2)}, u32[]{:S(2)}) collective-permute-start(f32[4,128,128]{2,1,0:T(8,128)S(1)} %get-tuple-element.61), channel_id=1, source_target_pairs={{0,32},{32,0},{64,96},{96,64},{128,160},{160,128},{192,224},{224,1... | collective-permute-start | bytes 786440 | tf_op jit(solution)/shard_map/ppermute | solution.py:283
  43.5 23.9 %collective-permute-start.12 = (bf16[64,8192]{1,0:T(8,128)(2,1)}, bf16[64,8192]{1,0:T(8,128)(2,1)S(1)}, u32[]{:S(2)}, u32[]{:S(2)}) collective-permute-start(bf16[64,8192]{1,0:T(8,128)(2,1)} %field_ref), channel_id=1, source_target_pairs={{0,32},{32,0},{64,96},{96,64},{128,160},{160,128},{192,224},{224,1... | collective-permute-start | bytes 3145736 | tf_op jit(solution)/shard_map/ppermute | solution.py:283
  47.3 20.2 %collective-permute-start.10 = (bf16[64,8192]{1,0:T(8,128)(2,1)S(1)}, bf16[64,8192]{1,0:T(8,128)(2,1)S(1)}, u32[]{:S(2)}, u32[]{:S(2)}) collective-permute-start(bf16[64,8192]{1,0:T(8,128)(2,1)S(1)} %collective-permute-done.6.rest_2_), channel_id=1, source_target_pairs={{0,32},{32,0},{64,96},{96,64},{128,160},{160,128},{192,224},{224,1... | collective-permute-start | bytes 3145736 | tf_op jit(solution)/shard_map/ppermute | solution.py:283
  47.4 20.1 %collective-permute-start.11 = (bf16[64,8192]{1,0:T(8,128)(2,1)S(1)}, bf16[64,8192]{1,0:T(8,128)(2,1)S(1)}, u32[]{:S(2)}, u32[]{:S(2)}) collective-permute-start(bf16[64,8192]{1,0:T(8,128)(2,1)S(1)} %collective-permute-done.7.rest_8_), channel_id=1, source_target_pairs={{0,32},{32,0},{64,96},{96,64},{128,160},{160,128},{192,224},{224,1... | collective-permute-start | bytes 3145736 | tf_op jit(solution)/shard_map/ppermute | solution.py:283
  47.9 19.6 %collective-permute-start.9 = (bf16[32,8192]{1,0:T(8,128)(2,1)S(1)}, bf16[32,8192]{1,0:T(8,128)(2,1)S(1)}, u32[]{:S(2)}, u32[]{:S(2)}) collective-permute-start(bf16[32,8192]{1,0:T(8,128)(2,1)S(1)} %slice.22), channel_id=1, source_target_pairs={{0,192},{32,224},{64,0},{96,32},{128,64},{160,96},{192,128},{224,1... | collective-permute-start | bytes 1572872 | tf_op jit(solution)/shard_map/ppermute | solution.py:280
  49.5 17.9 %collective-permute-start.8 = (bf16[32,8192]{1,0:T(8,128)(2,1)S(1)}, bf16[32,8192]{1,0:T(8,128)(2,1)S(1)}, u32[]{:S(2)}, u32[]{:S(2)}) collective-permute-start(bf16[32,8192]{1,0:T(8,128)(2,1)S(1)} %slice.21), channel_id=1, source_target_pairs={{0,64},{32,96},{64,128},{96,160},{128,192},{160,224},{192,0},{224,... | collective-permute-start | bytes 1572872 | tf_op jit(solution)/shard_map/ppermute | solution.py:280
  67.5 5.8 %collective-permute-start.13 = (f32[4,64,128]{2,1,0:T(8,128)S(1)}, f32[4,64,128]{2,1,0:T(8,128)S(1)}, u32[]{:S(2)}, u32[]{:S(2)}) collective-permute-start(f32[4,64,128]{2,1,0:T(8,128)S(1)} %slice.23), channel_id=1, source_target_pairs={{0,32},{32,0},{64,96},{96,64},{128,160},{160,128},{192,224},{224,1... | collective-permute-start | bytes 393224 | tf_op jit(solution)/shard_map/ppermute | solution.py:283
  71.3 6.7 %collective-permute-start.16 = (f32[2,64,128]{2,1,0:T(8,128)S(1)}, f32[2,64,128]{2,1,0:T(8,128)S(1)}, u32[]{:S(2)}, u32[]{:S(2)}) collective-permute-start(f32[2,64,128]{2,1,0:T(8,128)S(1)} %pad_maximum_fusion.1), channel_id=1, source_target_pairs={{0,192},{32,224},{64,0},{96,32},{128,64},{160,96},{192,128},{224,1... | collective-permute-start | bytes 196616 | tf_op jit(solution)/shard_map/ppermute | solution.py:280
  72.6 5.4 %collective-permute-start.15 = (f32[2,64,128]{2,1,0:T(8,128)S(1)}, f32[2,64,128]{2,1,0:T(8,128)S(1)}, u32[]{:S(2)}, u32[]{:S(2)}) collective-permute-start(f32[2,64,128]{2,1,0:T(8,128)S(1)} %slice.24), channel_id=1, source_target_pairs={{0,128},{32,160},{64,192},{96,224},{128,0},{160,32},{192,64},{224,... | collective-permute-start | bytes 196616 | tf_op jit(solution)/shard_map/ppermute | solution.py:280
  73.3 5.3 %collective-permute-start.14 = (f32[2,64,128]{2,1,0:T(8,128)S(1)}, f32[2,64,128]{2,1,0:T(8,128)S(1)}, u32[]{:S(2)}, u32[]{:S(2)}) collective-permute-start(f32[2,64,128]{2,1,0:T(8,128)S(1)} %slice.24), channel_id=1, source_target_pairs={{0,64},{32,96},{64,128},{96,160},{128,192},{160,224},{192,0},{224,... | collective-permute-start | bytes 196616 | tf_op jit(solution)/shard_map/ppermute | solution.py:280
  78.6 4.0 %collective-permute-start.18 = (bf16[32,8192]{1,0:T(8,128)(2,1)S(1)}, bf16[32,8192]{1,0:T(8,128)(2,1)S(1)}, u32[]{:S(2)}, u32[]{:S(2)}) collective-permute-start(bf16[32,8192]{1,0:T(8,128)(2,1)S(1)} %collective-permute-done.8.rest_4_), channel_id=1, source_target_pairs={{0,32},{32,0},{64,96},{96,64},{128,160},{160,128},{192,224},{224,1... | collective-permute-start | bytes 1572872 | tf_op jit(solution)/shard_map/ppermute | solution.py:283
  80.0 2.6 %collective-permute-start.19 = (bf16[32,8192]{1,0:T(8,128)(2,1)S(1)}, bf16[32,8192]{1,0:T(8,128)(2,1)S(1)}, u32[]{:S(2)}, u32[]{:S(2)}) collective-permute-start(bf16[32,8192]{1,0:T(8,128)(2,1)S(1)} %collective-permute-done.9.rest_5_), channel_id=1, source_target_pairs={{0,32},{32,0},{64,96},{96,64},{128,160},{160,128},{192,224},{224,1... | collective-permute-start | bytes 1572872 | tf_op jit(solution)/shard_map/ppermute | solution.py:283
  80.0 2.5 %collective-permute-start.17 = (f32[6,64,128]{2,1,0:T(8,128)S(1)}, f32[6,64,128]{2,1,0:T(8,128)S(1)}, u32[]{:S(2)}, u32[]{:S(2)}) collective-permute-start(f32[6,64,128]{2,1,0:T(8,128)S(1)} %pad_maximum_fusion), channel_id=1, source_target_pairs={{0,32},{32,0},{64,96},{96,64},{128,160},{160,128},{192,224},{224,1... | collective-permute-start | bytes 589832 | tf_op jit(solution)/shard_map/ppermute | solution.py:283

commit v5 on v4

--- a/solution.py
+++ b/solution.py
@@ -301,10 +301,13 @@
     table = jnp.pad(block_error_scale, (0, 128 - block_error_scale.shape[0])).reshape(1, 128)
     payloads = [payload] + [turned(payload, k) for k in (1, 2, 3)]
 
+    members_field, *payloads[3:] = lax.optimization_barrier((members_field, payloads[3]))
+    ahead = turned(members_field, 3)
+
     ids = member_ids.astype(F32).reshape(4, 128)
     after_spread = lax.optimization_barrier((members_field, noise_mine, ids, facts, table, *payloads))
     (field, noise_mine, ids, facts, table), payloads = after_spread[:5], after_spread[5:]
-    back, ahead = turned(field, 1), turned(field, 3)
+    back = turned(field, 1)
 
     own, other = pl.pallas_call(
         functools.partial(gram_kernel, factor=factor),
@@ -332,6 +335,7 @@
     far = jnp.stack([gram[0], gram[2]])
     grams = [turned(near, 1), turned(near, 2), turned(far, 3)]
     gram_other = swapped(gram)
+    beyond_others = [swapped(f) for f in beyond]
     inverse, upper, row, right = pl.pallas_call(
         begin_kernel,
         out_shape=(
@@ -344,9 +348,7 @@
         compiler_params=room(8),
         name="begin",
     )(place, ids, whole, gram_other)
-    inverse, *after = lax.optimization_barrier((inverse, *grams, *beyond))
-    grams, beyond = after[:3], after[3:]
-    beyond_others = [swapped(f) for f in beyond]
+    inverse, *grams = lax.optimization_barrier((inverse, *grams))
     theirs = swapped(jnp.concatenate(grams, axis=0))
     fields = [field, others[2], back, others[0], *beyond, *beyond_others, ahead, others[1]]
     transform, anomaly = pl.pallas_call(

time: 103 us -> 102 us (level)
  starting transfers between devices: 23.1 us -> 26.3 us
  waiting for transfers between devices: 9.98 us -> 7.39 us
  blocking collectives: 38.6 us -> 37.1 us
    ppermute x10, starting transfers between devices: 7.09 us -> 11.5 us  [turned(): lax.ppermute(array, 'ens', [(i, (i + 2 * steps) % 8) for i in range(8)])]
    ppermute x10, waiting for transfers between devices: 6.53 us -> 4.6 us  [turned(): lax.ppermute(array, 'ens', [(i, (i + 2 * steps) % 8) for i in range(8)])]
    all_to_all x1, blocking collectives: 20.7 us -> 19 us  [body(): lax.all_to_all(part.reshape(32, 16, 128), 'space', split_axis=0, concat_a...]
    ppermute x10, starting transfers between devices: 16 us -> 14.9 us  [swapped(): return lax.ppermute(array, 'ens', swap)]
  transfers between devices with their start and end apart: 20 -> 20, of which waited for: 6 -> 7; matrix products, arithmetic and copies ran while one was open for 5% -> 5% of each run, Pallas kernels for 6% -> 6%
where the time goes in v5:
time: 102 us; the launch traced here: 101 us
  blocking collectives  37.1 us (36%)
  starting transfers between devices  26.3 us (26%)
  Pallas kernels  25.7 us (25%)
  waiting for transfers between devices  7.39 us (7%)
  local copies, waits for them, and re-layouts  2.62 us (3%)
  other arithmetic  2.19 us (2%)
    all_to_all x1, blocking collectives, body(): lax.all_to_all(part.reshape(32, 16, 128), 'space', split_axis=0, concat_a...  19 us
    all_to_all x1, blocking collectives, body(): lax.all_to_all(jnp.broadcast_to(summed[None], (32, 16, 128)), 'space', sp...  18 us
    pallas_call x1, Pallas kernels, body(): pl.pallas_call(solve_kernel, out_shape=(shaped(rows, members, dtype=BF16)...  17.1 us
    ppermute x10, starting transfers between devices, swapped(): return lax.ppermute(array, 'ens', swap)  14.9 us
    ppermute x10, starting transfers between devices, turned(): lax.ppermute(array, 'ens', [(i, (i + 2 * steps) % 8) for i in range(8)])  11.5 us
    pallas_call x1, Pallas kernels, body(): pl.pallas_call(begin_kernel, out_shape=(shaped(128, 128), shaped(128, 384...  4.61 us
    ppermute x10, waiting for transfers between devices, turned(): lax.ppermute(array, 'ens', [(i, (i + 2 * steps) % 8) for i in range(8)])  4.6 us
    ppermute x10, waiting for transfers between devices, swapped(): return lax.ppermute(array, 'ens', swap)  2.79 us
  transfers between devices with their start and end apart: 20, of which 7 were waited for; matrix products, arithmetic and copies ran while one was open for 5% of the time, Pallas kernels for 6%

profile of v5, /device:TPU:1, one launch (start us, length us, event | category | flops | bytes accessed | tf_op | source)
XLA Modules:
  0.0 101.4 jit_solution(5910050718435792927)
XLA Ops:
  0.0 3.2 %collective-permute-start = (f32[64,1280]{1,0:T(8,128)}, f32[64,1280]{1,0:T(8,128)S(1)}, u32[]{:S(2)}, u32[]{:S(2)}) collective-permute-start(f32[64,1280]{1,0:T(8,128)} %param.9), channel_id=1, source_target_pairs={{0,32},{32,0},{64,96},{96,64},{128,160},{160,128},{192,224},{224,1... | collective-permute-start | bytes 983048 | tf_op jit(solution)/shard_map/ppermute | solution.py:283
  3.2 0.9 constant_dynamic-slice_fusion.1.mine_ref
  4.2 0.5 collective-permute-done.got_ref
  4.7 0.1 prepare.1.p0_ref
  4.8 1.1 %collective-permute-start.3 = (bf16[144,640]{1,0:T(8,128)(2,1)S(1)}, bf16[144,640]{1,0:T(8,128)(2,1)S(1)}, u32[]{:S(2)}, u32[]{:S(2)}) collective-permute-start(bf16[144,640]{1,0:T(8,128)(2,1)S(1)} %prepare.1.p0_ref), channel_id=1, source_target_pairs={{0,128},{32,160},{64,192},{96,224},{128,0},{160,32},{192,64},{224,... | collective-permute-start | bytes 552968 | tf_op jit(solution)/shard_map/ppermute | solution.py:280
  5.9 0.3 collective-permute-start.2
  6.2 2.4 %collective-permute-start.1 = (bf16[144,640]{1,0:T(8,128)(2,1)S(1)}, bf16[144,640]{1,0:T(8,128)(2,1)S(1)}, u32[]{:S(2)}, u32[]{:S(2)}) collective-permute-start(bf16[144,640]{1,0:T(8,128)(2,1)S(1)} %prepare.1.p0_ref), channel_id=1, source_target_pairs={{0,192},{32,224},{64,0},{96,32},{128,64},{160,96},{192,128},{224,1... | collective-permute-start | bytes 552968 | tf_op jit(solution)/shard_map/ppermute | solution.py:280
  8.5 0.9 constant_dynamic-slice_fusion.mine_ref
  9.5 1.3 %collective-permute-start.4 = (f32[64,1280]{1,0:T(8,128)}, f32[64,1280]{1,0:T(8,128)S(1)}, u32[]{:S(2)}, u32[]{:S(2)}) collective-permute-start(f32[64,1280]{1,0:T(8,128)} %param.10), channel_id=1, source_target_pairs={{0,32},{32,0},{64,96},{96,64},{128,160},{160,128},{192,224},{224,1... | collective-permute-start | bytes 983048 | tf_op jit(solution)/shard_map/ppermute | solution.py:283
  10.8 0.7 convert_bitcast_fusion.1.ids_ref
  11.5 0.7 convert_bitcast_fusion
  12.2 0.7 pad_maximum_fusion.2.facts_ref
  12.9 0.7 pad_bitcast_fusion.table_ref
  13.5 1.0 collective-permute-done.1.p3_ref
  14.5 0.0 collective-permute-done.3.p2_ref
  14.5 2.4 %collective-permute-done.2.p1_ref = bf16[144,640]{1,0:T(8,128)(2,1)S(1)} collective-permute-done((bf16[144,640]{1,0:T(8,128)(2,1)S(1)}, bf16[144,640]{1,0:T(8,128)(2,1)S(1)}, u32[]{:S(2)}, u32[]{:S(2)}) %collective-permute-start.2) | collective-permute-done | bytes 184352 | tf_op jit(solution)/shard_map/ppermute | solution.py:280
  16.9 0.0 collective-permute-start.6
  16.9 2.7 %collective-permute-start.7 = (bf16[64,8192]{1,0:T(8,128)(2,1)}, bf16[64,8192]{1,0:T(8,128)(2,1)S(1)}, u32[]{:S(2)}, u32[]{:S(2)}) collective-permute-start(bf16[64,8192]{1,0:T(8,128)(2,1)} %field_ref), channel_id=1, source_target_pairs={{0,192},{32,224},{64,0},{96,32},{128,64},{160,96},{192,128},{224,1... | collective-permute-start | bytes 3145736 | tf_op jit(solution)/shard_map/ppermute | solution.py:280
  19.5 0.0 collective-permute-done.4.got_ref
  19.6 1.4 %gram.1 = (f32[4,128,128]{2,1,0:T(8,128)S(1)}, f32[4,128,128]{2,1,0:T(8,128)S(1)}) custom-call(s32[1]{0:T(128)} %bitcast.place_ref, bf16[144,640]{1,0:T(8,128)(2,1)S(1)} %prepare.1.p0_ref, bf16[144,640]{1,0:T(8,128)(2,1)S(1)} %collective-permute-done.2.p1_ref, bf16[144,640]{1,0:T(8,128)(2,1)S(1)} %collective-permute-done.3.p2_ref, ...), custom_call_target="tpu_custom_call" | custom-call | tf_op jit(solution)/shard_map/gram/pallas_call | solution.py:312
  20.9 1.1 %collective-permute-start.5 = (f32[4,128,128]{2,1,0:T(8,128)S(1)}, f32[4,128,128]{2,1,0:T(8,128)S(1)}, u32[]{:S(2)}, u32[]{:S(2)}) collective-permute-start(f32[4,128,128]{2,1,0:T(8,128)S(1)} %get-tuple-element.63), channel_id=1, source_target_pairs={{0,32},{32,0},{64,96},{96,64},{128,160},{160,128},{192,224},{224,1... | collective-permute-start | bytes 786440 | tf_op jit(solution)/shard_map/ppermute | solution.py:283
  22.1 1.2 %collective-permute-done.5 = f32[4,128,128]{2,1,0:T(8,128)S(1)} collective-permute-done((f32[4,128,128]{2,1,0:T(8,128)S(1)}, f32[4,128,128]{2,1,0:T(8,128)S(1)}, u32[]{:S(2)}, u32[]{:S(2)}) %collective-permute-start.5) | collective-permute-done | bytes 262176 | tf_op jit(solution)/shard_map/ppermute | solution.py:283
  23.2 19.0 %all_to_all.10 = f32[32,16,128]{2,1,0:T(8,128)S(1)} all-to-all(f32[32,16,128]{2,1,0:T(8,128)S(1)} %bitcast.15), channel_id=1, replica_groups=mesh['ens'=8,'space'=32] {'space'}, dimensions={0} | all-to-all | bytes 524288 | tf_op jit(solution)/shard_map/all_to_all | solution.py:321
  42.3 0.2 collective-permute-done.6.rest_2_
  42.5 0.0 collective-permute-done.7.rest_8_
  42.5 3.6 %collective-permute-start.12 = (bf16[64,8192]{1,0:T(8,128)(2,1)}, bf16[64,8192]{1,0:T(8,128)(2,1)S(1)}, u32[]{:S(2)}, u32[]{:S(2)}) collective-permute-start(bf16[64,8192]{1,0:T(8,128)(2,1)} %field_ref), channel_id=1, source_target_pairs={{0,32},{32,0},{64,96},{96,64},{128,160},{160,128},{192,224},{224,1... | collective-permute-start | bytes 3145736 | tf_op jit(solution)/shard_map/ppermute | solution.py:283
  46.1 0.1 collective-permute-start.10
  46.2 0.4 collective-permute-start.11
  46.7 1.3 %collective-permute-start.9 = (bf16[32,8192]{1,0:T(8,128)(2,1)S(1)}, bf16[32,8192]{1,0:T(8,128)(2,1)S(1)}, u32[]{:S(2)}, u32[]{:S(2)}) collective-permute-start(bf16[32,8192]{1,0:T(8,128)(2,1)S(1)} %slice.22), channel_id=1, source_target_pairs={{0,192},{32,224},{64,0},{96,32},{128,64},{160,96},{192,128},{224,1... | collective-permute-start | bytes 1572872 | tf_op jit(solution)/shard_map/ppermute | solution.py:280
  48.0 0.3 collective-permute-start.8
  48.3 18.0 %all_to_all.11 = f32[32,16,128]{2,1,0:T(8,128)S(1)} all-to-all(f32[32,16,128]{2,1,0:T(8,128)S(1)} %broadcast_in_dim.2), channel_id=1, replica_groups=mesh['ens'=8,'space'=32] {'space'}, dimensions={0} | all-to-all | bytes 524288 | tf_op jit(solution)/shard_map/all_to_all | solution.py:327
  66.3 0.0 collective-permute-done.9.rest_5_
  66.3 0.0 collective-permute-done.8.rest_4_
  66.3 0.0 collective-permute-done.12.rest_1_
  66.3 0.0 collective-permute-done.10.rest_3_
  66.4 0.0 collective-permute-done.11.rest_9_
  66.4 3.5 %collective-permute-start.13 = (f32[4,64,128]{2,1,0:T(8,128)S(1)}, f32[4,64,128]{2,1,0:T(8,128)S(1)}, u32[]{:S(2)}, u32[]{:S(2)}) collective-permute-start(f32[4,64,128]{2,1,0:T(8,128)S(1)} %slice.23), channel_id=1, source_target_pairs={{0,32},{32,0},{64,96},{96,64},{128,160},{160,128},{192,224},{224,1... | collective-permute-start | bytes 393224 | tf_op jit(solution)/shard_map/ppermute | solution.py:283
  69.9 0.1 collective-permute-start.18
  70.0 0.4 collective-permute-start.19
  70.4 2.8 %collective-permute-start.16 = (f32[2,64,128]{2,1,0:T(8,128)S(1)}, f32[2,64,128]{2,1,0:T(8,128)S(1)}, u32[]{:S(2)}, u32[]{:S(2)}) collective-permute-start(f32[2,64,128]{2,1,0:T(8,128)S(1)} %pad_maximum_fusion.1), channel_id=1, source_target_pairs={{0,192},{32,224},{64,0},{96,32},{128,64},{160,96},{192,128},{224,1... | collective-permute-start | bytes 196616 | tf_op jit(solution)/shard_map/ppermute | solution.py:280
  73.2 0.7 collective-permute-start.14
  73.9 4.6 %begin.1 = (f32[128,128]{1,0:T(8,128)S(1)}, f32[128,384]{1,0:T(8,128)S(1)}, f32[128,384]{1,0:T(8,128)S(1)}, f32[64,512]{1,0:T(8,128)S(1)}) custom-call(s32[1]{0:T(128)} %bitcast.place_ref, f32[4,128]{1,0:T(4,128)S(1)} %convert_bitcast_fusion.1.ids_ref, f32[4,128,128]{2,1,0:T(8,128)S(1)} %bitcast.14, f32[4,64,128]{2,1,0:T(8,128)S(1)} %collective-permute-done.13.other_ref), custom_call_target="tpu_custom_call" | custom-call | tf_op jit(solution)/shard_map/begin/pallas_call | solution.py:339
  78.5 0.0 collective-permute-done.16.g3_ref
  78.5 1.1 %collective-permute-done.14.g1_ref = f32[2,64,128]{2,1,0:T(8,128)S(1)} collective-permute-done((f32[2,64,128]{2,1,0:T(8,128)S(1)}, f32[2,64,128]{2,1,0:T(8,128)S(1)}, u32[]{:S(2)}, u32[]{:S(2)}) %collective-permute-start.14) | collective-permute-done | bytes 65568 | tf_op jit(solution)/shard_map/ppermute | solution.py:280
  79.6 1.1 %collective-permute-start.17 = (f32[6,64,128]{2,1,0:T(8,128)S(1)}, f32[6,64,128]{2,1,0:T(8,128)S(1)}, u32[]{:S(2)}, u32[]{:S(2)}) collective-permute-start(f32[6,64,128]{2,1,0:T(8,128)S(1)} %pad_maximum_fusion), channel_id=1, source_target_pairs={{0,32},{32,0},{64,96},{96,64},{128,160},{160,128},{192,224},{224,1... | collective-permute-start | bytes 589832 | tf_op jit(solution)/shard_map/ppermute | solution.py:283
  80.7 1.1 %collective-permute-done.17.theirs_ref = f32[6,64,128]{2,1,0:T(8,128)S(1)} collective-permute-done((f32[6,64,128]{2,1,0:T(8,128)S(1)}, f32[6,64,128]{2,1,0:T(8,128)S(1)}, u32[]{:S(2)}, u32[]{:S(2)}) %collective-permute-start.17) | collective-permute-done | bytes 196640 | tf_op jit(solution)/shard_map/ppermute | solution.py:283
  81.7 17.1 %solve.1 = (bf16[64,512]{1,0:T(8,128)(2,1)S(1)}, bf16[512,8192]{1,0:T(8,128)(2,1)S(1)}) custom-call(s32[1]{0:T(128)} %bitcast.place_ref, f32[4,128]{1,0:T(4,128)S(1)} %convert_bitcast_fusion.1.ids_ref, f32[128,128]{1,0:T(8,128)S(1)} %get-tuple-element.71.inverse_ref, f32[128,384]{1,0:T(8,128)S(1)} %get-tuple-element.72.upper_ref, ...), custom_call_target="tpu_custom_call" | custom-call | tf_op jit(solution)/shard_map/solve/pallas_call | solution.py:354
  98.9 2.5 %update.1 = bf16[64,8192]{1,0:T(8,128)(2,1)} custom-call(bf16[64,512]{1,0:T(8,128)(2,1)S(1)} %get-tuple-element.83.t_ref, bf16[64,8192]{1,0:T(8,128)(2,1)S(1)} %copy-done, bf16[512,8192]{1,0:T(8,128)(2,1)S(1)} %get-tuple-element.84.anomaly_ref), custom_call_target="tpu_custom_call" | custom-call | tf_op jit(solution)/shard_map/update/pallas_call | solution.py:362
  (17 shorter events, 0.2 us)
Async XLA Ops:
  0.0 81.7 %copy-start = (bf16[64,8192]{1,0:T(8,128)(2,1)S(1)}, bf16[64,8192]{1,0:T(8,128)(2,1)}, u32[]{:S(2)}) copy-start(bf16[64,8192]{1,0:T(8,128)(2,1)} %field_ref) | copy-start | bytes 3145732
  0.0 4.7 %collective-permute-start = (f32[64,1280]{1,0:T(8,128)}, f32[64,1280]{1,0:T(8,128)S(1)}, u32[]{:S(2)}, u32[]{:S(2)}) collective-permute-start(f32[64,1280]{1,0:T(8,128)} %param.9), channel_id=1, source_target_pairs={{0,32},{32,0},{64,96},{96,64},{128,160},{160,128},{192,224},{224,1... | collective-permute-start | bytes 983048 | tf_op jit(solution)/shard_map/ppermute | solution.py:283
  4.8 9.7 %collective-permute-start.3 = (bf16[144,640]{1,0:T(8,128)(2,1)S(1)}, bf16[144,640]{1,0:T(8,128)(2,1)S(1)}, u32[]{:S(2)}, u32[]{:S(2)}) collective-permute-start(bf16[144,640]{1,0:T(8,128)(2,1)S(1)} %prepare.1.p0_ref), channel_id=1, source_target_pairs={{0,128},{32,160},{64,192},{96,224},{128,0},{160,32},{192,64},{224,... | collective-permute-start | bytes 552968 | tf_op jit(solution)/shard_map/ppermute | solution.py:280
  5.9 11.0 %collective-permute-start.2 = (bf16[144,640]{1,0:T(8,128)(2,1)S(1)}, bf16[144,640]{1,0:T(8,128)(2,1)S(1)}, u32[]{:S(2)}, u32[]{:S(2)}) collective-permute-start(bf16[144,640]{1,0:T(8,128)(2,1)S(1)} %prepare.1.p0_ref), channel_id=1, source_target_pairs={{0,64},{32,96},{64,128},{96,160},{128,192},{160,224},{192,0},{224,... | collective-permute-start | bytes 552968 | tf_op jit(solution)/shard_map/ppermute | solution.py:280
  6.2 8.3 %collective-permute-start.1 = (bf16[144,640]{1,0:T(8,128)(2,1)S(1)}, bf16[144,640]{1,0:T(8,128)(2,1)S(1)}, u32[]{:S(2)}, u32[]{:S(2)}) collective-permute-start(bf16[144,640]{1,0:T(8,128)(2,1)S(1)} %prepare.1.p0_ref), channel_id=1, source_target_pairs={{0,192},{32,224},{64,0},{96,32},{128,64},{160,96},{192,128},{224,1... | collective-permute-start | bytes 552968 | tf_op jit(solution)/shard_map/ppermute | solution.py:280
  9.5 10.1 %collective-permute-start.4 = (f32[64,1280]{1,0:T(8,128)}, f32[64,1280]{1,0:T(8,128)S(1)}, u32[]{:S(2)}, u32[]{:S(2)}) collective-permute-start(f32[64,1280]{1,0:T(8,128)} %param.10), channel_id=1, source_target_pairs={{0,32},{32,0},{64,96},{96,64},{128,160},{160,128},{192,224},{224,1... | collective-permute-start | bytes 983048 | tf_op jit(solution)/shard_map/ppermute | solution.py:283
  16.9 25.7 %collective-permute-start.6 = (bf16[64,8192]{1,0:T(8,128)(2,1)}, bf16[64,8192]{1,0:T(8,128)(2,1)S(1)}, u32[]{:S(2)}, u32[]{:S(2)}) collective-permute-start(bf16[64,8192]{1,0:T(8,128)(2,1)} %field_ref), channel_id=1, source_target_pairs={{0,64},{32,96},{64,128},{96,160},{128,192},{160,224},{192,0},{224,... | collective-permute-start | bytes 3145736 | tf_op jit(solution)/shard_map/ppermute | solution.py:280
  16.9 25.7 %collective-permute-start.7 = (bf16[64,8192]{1,0:T(8,128)(2,1)}, bf16[64,8192]{1,0:T(8,128)(2,1)S(1)}, u32[]{:S(2)}, u32[]{:S(2)}) collective-permute-start(bf16[64,8192]{1,0:T(8,128)(2,1)} %field_ref), channel_id=1, source_target_pairs={{0,192},{32,224},{64,0},{96,32},{128,64},{160,96},{192,128},{224,1... | collective-permute-start | bytes 3145736 | tf_op jit(solution)/shard_map/ppermute | solution.py:280
  20.9 2.3 %collective-permute-start.5 = (f32[4,128,128]{2,1,0:T(8,128)S(1)}, f32[4,128,128]{2,1,0:T(8,128)S(1)}, u32[]{:S(2)}, u32[]{:S(2)}) collective-permute-start(f32[4,128,128]{2,1,0:T(8,128)S(1)} %get-tuple-element.63), channel_id=1, source_target_pairs={{0,32},{32,0},{64,96},{96,64},{128,160},{160,128},{192,224},{224,1... | collective-permute-start | bytes 786440 | tf_op jit(solution)/shard_map/ppermute | solution.py:283
  42.5 23.8 %collective-permute-start.12 = (bf16[64,8192]{1,0:T(8,128)(2,1)}, bf16[64,8192]{1,0:T(8,128)(2,1)S(1)}, u32[]{:S(2)}, u32[]{:S(2)}) collective-permute-start(bf16[64,8192]{1,0:T(8,128)(2,1)} %field_ref), channel_id=1, source_target_pairs={{0,32},{32,0},{64,96},{96,64},{128,160},{160,128},{192,224},{224,1... | collective-permute-start | bytes 3145736 | tf_op jit(solution)/shard_map/ppermute | solution.py:283
  46.1 20.2 %collective-permute-start.10 = (bf16[64,8192]{1,0:T(8,128)(2,1)S(1)}, bf16[64,8192]{1,0:T(8,128)(2,1)S(1)}, u32[]{:S(2)}, u32[]{:S(2)}) collective-permute-start(bf16[64,8192]{1,0:T(8,128)(2,1)S(1)} %collective-permute-done.6.rest_2_), channel_id=1, source_target_pairs={{0,32},{32,0},{64,96},{96,64},{128,160},{160,128},{192,224},{224,1... | collective-permute-start | bytes 3145736 | tf_op jit(solution)/shard_map/ppermute | solution.py:283
  46.2 20.1 %collective-permute-start.11 = (bf16[64,8192]{1,0:T(8,128)(2,1)S(1)}, bf16[64,8192]{1,0:T(8,128)(2,1)S(1)}, u32[]{:S(2)}, u32[]{:S(2)}) collective-permute-start(bf16[64,8192]{1,0:T(8,128)(2,1)S(1)} %collective-permute-done.7.rest_8_), channel_id=1, source_target_pairs={{0,32},{32,0},{64,96},{96,64},{128,160},{160,128},{192,224},{224,1... | collective-permute-start | bytes 3145736 | tf_op jit(solution)/shard_map/ppermute | solution.py:283
  46.7 19.6 %collective-permute-start.9 = (bf16[32,8192]{1,0:T(8,128)(2,1)S(1)}, bf16[32,8192]{1,0:T(8,128)(2,1)S(1)}, u32[]{:S(2)}, u32[]{:S(2)}) collective-permute-start(bf16[32,8192]{1,0:T(8,128)(2,1)S(1)} %slice.22), channel_id=1, source_target_pairs={{0,192},{32,224},{64,0},{96,32},{128,64},{160,96},{192,128},{224,1... | collective-permute-start | bytes 1572872 | tf_op jit(solution)/shard_map/ppermute | solution.py:280
  48.0 18.3 %collective-permute-start.8 = (bf16[32,8192]{1,0:T(8,128)(2,1)S(1)}, bf16[32,8192]{1,0:T(8,128)(2,1)S(1)}, u32[]{:S(2)}, u32[]{:S(2)}) collective-permute-start(bf16[32,8192]{1,0:T(8,128)(2,1)S(1)} %slice.21), channel_id=1, source_target_pairs={{0,64},{32,96},{64,128},{96,160},{128,192},{160,224},{192,0},{224,... | collective-permute-start | bytes 1572872 | tf_op jit(solution)/shard_map/ppermute | solution.py:280
  66.4 6.8 %collective-permute-start.13 = (f32[4,64,128]{2,1,0:T(8,128)S(1)}, f32[4,64,128]{2,1,0:T(8,128)S(1)}, u32[]{:S(2)}, u32[]{:S(2)}) collective-permute-start(f32[4,64,128]{2,1,0:T(8,128)S(1)} %slice.23), channel_id=1, source_target_pairs={{0,32},{32,0},{64,96},{96,64},{128,160},{160,128},{192,224},{224,1... | collective-permute-start | bytes 393224 | tf_op jit(solution)/shard_map/ppermute | solution.py:283
  69.9 11.9 %collective-permute-start.18 = (bf16[32,8192]{1,0:T(8,128)(2,1)S(1)}, bf16[32,8192]{1,0:T(8,128)(2,1)S(1)}, u32[]{:S(2)}, u32[]{:S(2)}) collective-permute-start(bf16[32,8192]{1,0:T(8,128)(2,1)S(1)} %collective-permute-done.8.rest_4_), channel_id=1, source_target_pairs={{0,32},{32,0},{64,96},{96,64},{128,160},{160,128},{192,224},{224,1... | collective-permute-start | bytes 1572872 | tf_op jit(solution)/shard_map/ppermute | solution.py:283
  70.0 11.8 %collective-permute-start.19 = (bf16[32,8192]{1,0:T(8,128)(2,1)S(1)}, bf16[32,8192]{1,0:T(8,128)(2,1)S(1)}, u32[]{:S(2)}, u32[]{:S(2)}) collective-permute-start(bf16[32,8192]{1,0:T(8,128)(2,1)S(1)} %collective-permute-done.9.rest_5_), channel_id=1, source_target_pairs={{0,32},{32,0},{64,96},{96,64},{128,160},{160,128},{192,224},{224,1... | collective-permute-start | bytes 1572872 | tf_op jit(solution)/shard_map/ppermute | solution.py:283
  70.4 8.1 %collective-permute-start.16 = (f32[2,64,128]{2,1,0:T(8,128)S(1)}, f32[2,64,128]{2,1,0:T(8,128)S(1)}, u32[]{:S(2)}, u32[]{:S(2)}) collective-permute-start(f32[2,64,128]{2,1,0:T(8,128)S(1)} %pad_maximum_fusion.1), channel_id=1, source_target_pairs={{0,192},{32,224},{64,0},{96,32},{128,64},{160,96},{192,128},{224,1... | collective-permute-start | bytes 196616 | tf_op jit(solution)/shard_map/ppermute | solution.py:280
  73.2 5.3 %collective-permute-start.15 = (f32[2,64,128]{2,1,0:T(8,128)S(1)}, f32[2,64,128]{2,1,0:T(8,128)S(1)}, u32[]{:S(2)}, u32[]{:S(2)}) collective-permute-start(f32[2,64,128]{2,1,0:T(8,128)S(1)} %slice.24), channel_id=1, source_target_pairs={{0,128},{32,160},{64,192},{96,224},{128,0},{160,32},{192,64},{224,... | collective-permute-start | bytes 196616 | tf_op jit(solution)/shard_map/ppermute | solution.py:280
  73.2 6.4 %collective-permute-start.14 = (f32[2,64,128]{2,1,0:T(8,128)S(1)}, f32[2,64,128]{2,1,0:T(8,128)S(1)}, u32[]{:S(2)}, u32[]{:S(2)}) collective-permute-start(f32[2,64,128]{2,1,0:T(8,128)S(1)} %slice.24), channel_id=1, source_target_pairs={{0,64},{32,96},{64,128},{96,160},{128,192},{160,224},{192,0},{224,... | collective-permute-start | bytes 196616 | tf_op jit(solution)/shard_map/ppermute | solution.py:280
  79.6 2.1 %collective-permute-start.17 = (f32[6,64,128]{2,1,0:T(8,128)S(1)}, f32[6,64,128]{2,1,0:T(8,128)S(1)}, u32[]{:S(2)}, u32[]{:S(2)}) collective-permute-start(f32[6,64,128]{2,1,0:T(8,128)S(1)} %pad_maximum_fusion), channel_id=1, source_target_pairs={{0,32},{32,0},{64,96},{96,64},{128,160},{160,128},{192,224},{224,1... | collective-permute-start | bytes 589832 | tf_op jit(solution)/shard_map/ppermute | solution.py:283

commit v6 on v5

--- a/solution.py
+++ b/solution.py
@@ -322,7 +322,8 @@
     summed = jnp.sum(spread_out, axis=0)
     summed, back, ahead, near_field = lax.optimization_barrier((summed, back, ahead, field))
     cut = rows // 2
-    beyond = [turned(back[:cut], 1), turned(ahead[cut:], 3)]
+    low, high, back, ahead, near_field = lax.optimization_barrier((back[:cut], ahead[cut:], back, ahead, near_field))
+    beyond = [turned(low, 1), turned(high, 3)]
     others = [swapped(back), swapped(ahead), swapped(near_field)]
     whole = lax.all_to_all(
         jnp.broadcast_to(summed[None], (32, 16, 128)), "space", split_axis=0, concat_axis=0

time: 102 us -> 101 us (level)
  blocking collectives: 37.1 us -> 35.8 us
    all_to_all x1, blocking collectives: 18 us -> 16.8 us  [body(): lax.all_to_all(jnp.broadcast_to(summed[None], (32, 16, 128)), 'space', sp...]
where the time goes in v6:
time: 101 us; the launch traced here: 100 us
  blocking collectives  35.8 us (35%)
  starting transfers between devices  26.4 us (26%)
  Pallas kernels  25.7 us (25%)
  waiting for transfers between devices  7.4 us (7%)
  local copies, waits for them, and re-layouts  2.62 us (3%)
  other arithmetic  2.19 us (2%)
    all_to_all x1, blocking collectives, body(): lax.all_to_all(part.reshape(32, 16, 128), 'space', split_axis=0, concat_a...  19 us
    pallas_call x1, Pallas kernels, body(): pl.pallas_call(solve_kernel, out_shape=(shaped(rows, members, dtype=BF16)...  17.1 us
    all_to_all x1, blocking collectives, body(): lax.all_to_all(jnp.broadcast_to(summed[None], (32, 16, 128)), 'space', sp...  16.8 us
    ppermute x10, starting transfers between devices, swapped(): return lax.ppermute(array, 'ens', swap)  15.2 us
    ppermute x10, starting transfers between devices, turned(): lax.ppermute(array, 'ens', [(i, (i + 2 * steps) % 8) for i in range(8)])  11.2 us
    ppermute x10, waiting for transfers between devices, turned(): lax.ppermute(array, 'ens', [(i, (i + 2 * steps) % 8) for i in range(8)])  4.62 us
    pallas_call x1, Pallas kernels, body(): pl.pallas_call(begin_kernel, out_shape=(shaped(128, 128), shaped(128, 384...  4.61 us
    ppermute x10, waiting for transfers between devices, swapped(): return lax.ppermute(array, 'ens', swap)  2.79 us
  transfers between devices with their start and end apart: 20, of which 7 were waited for; matrix products, arithmetic and copies ran while one was open for 5% of the time, Pallas kernels for 6%

profile of v6, /device:TPU:1, one launch (start us, length us, event | category | flops | bytes accessed | tf_op | source)
XLA Modules:
  0.0 100.3 jit_solution(1091393064757851663)
XLA Ops:
  0.0 3.2 %collective-permute-start = (f32[64,1280]{1,0:T(8,128)}, f32[64,1280]{1,0:T(8,128)S(1)}, u32[]{:S(2)}, u32[]{:S(2)}) collective-permute-start(f32[64,1280]{1,0:T(8,128)} %param.9), channel_id=1, source_target_pairs={{0,32},{32,0},{64,96},{96,64},{128,160},{160,128},{192,224},{224,1... | collective-permute-start | bytes 983048 | tf_op jit(solution)/shard_map/ppermute | solution.py:283
  3.2 0.9 constant_dynamic-slice_fusion.1.mine_ref
  4.2 0.5 collective-permute-done.got_ref
  4.7 0.1 prepare.1.p0_ref
  4.8 1.1 %collective-permute-start.3 = (bf16[144,640]{1,0:T(8,128)(2,1)S(1)}, bf16[144,640]{1,0:T(8,128)(2,1)S(1)}, u32[]{:S(2)}, u32[]{:S(2)}) collective-permute-start(bf16[144,640]{1,0:T(8,128)(2,1)S(1)} %prepare.1.p0_ref), channel_id=1, source_target_pairs={{0,128},{32,160},{64,192},{96,224},{128,0},{160,32},{192,64},{224,... | collective-permute-start | bytes 552968 | tf_op jit(solution)/shard_map/ppermute | solution.py:280
  5.9 0.3 collective-permute-start.2
  6.2 2.4 %collective-permute-start.1 = (bf16[144,640]{1,0:T(8,128)(2,1)S(1)}, bf16[144,640]{1,0:T(8,128)(2,1)S(1)}, u32[]{:S(2)}, u32[]{:S(2)}) collective-permute-start(bf16[144,640]{1,0:T(8,128)(2,1)S(1)} %prepare.1.p0_ref), channel_id=1, source_target_pairs={{0,192},{32,224},{64,0},{96,32},{128,64},{160,96},{192,128},{224,1... | collective-permute-start | bytes 552968 | tf_op jit(solution)/shard_map/ppermute | solution.py:280
  8.5 0.9 constant_dynamic-slice_fusion.mine_ref
  9.5 1.3 %collective-permute-start.4 = (f32[64,1280]{1,0:T(8,128)}, f32[64,1280]{1,0:T(8,128)S(1)}, u32[]{:S(2)}, u32[]{:S(2)}) collective-permute-start(f32[64,1280]{1,0:T(8,128)} %param.10), channel_id=1, source_target_pairs={{0,32},{32,0},{64,96},{96,64},{128,160},{160,128},{192,224},{224,1... | collective-permute-start | bytes 983048 | tf_op jit(solution)/shard_map/ppermute | solution.py:283
  10.8 0.7 convert_bitcast_fusion.1.ids_ref
  11.5 0.7 convert_bitcast_fusion
  12.2 0.7 pad_maximum_fusion.2.facts_ref
  12.9 0.7 pad_bitcast_fusion.table_ref
  13.5 1.0 collective-permute-done.1.p3_ref
  14.5 2.4 %collective-permute-done.2.p1_ref = bf16[144,640]{1,0:T(8,128)(2,1)S(1)} collective-permute-done((bf16[144,640]{1,0:T(8,128)(2,1)S(1)}, bf16[144,640]{1,0:T(8,128)(2,1)S(1)}, u32[]{:S(2)}, u32[]{:S(2)}) %collective-permute-start.2) | collective-permute-done | bytes 184352 | tf_op jit(solution)/shard_map/ppermute | solution.py:280
  16.9 2.7 %collective-permute-start.7 = (bf16[64,8192]{1,0:T(8,128)(2,1)}, bf16[64,8192]{1,0:T(8,128)(2,1)S(1)}, u32[]{:S(2)}, u32[]{:S(2)}) collective-permute-start(bf16[64,8192]{1,0:T(8,128)(2,1)} %field_ref), channel_id=1, source_target_pairs={{0,192},{32,224},{64,0},{96,32},{128,64},{160,96},{192,128},{224,1... | collective-permute-start | bytes 3145736 | tf_op jit(solution)/shard_map/ppermute | solution.py:280
  19.5 0.0 collective-permute-done.4.got_ref
  19.6 1.4 %gram.1 = (f32[4,128,128]{2,1,0:T(8,128)S(1)}, f32[4,128,128]{2,1,0:T(8,128)S(1)}) custom-call(s32[1]{0:T(128)} %bitcast.place_ref, bf16[144,640]{1,0:T(8,128)(2,1)S(1)} %prepare.1.p0_ref, bf16[144,640]{1,0:T(8,128)(2,1)S(1)} %collective-permute-done.2.p1_ref, bf16[144,640]{1,0:T(8,128)(2,1)S(1)} %collective-permute-done.3.p2_ref, ...), custom_call_target="tpu_custom_call" | custom-call | tf_op jit(solution)/shard_map/gram/pallas_call | solution.py:312
  20.9 1.1 %collective-permute-start.5 = (f32[4,128,128]{2,1,0:T(8,128)S(1)}, f32[4,128,128]{2,1,0:T(8,128)S(1)}, u32[]{:S(2)}, u32[]{:S(2)}) collective-permute-start(f32[4,128,128]{2,1,0:T(8,128)S(1)} %get-tuple-element.68), channel_id=1, source_target_pairs={{0,32},{32,0},{64,96},{96,64},{128,160},{160,128},{192,224},{224,1... | collective-permute-start | bytes 786440 | tf_op jit(solution)/shard_map/ppermute | solution.py:283
  22.1 1.2 %collective-permute-done.5 = f32[4,128,128]{2,1,0:T(8,128)S(1)} collective-permute-done((f32[4,128,128]{2,1,0:T(8,128)S(1)}, f32[4,128,128]{2,1,0:T(8,128)S(1)}, u32[]{:S(2)}, u32[]{:S(2)}) %collective-permute-start.5) | collective-permute-done | bytes 262176 | tf_op jit(solution)/shard_map/ppermute | solution.py:283
  23.2 19.0 %all_to_all.10 = f32[32,16,128]{2,1,0:T(8,128)S(1)} all-to-all(f32[32,16,128]{2,1,0:T(8,128)S(1)} %bitcast.15), channel_id=1, replica_groups=mesh['ens'=8,'space'=32] {'space'}, dimensions={0} | all-to-all | bytes 524288 | tf_op jit(solution)/shard_map/all_to_all | solution.py:321
  42.3 0.2 collective-permute-done.6.rest_2_
  42.5 0.0 collective-permute-done.7.rest_8_
  42.6 3.6 %collective-permute-start.12 = (bf16[64,8192]{1,0:T(8,128)(2,1)}, bf16[64,8192]{1,0:T(8,128)(2,1)S(1)}, u32[]{:S(2)}, u32[]{:S(2)}) collective-permute-start(bf16[64,8192]{1,0:T(8,128)(2,1)} %field_ref), channel_id=1, source_target_pairs={{0,32},{32,0},{64,96},{96,64},{128,160},{160,128},{192,224},{224,1... | collective-permute-start | bytes 3145736 | tf_op jit(solution)/shard_map/ppermute | solution.py:283
  46.2 0.1 collective-permute-start.10
  46.3 0.4 collective-permute-start.11
  46.7 0.0 collective-permute-start.8
  46.7 2.7 %collective-permute-start.9 = (bf16[32,8192]{1,0:T(8,128)(2,1)S(1)}, bf16[32,8192]{1,0:T(8,128)(2,1)S(1)}, u32[]{:S(2)}, u32[]{:S(2)}) collective-permute-start(bf16[32,8192]{1,0:T(8,128)(2,1)S(1)} %slice.22), channel_id=1, source_target_pairs={{0,192},{32,224},{64,0},{96,32},{128,64},{160,96},{192,128},{224,1... | collective-permute-start | bytes 1572872 | tf_op jit(solution)/shard_map/ppermute | solution.py:280
  49.5 16.8 %all_to_all.11 = f32[32,16,128]{2,1,0:T(8,128)S(1)} all-to-all(f32[32,16,128]{2,1,0:T(8,128)S(1)} %broadcast_in_dim.2), channel_id=1, replica_groups=mesh['ens'=8,'space'=32] {'space'}, dimensions={0} | all-to-all | bytes 524288 | tf_op jit(solution)/shard_map/all_to_all | solution.py:328
  66.2 0.0 collective-permute-done.9.rest_5_
  66.2 0.0 collective-permute-done.12.rest_1_
  66.2 0.0 collective-permute-done.10.rest_3_
  66.2 0.0 collective-permute-done.11.rest_9_
  66.3 3.8 %collective-permute-start.13 = (f32[4,64,128]{2,1,0:T(8,128)S(1)}, f32[4,64,128]{2,1,0:T(8,128)S(1)}, u32[]{:S(2)}, u32[]{:S(2)}) collective-permute-start(f32[4,64,128]{2,1,0:T(8,128)S(1)} %slice.23), channel_id=1, source_target_pairs={{0,32},{32,0},{64,96},{96,64},{128,160},{160,128},{192,224},{224,1... | collective-permute-start | bytes 393224 | tf_op jit(solution)/shard_map/ppermute | solution.py:283
  70.1 0.1 collective-permute-start.18
  70.2 0.4 collective-permute-start.19
  70.6 1.4 %collective-permute-start.16 = (f32[2,64,128]{2,1,0:T(8,128)S(1)}, f32[2,64,128]{2,1,0:T(8,128)S(1)}, u32[]{:S(2)}, u32[]{:S(2)}) collective-permute-start(f32[2,64,128]{2,1,0:T(8,128)S(1)} %pad_maximum_fusion.1), channel_id=1, source_target_pairs={{0,192},{32,224},{64,0},{96,32},{128,64},{160,96},{192,128},{224,1... | collective-permute-start | bytes 196616 | tf_op jit(solution)/shard_map/ppermute | solution.py:280
  72.1 0.0 collective-permute-start.15
  72.1 0.0 collective-permute-done.13.other_ref
  72.1 0.7 collective-permute-start.14
  72.7 4.6 %begin.1 = (f32[128,128]{1,0:T(8,128)S(1)}, f32[128,384]{1,0:T(8,128)S(1)}, f32[128,384]{1,0:T(8,128)S(1)}, f32[64,512]{1,0:T(8,128)S(1)}) custom-call(s32[1]{0:T(128)} %bitcast.place_ref, f32[4,128]{1,0:T(4,128)S(1)} %convert_bitcast_fusion.1.ids_ref, f32[4,128,128]{2,1,0:T(8,128)S(1)} %bitcast.14, f32[4,64,128]{2,1,0:T(8,128)S(1)} %collective-permute-done.13.other_ref), custom_call_target="tpu_custom_call" | custom-call | tf_op jit(solution)/shard_map/begin/pallas_call | solution.py:340
  77.4 0.0 collective-permute-done.16.g3_ref
  77.4 1.1 %collective-permute-done.14.g1_ref = f32[2,64,128]{2,1,0:T(8,128)S(1)} collective-permute-done((f32[2,64,128]{2,1,0:T(8,128)S(1)}, f32[2,64,128]{2,1,0:T(8,128)S(1)}, u32[]{:S(2)}, u32[]{:S(2)}) %collective-permute-start.14) | collective-permute-done | bytes 65568 | tf_op jit(solution)/shard_map/ppermute | solution.py:280
  78.5 1.1 %collective-permute-start.17 = (f32[6,64,128]{2,1,0:T(8,128)S(1)}, f32[6,64,128]{2,1,0:T(8,128)S(1)}, u32[]{:S(2)}, u32[]{:S(2)}) collective-permute-start(f32[6,64,128]{2,1,0:T(8,128)S(1)} %pad_maximum_fusion), channel_id=1, source_target_pairs={{0,32},{32,0},{64,96},{96,64},{128,160},{160,128},{192,224},{224,1... | collective-permute-start | bytes 589832 | tf_op jit(solution)/shard_map/ppermute | solution.py:283
  79.5 1.1 %collective-permute-done.17.theirs_ref = f32[6,64,128]{2,1,0:T(8,128)S(1)} collective-permute-done((f32[6,64,128]{2,1,0:T(8,128)S(1)}, f32[6,64,128]{2,1,0:T(8,128)S(1)}, u32[]{:S(2)}, u32[]{:S(2)}) %collective-permute-start.17) | collective-permute-done | bytes 196640 | tf_op jit(solution)/shard_map/ppermute | solution.py:283
  80.6 0.0 collective-permute-done.18.rest_6_
  80.6 17.1 %solve.1 = (bf16[64,512]{1,0:T(8,128)(2,1)S(1)}, bf16[512,8192]{1,0:T(8,128)(2,1)S(1)}) custom-call(s32[1]{0:T(128)} %bitcast.place_ref, f32[4,128]{1,0:T(4,128)S(1)} %convert_bitcast_fusion.1.ids_ref, f32[128,128]{1,0:T(8,128)S(1)} %get-tuple-element.81.inverse_ref, f32[128,384]{1,0:T(8,128)S(1)} %get-tuple-element.82.upper_ref, ...), custom_call_target="tpu_custom_call" | custom-call | tf_op jit(solution)/shard_map/solve/pallas_call | solution.py:355
  97.8 2.5 %update.1 = bf16[64,8192]{1,0:T(8,128)(2,1)} custom-call(bf16[64,512]{1,0:T(8,128)(2,1)S(1)} %get-tuple-element.93.t_ref, bf16[64,8192]{1,0:T(8,128)(2,1)S(1)} %copy-done, bf16[512,8192]{1,0:T(8,128)(2,1)S(1)} %get-tuple-element.94.anomaly_ref), custom_call_target="tpu_custom_call" | custom-call | tf_op jit(solution)/shard_map/update/pallas_call | solution.py:363
  (17 shorter events, 0.2 us)
Async XLA Ops:
  0.0 80.6 %copy-start = (bf16[64,8192]{1,0:T(8,128)(2,1)S(1)}, bf16[64,8192]{1,0:T(8,128)(2,1)}, u32[]{:S(2)}) copy-start(bf16[64,8192]{1,0:T(8,128)(2,1)} %field_ref) | copy-start | bytes 3145732
  0.0 4.7 %collective-permute-start = (f32[64,1280]{1,0:T(8,128)}, f32[64,1280]{1,0:T(8,128)S(1)}, u32[]{:S(2)}, u32[]{:S(2)}) collective-permute-start(f32[64,1280]{1,0:T(8,128)} %param.9), channel_id=1, source_target_pairs={{0,32},{32,0},{64,96},{96,64},{128,160},{160,128},{192,224},{224,1... | collective-permute-start | bytes 983048 | tf_op jit(solution)/shard_map/ppermute | solution.py:283
  4.8 9.7 %collective-permute-start.3 = (bf16[144,640]{1,0:T(8,128)(2,1)S(1)}, bf16[144,640]{1,0:T(8,128)(2,1)S(1)}, u32[]{:S(2)}, u32[]{:S(2)}) collective-permute-start(bf16[144,640]{1,0:T(8,128)(2,1)S(1)} %prepare.1.p0_ref), channel_id=1, source_target_pairs={{0,128},{32,160},{64,192},{96,224},{128,0},{160,32},{192,64},{224,... | collective-permute-start | bytes 552968 | tf_op jit(solution)/shard_map/ppermute | solution.py:280
  5.9 11.0 %collective-permute-start.2 = (bf16[144,640]{1,0:T(8,128)(2,1)S(1)}, bf16[144,640]{1,0:T(8,128)(2,1)S(1)}, u32[]{:S(2)}, u32[]{:S(2)}) collective-permute-start(bf16[144,640]{1,0:T(8,128)(2,1)S(1)} %prepare.1.p0_ref), channel_id=1, source_target_pairs={{0,64},{32,96},{64,128},{96,160},{128,192},{160,224},{192,0},{224,... | collective-permute-start | bytes 552968 | tf_op jit(solution)/shard_map/ppermute | solution.py:280
  6.2 8.3 %collective-permute-start.1 = (bf16[144,640]{1,0:T(8,128)(2,1)S(1)}, bf16[144,640]{1,0:T(8,128)(2,1)S(1)}, u32[]{:S(2)}, u32[]{:S(2)}) collective-permute-start(bf16[144,640]{1,0:T(8,128)(2,1)S(1)} %prepare.1.p0_ref), channel_id=1, source_target_pairs={{0,192},{32,224},{64,0},{96,32},{128,64},{160,96},{192,128},{224,1... | collective-permute-start | bytes 552968 | tf_op jit(solution)/shard_map/ppermute | solution.py:280
  9.5 10.1 %collective-permute-start.4 = (f32[64,1280]{1,0:T(8,128)}, f32[64,1280]{1,0:T(8,128)S(1)}, u32[]{:S(2)}, u32[]{:S(2)}) collective-permute-start(f32[64,1280]{1,0:T(8,128)} %param.10), channel_id=1, source_target_pairs={{0,32},{32,0},{64,96},{96,64},{128,160},{160,128},{192,224},{224,1... | collective-permute-start | bytes 983048 | tf_op jit(solution)/shard_map/ppermute | solution.py:283
  16.9 25.7 %collective-permute-start.6 = (bf16[64,8192]{1,0:T(8,128)(2,1)}, bf16[64,8192]{1,0:T(8,128)(2,1)S(1)}, u32[]{:S(2)}, u32[]{:S(2)}) collective-permute-start(bf16[64,8192]{1,0:T(8,128)(2,1)} %field_ref), channel_id=1, source_target_pairs={{0,64},{32,96},{64,128},{96,160},{128,192},{160,224},{192,0},{224,... | collective-permute-start | bytes 3145736 | tf_op jit(solution)/shard_map/ppermute | solution.py:280
  16.9 25.7 %collective-permute-start.7 = (bf16[64,8192]{1,0:T(8,128)(2,1)}, bf16[64,8192]{1,0:T(8,128)(2,1)S(1)}, u32[]{:S(2)}, u32[]{:S(2)}) collective-permute-start(bf16[64,8192]{1,0:T(8,128)(2,1)} %field_ref), channel_id=1, source_target_pairs={{0,192},{32,224},{64,0},{96,32},{128,64},{160,96},{192,128},{224,1... | collective-permute-start | bytes 3145736 | tf_op jit(solution)/shard_map/ppermute | solution.py:280
  20.9 2.3 %collective-permute-start.5 = (f32[4,128,128]{2,1,0:T(8,128)S(1)}, f32[4,128,128]{2,1,0:T(8,128)S(1)}, u32[]{:S(2)}, u32[]{:S(2)}) collective-permute-start(f32[4,128,128]{2,1,0:T(8,128)S(1)} %get-tuple-element.68), channel_id=1, source_target_pairs={{0,32},{32,0},{64,96},{96,64},{128,160},{160,128},{192,224},{224,1... | collective-permute-start | bytes 786440 | tf_op jit(solution)/shard_map/ppermute | solution.py:283
  42.6 23.6 %collective-permute-start.12 = (bf16[64,8192]{1,0:T(8,128)(2,1)}, bf16[64,8192]{1,0:T(8,128)(2,1)S(1)}, u32[]{:S(2)}, u32[]{:S(2)}) collective-permute-start(bf16[64,8192]{1,0:T(8,128)(2,1)} %field_ref), channel_id=1, source_target_pairs={{0,32},{32,0},{64,96},{96,64},{128,160},{160,128},{192,224},{224,1... | collective-permute-start | bytes 3145736 | tf_op jit(solution)/shard_map/ppermute | solution.py:283
  46.2 20.0 %collective-permute-start.10 = (bf16[64,8192]{1,0:T(8,128)(2,1)S(1)}, bf16[64,8192]{1,0:T(8,128)(2,1)S(1)}, u32[]{:S(2)}, u32[]{:S(2)}) collective-permute-start(bf16[64,8192]{1,0:T(8,128)(2,1)S(1)} %collective-permute-done.6.rest_2_), channel_id=1, source_target_pairs={{0,32},{32,0},{64,96},{96,64},{128,160},{160,128},{192,224},{224,1... | collective-permute-start | bytes 3145736 | tf_op jit(solution)/shard_map/ppermute | solution.py:283
  46.3 19.9 %collective-permute-start.11 = (bf16[64,8192]{1,0:T(8,128)(2,1)S(1)}, bf16[64,8192]{1,0:T(8,128)(2,1)S(1)}, u32[]{:S(2)}, u32[]{:S(2)}) collective-permute-start(bf16[64,8192]{1,0:T(8,128)(2,1)S(1)} %collective-permute-done.7.rest_8_), channel_id=1, source_target_pairs={{0,32},{32,0},{64,96},{96,64},{128,160},{160,128},{192,224},{224,1... | collective-permute-start | bytes 3145736 | tf_op jit(solution)/shard_map/ppermute | solution.py:283
  46.7 19.5 %collective-permute-start.8 = (bf16[32,8192]{1,0:T(8,128)(2,1)S(1)}, bf16[32,8192]{1,0:T(8,128)(2,1)S(1)}, u32[]{:S(2)}, u32[]{:S(2)}) collective-permute-start(bf16[32,8192]{1,0:T(8,128)(2,1)S(1)} %slice.21), channel_id=1, source_target_pairs={{0,64},{32,96},{64,128},{96,160},{128,192},{160,224},{192,0},{224,... | collective-permute-start | bytes 1572872 | tf_op jit(solution)/shard_map/ppermute | solution.py:280
  46.7 19.5 %collective-permute-start.9 = (bf16[32,8192]{1,0:T(8,128)(2,1)S(1)}, bf16[32,8192]{1,0:T(8,128)(2,1)S(1)}, u32[]{:S(2)}, u32[]{:S(2)}) collective-permute-start(bf16[32,8192]{1,0:T(8,128)(2,1)S(1)} %slice.22), channel_id=1, source_target_pairs={{0,192},{32,224},{64,0},{96,32},{128,64},{160,96},{192,128},{224,1... | collective-permute-start | bytes 1572872 | tf_op jit(solution)/shard_map/ppermute | solution.py:280
  66.3 5.8 %collective-permute-start.13 = (f32[4,64,128]{2,1,0:T(8,128)S(1)}, f32[4,64,128]{2,1,0:T(8,128)S(1)}, u32[]{:S(2)}, u32[]{:S(2)}) collective-permute-start(f32[4,64,128]{2,1,0:T(8,128)S(1)} %slice.23), channel_id=1, source_target_pairs={{0,32},{32,0},{64,96},{96,64},{128,160},{160,128},{192,224},{224,1... | collective-permute-start | bytes 393224 | tf_op jit(solution)/shard_map/ppermute | solution.py:283
  70.1 10.5 %collective-permute-start.18 = (bf16[32,8192]{1,0:T(8,128)(2,1)S(1)}, bf16[32,8192]{1,0:T(8,128)(2,1)S(1)}, u32[]{:S(2)}, u32[]{:S(2)}) collective-permute-start(bf16[32,8192]{1,0:T(8,128)(2,1)S(1)} %collective-permute-done.8.rest_4_), channel_id=1, source_target_pairs={{0,32},{32,0},{64,96},{96,64},{128,160},{160,128},{192,224},{224,1... | collective-permute-start | bytes 1572872 | tf_op jit(solution)/shard_map/ppermute | solution.py:283
  70.2 10.4 %collective-permute-start.19 = (bf16[32,8192]{1,0:T(8,128)(2,1)S(1)}, bf16[32,8192]{1,0:T(8,128)(2,1)S(1)}, u32[]{:S(2)}, u32[]{:S(2)}) collective-permute-start(bf16[32,8192]{1,0:T(8,128)(2,1)S(1)} %collective-permute-done.9.rest_5_), channel_id=1, source_target_pairs={{0,32},{32,0},{64,96},{96,64},{128,160},{160,128},{192,224},{224,1... | collective-permute-start | bytes 1572872 | tf_op jit(solution)/shard_map/ppermute | solution.py:283
  70.6 6.7 %collective-permute-start.16 = (f32[2,64,128]{2,1,0:T(8,128)S(1)}, f32[2,64,128]{2,1,0:T(8,128)S(1)}, u32[]{:S(2)}, u32[]{:S(2)}) collective-permute-start(f32[2,64,128]{2,1,0:T(8,128)S(1)} %pad_maximum_fusion.1), channel_id=1, source_target_pairs={{0,192},{32,224},{64,0},{96,32},{128,64},{160,96},{192,128},{224,1... | collective-permute-start | bytes 196616 | tf_op jit(solution)/shard_map/ppermute | solution.py:280
  72.1 5.3 %collective-permute-start.15 = (f32[2,64,128]{2,1,0:T(8,128)S(1)}, f32[2,64,128]{2,1,0:T(8,128)S(1)}, u32[]{:S(2)}, u32[]{:S(2)}) collective-permute-start(f32[2,64,128]{2,1,0:T(8,128)S(1)} %slice.24), channel_id=1, source_target_pairs={{0,128},{32,160},{64,192},{96,224},{128,0},{160,32},{192,64},{224,... | collective-permute-start | bytes 196616 | tf_op jit(solution)/shard_map/ppermute | solution.py:280
  72.1 6.4 %collective-permute-start.14 = (f32[2,64,128]{2,1,0:T(8,128)S(1)}, f32[2,64,128]{2,1,0:T(8,128)S(1)}, u32[]{:S(2)}, u32[]{:S(2)}) collective-permute-start(f32[2,64,128]{2,1,0:T(8,128)S(1)} %slice.24), channel_id=1, source_target_pairs={{0,64},{32,96},{64,128},{96,160},{128,192},{160,224},{192,0},{224,... | collective-permute-start | bytes 196616 | tf_op jit(solution)/shard_map/ppermute | solution.py:280
  78.5 2.1 %collective-permute-start.17 = (f32[6,64,128]{2,1,0:T(8,128)S(1)}, f32[6,64,128]{2,1,0:T(8,128)S(1)}, u32[]{:S(2)}, u32[]{:S(2)}) collective-permute-start(f32[6,64,128]{2,1,0:T(8,128)S(1)} %pad_maximum_fusion), channel_id=1, source_target_pairs={{0,32},{32,0},{64,96},{96,64},{128,160},{160,128},{192,224},{224,1... | collective-permute-start | bytes 589832 | tf_op jit(solution)/shard_map/ppermute | solution.py:283
